TPU v7x, 256 devices: a whole 4x4x8 slice. The times are simulated.
256 devices in a mesh: dp: 32 (over z, x), tensor: 8 (over y, core).
Axes of the slice: x: 4, y: 4, z: 8, core: 2. Of those that a mesh axis runs over, the one named last changes fastest.
Arguments:
- hidden: bfloat16 [1024, 8192], P('dp', 'tensor'), may hold values from -6 to 6
- queries: bfloat16 [1024, 8192], P('dp', 'tensor'), may hold values from -128 to 128
- rotated_key_cache: bfloat16 [1024, 384, 1024], P('dp', None, 'tensor'), may hold values from -4 to 4
- stored_value_cache: bfloat16 [1024, 384, 1024], P('dp', None, 'tensor'), may hold values from -6 to 6
- lengths: int32 [1024], P('dp'), may hold values from 2 to 384, as said below
- tenants: int32 [1024], P('dp'), may hold values from 0 to 511, as said below
- key_value_weight: bfloat16 [8192, 2048], P(None, 'tensor'), may hold values from -0.0625 to 0.0625
- adapter_down_maps: bfloat16 [512, 8192, 64], P('dp', 'tensor'), may hold values from -0.0625 to 0.0625
- adapter_up_maps: bfloat16 [512, 64, 1024], P('dp', None, 'tensor'), may hold values from -0.75 to 0.75
Outputs:
- attended: bfloat16 [1024, 8192], P('dp', 'tensor')
- new_entries: bfloat16 [1024, 2048], P('dp', 'tensor')
Inputs may be any that keep to these rules, and one draw needn't show every extreme that they name: `tenants`: adapters k * 16 to (k + 1) * 16 - 1 form the k-th block of the pool. Among the 32 rows of one index of dp at most 2 use adapters of one block; one block is used by exactly 2 rows of every index of dp. `lengths`: the first row of each index of dp has 384 cached positions.
All inputs are finite; a program needn't handle non-finite values.
Results may differ from a plain program's by a relative error of at most 0.0075.
Values may be sent and summed in bfloat16 or wider, within the bound.
No kernel may reach another device: no remote copies, remote signals or barrier semaphores. Data moves between devices by JAX's collectives and lax.ppermute only.
A program may use at most 64 MiB of HBM per device.

v0:
```python
import jax
import jax.numpy as jnp
from jax import lax
from jax.sharding import PartitionSpec as P

HEADS = 64
KEY_VALUE_HEADS = 8
HEAD_SIZE = 128


rope_base = 500000.0


def rotate(values, positions):
    half_dim = values.shape[-1] // 2
    inverse = rope_base ** (-(jnp.arange(half_dim, dtype=jnp.float32) * 2.0) / values.shape[-1])
    angles = positions.astype(jnp.float32)[:, None] * inverse[None, :]
    cosine = jnp.cos(angles)[:, None, :]
    sine_part = jnp.sin(angles)[:, None, :]
    front_half = values[..., :half_dim]
    back_half = values[..., half_dim:]
    return jnp.concatenate(
        [front_half * cosine - back_half * sine_part, back_half * cosine + front_half * sine_part],
        axis=-1,
    )


def attend(query_heads, cache_keys, cache_values, new_key, fresh_value, row_lengths):
    score_scale = query_heads.shape[-1] ** (-0.5)
    scores = (
        jnp.einsum("rkgd,rlkd->rkgl", query_heads, cache_keys, preferred_element_type=jnp.float32)
        * score_scale
    )
    visible = jnp.arange(cache_keys.shape[1], dtype=jnp.int32)[None, :] < row_lengths[:, None]
    scores = jnp.where(visible[:, None, None, :], scores, -jnp.inf)
    own_score = (
        jnp.einsum("rkgd,rkd->rkg", query_heads, new_key, preferred_element_type=jnp.float32)
        * score_scale
    )
    largest = jnp.maximum(jnp.max(scores, axis=-1), own_score)
    weights = jnp.exp(scores - largest[..., None])
    own_weight = jnp.exp(own_score - largest)
    denominator = jnp.sum(weights, axis=-1) + own_weight
    weights = (weights / denominator[..., None]).astype(jnp.bfloat16)
    own_weight = (own_weight / denominator).astype(jnp.bfloat16)
    attended = jnp.einsum(
        "rkgl,rlkd->rkgd", weights, cache_values, preferred_element_type=jnp.float32
    )
    attended = (
        attended
        + own_weight.astype(jnp.float32)[..., None] * fresh_value.astype(jnp.float32)[:, :, None, :]
    )
    return attended.astype(jnp.bfloat16)


def on_device(
    hidden,
    queries,
    rotated_key_cache,
    stored_value_cache,
    lengths,
    tenants,
    key_value_weight,
    adapter_down_maps,
    adapter_up_maps,
):
    count_of_rows = hidden.shape[0]
    peer_count = lax.axis_size("dp")
    capacity = 2 * count_of_rows // peer_count
    slot_count = peer_count * capacity
    adapter_pool_count = adapter_down_maps.shape[0]
    column_count = key_value_weight.shape[1]
    shard_heads = column_count // (2 * HEAD_SIZE)
    group_size = HEADS // KEY_VALUE_HEADS
    projected_values = jnp.dot(
        lax.all_gather(hidden, "tensor", axis=1, tiled=True),
        key_value_weight,
        preferred_element_type=jnp.float32,
    )
    projected_values = projected_values.reshape(count_of_rows, shard_heads, 2, HEAD_SIZE)
    new_key = rotate(projected_values[:, :, 0], lengths).astype(jnp.bfloat16)
    owner_index = tenants // adapter_pool_count
    local_adapter = tenants % adapter_pool_count
    owner_match = (owner_index[:, None] == jnp.arange(peer_count, dtype=jnp.int32)[None, :]).astype(
        jnp.int32
    )
    earlier = jnp.cumsum(owner_match, axis=0) - owner_match
    rank_within = jnp.sum(earlier * owner_match, axis=1)
    slot_index = owner_index * capacity + rank_within
    placing = slot_index[None, :] == jnp.arange(slot_count, dtype=jnp.int32)[:, None]
    place_matrix = placing.astype(jnp.bfloat16)
    outgoing = jnp.dot(place_matrix, hidden, preferred_element_type=jnp.float32).astype(
        jnp.bfloat16
    )
    outgoing = outgoing.reshape(peer_count, capacity, hidden.shape[1])
    adapter_slots = jnp.sum(jnp.where(placing, local_adapter[None, :], 0), axis=1).reshape(
        peer_count, capacity
    )
    incoming = lax.all_to_all(outgoing, "dp", split_axis=0, concat_axis=0, tiled=True)
    arrived = lax.all_to_all(adapter_slots, "dp", split_axis=0, concat_axis=0, tiled=True)
    flattened_rows = incoming.reshape(slot_count, incoming.shape[2])
    flat_ids = arrived.reshape(slot_count)
    adapter_pick = (
        flat_ids[:, None] == jnp.arange(adapter_pool_count, dtype=jnp.int32)[None, :]
    ).astype(jnp.float32)
    all_rank_outputs = jnp.einsum(
        "hk,lkt->hlt", flattened_rows, adapter_down_maps, preferred_element_type=jnp.float32
    )
    partial_rank = jnp.sum(all_rank_outputs * adapter_pick[:, :, None], axis=1)
    rank_reduced = lax.psum(partial_rank, "tensor").astype(jnp.bfloat16)
    all_adapter_deltas = jnp.einsum(
        "hp,lpt->hlt", rank_reduced, adapter_up_maps, preferred_element_type=jnp.float32
    )
    expanded = jnp.sum(all_adapter_deltas * adapter_pick[:, :, None], axis=1)
    served = expanded.astype(jnp.bfloat16)
    returned = lax.all_to_all(
        served.reshape(peer_count, capacity, served.shape[1]),
        "dp",
        split_axis=0,
        concat_axis=0,
        tiled=True,
    )
    adapter_delta = jnp.dot(
        place_matrix.T,
        returned.reshape(slot_count, served.shape[1]),
        preferred_element_type=jnp.float32,
    )
    fresh_value = (
        projected_values[:, :, 1] + adapter_delta.reshape(count_of_rows, shard_heads, HEAD_SIZE)
    ).astype(jnp.bfloat16)
    new_entries = jnp.stack([new_key, fresh_value], axis=2).reshape(count_of_rows, column_count)
    cache_length = rotated_key_cache.shape[1]
    attended = attend(
        queries.reshape(count_of_rows, shard_heads, group_size, HEAD_SIZE),
        rotated_key_cache.reshape(count_of_rows, cache_length, shard_heads, HEAD_SIZE),
        stored_value_cache.reshape(count_of_rows, cache_length, shard_heads, HEAD_SIZE),
        new_key,
        fresh_value,
        lengths,
    )
    return (attended.reshape(count_of_rows, shard_heads * group_size * HEAD_SIZE), new_entries)


def solution(mesh):
    in_specs = (
        P("dp", "tensor"),
        P("dp", "tensor"),
        P("dp", None, "tensor"),
        P("dp", None, "tensor"),
        P("dp"),
        P("dp"),
        P(None, "tensor"),
        P("dp", "tensor", None),
        P("dp", None, "tensor"),
    )
    out_specs = (P("dp", "tensor"), P("dp", "tensor"))
    return jax.shard_map(
        on_device, mesh=mesh, in_specs=in_specs, out_specs=out_specs, check_vma=False
    )
```

profile of v0, /device:TPU:2, one launch (start us, length us, event | category | flops | bytes accessed | tf_op | source)
XLA Modules:
  0.0 113.7 jit_solution(9066016447504081428)
XLA Ops:
  0.6 0.0 copy-start
  0.6 0.0 copy-start.6
  0.7 0.8 and_select_fusion.1
  1.5 0.1 fusion.18
  1.6 0.1 reduce_window_sum.11
  1.6 0.2 select_reduce_fusion.1
  1.8 0.0 copy-start.7
  1.8 0.1 select_reduce_fusion
  1.9 0.7 all_to_all.13
  2.6 11.7 %all-to-all-start.1 = ((s32[32,1,2]{2,1,0:T(1,128)}), s32[32,1,2]{2,1,0:T(1,128)}, u32[]{:S(2)}, u32[]{:S(2)}) async-start(s32[32,1,2]{2,1,0:T(1,128)} %bitcast.7), calls=%async_computation.1 | async-start | bytes 32768 | tf_op jit(solution)/shard_map/all_to_all | solution.py:100
  14.3 1.8 %convolution_convert_fusion = bf16[64,1024]{1,0:T(8,128)(2,1)} fusion(bf16[32,1024]{1,0:T(8,128)(2,1)} %param.9, s32[32]{0:T(128)S(1)} %multiply_add_fusion), kind=kOutput, calls=%fused_computation.6 | convolution fusion | flops 4261888 | bytes 196736 | tf_op jit(solution)/shard_map/dot_general | solution.py:92
  16.1 13.8 %all_gather.3 = bf16[32,8192]{1,0:T(8,128)(2,1)S(1)} all-gather(bf16[32,1024]{1,0:T(8,128)(2,1)} %param.9), channel_id=1, replica_groups=mesh['dp'=32,'tensor'=8] {'tensor'}, dimensions={1}, use_global_device_ids=true | all-gather | bytes 589824 | tf_op jit(solution)/shard_map/all_gather | solution.py:76
  29.9 0.7 convert_element_type.62
  30.6 1.3 %iota_compare_fusion = pred[32,384]{1,0:T(8,128)(4,1)} fusion(s32[32]{0:T(128)} %param.13), kind=kLoop, calls=%fused_computation.17 | loop fusion | flops 12288 | bytes 12416 | tf_op jit(solution)/shard_map/lt | solution.py:34
  31.9 0.0 copy-done.7
  31.9 3.0 %fusion.29 = f32[32,256]{1,0:T(8,128)S(1)} fusion(bf16[32,8192]{1,0:T(8,128)(2,1)S(1)} %all_gather.3, bf16[8192,256]{1,0:T(8,128)(2,1)} %param.15), kind=kOutput, calls=%fused_computation.59 | convolution fusion | flops 134217728 | bytes 4751360 | tf_op jit(solution)/shard_map/dot_general | solution.py:75
  35.0 0.6 fusion.26
  35.6 0.1 fusion.13
  35.8 0.1 maximum_bitcast_fusion
  35.8 0.5 copy-done.1
  36.3 0.0 copy-done.3
  36.4 0.1 fusion.19
  36.5 0.0 copy-done
  36.5 2.0 %fusion.27 = (f32[32,8]{1,0:T(8,128)S(1)}, f32[32,8,384]{2,1,0:T(8,128)S(1)}) fusion(bf16[32,8,128]{2,1,0:T(8,128)(2,1)S(1)} %bitcast.45, bf16[32,384,128]{2,1,0:T(8,128)(2,1)S(1)} %copy-done, pred[32,384]{1,0:T(8,128)(4,1)} %iota_compare_fusion), kind=kOutput, calls=%fused_computation.57 | convolution fusion | flops 25460480 | bytes 3617792 | tf_op jit(solution)/shard_map/rkgd,rlkd->rkgl/dot_general | solution.py:31
  38.5 0.0 copy-done.5
  38.5 0.6 multiply_maximum_fusion
  39.1 1.6 %reshape.274 = bf16[32,2,1024]{2,1,0:T(2,128)(2,1)} reshape(bf16[64,1024]{1,0:T(8,128)(2,1)} %convolution_convert_fusion) | data formatting | bytes 262144 | tf_op jit(solution)/shard_map/reshape | solution.py:95
  40.7 0.0 all-to-all-done.1
  40.7 9.8 %all-to-all-start = ((bf16[32,2,1024]{2,1,0:T(2,128)(2,1)}), bf16[32,2,1024]{2,1,0:T(2,128)(2,1)}, u32[]{:S(2)}, u32[]{:S(2)}) async-start(bf16[32,2,1024]{2,1,0:T(2,128)(2,1)} %reshape.274), calls=%async_computation | async-start | bytes 262144 | tf_op jit(solution)/shard_map/all_to_all | solution.py:99
  50.6 1.5 %fusion.5 = f32[32,8]{1,0:T(8,128)} fusion(f32[32,8,384]{2,1,0:T(8,128)S(1)} %get-tuple-element.11, f32[32,8]{1,0:T(8,128)} %multiply_maximum_fusion), kind=kLoop, calls=%fused_computation.13 | loop fusion | flops 196352 | bytes 395264 | tf_op jit(solution)/shard_map/reduce_sum | solution.py:43
  52.1 0.5 broadcast.143
  52.6 2.0 %reduce.7 = s32[32,2]{1,0:T(8,128)} reduce(s32[32,1,2]{2,1,0:T(1,128)} %all-to-all-done.1, s32[]{:T(128)} %broadcast.143), dimensions={1}, to_apply=%all_to_all.14.reduce_sub_computation.3 | reduce | bytes 516 | tf_op jit(solution)/shard_map/all_to_all | solution.py:100
  54.6 1.4 %eq.53 = s32[64]{0:T(128)} reshape(s32[32,2]{1,0:T(8,128)} %reduce.7) | data formatting | bytes 512 | tf_op jit(solution)/shard_map/eq | solution.py:104
  56.0 1.2 %fusion.24 = f32[64,16]{0,1:T(8,128)} fusion(s32[64]{0:T(128)} %eq.53), kind=kLoop, calls=%fused_computation.47 | loop fusion | flops 2048 | bytes 4352 | tf_op jit(solution)/shard_map/convert_element_type | solution.py:105
  57.2 2.5 %all-to-all-done = bf16[32,2,1024]{2,1,0:T(2,128)(2,1)} async-done(((bf16[32,2,1024]{2,1,0:T(2,128)(2,1)}), bf16[32,2,1024]{2,1,0:T(2,128)(2,1)}, u32[]{:S(2)}, u32[]{:S(2)}) %all-to-all-start) | async-done | bytes 131104 | tf_op jit(solution)/shard_map/all_to_all | solution.py:99
  59.8 1.6 %reshape.281 = bf16[64,1024,1]{1,0,2:T(8,128)(2,1)} reshape(bf16[32,2,1024]{2,1,0:T(2,128)(2,1)} %all-to-all-done) | data formatting | bytes 262144 | tf_op jit(solution)/shard_map/reshape | solution.py:101
  61.4 3.3 %fusion.1 = f32[64,64]{1,0:T(8,128)} fusion(bf16[64,1024,1]{1,0,2:T(8,128)(2,1)} %reshape.281, bf16[16,1024,64]{1,2,0:T(8,128)(2,1)} %param.16, f32[64,16]{0,1:T(8,128)} %fusion.24), kind=kOutput, calls=%fused_computation.4 | convolution fusion | flops 134344704 | bytes 2248704 | tf_op jit(solution)/shard_map/hk,lkt->hlt/dot_general | solution.py:106
  64.7 25.6 %psum.7 = bf16[64,64]{1,0:T(8,128)(2,1)} all-reduce(f32[64,64]{1,0:T(8,128)} %fusion.1), channel_id=1, replica_groups=mesh['dp'=32,'tensor'=8] {'tensor'}, use_global_device_ids=true, to_apply=%region_6.7 | all-reduce | flops 4096 | bytes 24576 | tf_op jit(solution)/shard_map/psum | solution.py:110
  90.3 1.8 %fusion.2 = bf16[64,128]{1,0:T(8,128)(2,1)} fusion(bf16[16,64,128]{2,1,0:T(8,128)(2,1)} %param.17, f32[64,16]{0,1:T(8,128)} %fusion.24, bf16[64,64]{1,0:T(8,128)(2,1)} %psum.7), kind=kOutput, calls=%fused_computation.5 | convolution fusion | flops 17031168 | bytes 290816 | tf_op jit(solution)/shard_map/hp,lpt->hlt/dot_general | solution.py:111
  92.1 8.3 %all-to-all-start.2 = ((bf16[32,2,128]{2,1,0:T(2,128)(2,1)}), bf16[32,2,128]{2,1,0:T(2,128)(2,1)}, u32[]{:S(2)}, u32[]{:S(2)}) async-start(bf16[32,2,128]{2,1,0:T(2,128)(2,1)} %bitcast.57), calls=%async_computation.2 | async-start | bytes 32768 | tf_op jit(solution)/shard_map/all_to_all | solution.py:116
  100.4 1.4 %fusion.21 = (f32[32,8]{1,0:T(8,128)}, f32[32,8]{1,0:T(8,128)}) fusion(f32[32,8]{1,0:T(8,128)} %bitcast.53, f32[32,8]{1,0:T(8,128)} %fusion.5, f32[32,8]{1,0:T(8,128)S(1)} %get-tuple-element.10), kind=kLoop, calls=%fused_computation.42 | loop fusion | flops 1792 | bytes 5120 | tf_op jit(solution)/shard_map/convert_element_type | solution.py:51
  101.7 7.0 %all-to-all-done.2 = bf16[32,2,128]{2,1,0:T(2,128)(2,1)} async-done(((bf16[32,2,128]{2,1,0:T(2,128)(2,1)}), bf16[32,2,128]{2,1,0:T(2,128)(2,1)}, u32[]{:S(2)}, u32[]{:S(2)}) %all-to-all-start.2) | async-done | bytes 16416 | tf_op jit(solution)/shard_map/all_to_all | solution.py:116
  108.8 0.9 fusion.28
  109.7 2.6 %fusion.3 = bf16[32,8,128]{2,1,0:T(8,128)(2,1)S(1)} fusion(bf16[32,384,128]{2,1,0:T(8,128)(2,1)} %param.12, f32[32,8,384]{2,1,0:T(8,128)S(1)} %get-tuple-element.11, f32[32,8]{1,0:T(8,128)} %get-tuple-element.3, f32[32,8]{1,0:T(8,128)} %multiply_maximum_fusion, f32[32,128]{1,0:T(8,128)S(1)} %get-tuple-element.12, f32[32,8]{1,0:T(8,128)} %get-tuple-element.2), kind=kOutput, calls=%fused_computation.8 | convolution fusion | flops 25559040 | bytes 3623936 | tf_op jit(solution)/shard_map/rkgl,rlkd->rkgd/dot_general | solution.py:46
  112.4 0.7 copy.37
  113.0 0.0 copy-done.2
  113.0 0.1 pad_maximum_fusion
  113.1 0.6 copy.38
  (12 shorter events, 0.1 us)
Async XLA Ops:
  0.6 35.9 %copy-start = (bf16[32,384,128]{2,1,0:T(8,128)(2,1)S(1)}, bf16[32,384,128]{2,1,0:T(8,128)(2,1)}, u32[]{:S(2)}) copy-start(bf16[32,384,128]{2,1,0:T(8,128)(2,1)} %param.11) | copy-start | bytes 9437188
  0.6 34.9 %copy-start.6 = (bf16[32,1024]{1,0:T(8,128)(2,1)S(1)}, bf16[32,1024]{1,0:T(8,128)(2,1)}, u32[]{:S(2)}) copy-start(bf16[32,1024]{1,0:T(8,128)(2,1)} %param.10) | copy-start | bytes 196612
  1.8 30.1 %copy-start.7 = (s32[32]{0:T(128)}, s32[32]{0:T(128)S(1)}, u32[]{:S(2)}) copy-start(s32[32]{0:T(128)S(1)} %multiply_add_fusion) | copy-start | bytes 388
  2.6 38.1 %all-to-all-start.1 = ((s32[32,1,2]{2,1,0:T(1,128)}), s32[32,1,2]{2,1,0:T(1,128)}, u32[]{:S(2)}, u32[]{:S(2)}) async-start(s32[32,1,2]{2,1,0:T(1,128)} %bitcast.7), calls=%async_computation.1 | async-start | bytes 32768 | tf_op jit(solution)/shard_map/all_to_all | solution.py:100
  35.7 0.6 copy-start.1
  35.8 0.6 copy-start.3
  36.5 2.0 %copy-start.5 = (f32[32,1,8]{2,1,0:T(1,128)}, f32[32,1,8]{2,1,0:T(1,128)S(1)}, u32[]{:S(2)}) copy-start(f32[32,1,8]{2,1,0:T(1,128)S(1)} %fusion.19) | copy-start | bytes 3076
  40.7 19.0 %all-to-all-start = ((bf16[32,2,1024]{2,1,0:T(2,128)(2,1)}), bf16[32,2,1024]{2,1,0:T(2,128)(2,1)}, u32[]{:S(2)}, u32[]{:S(2)}) async-start(bf16[32,2,1024]{2,1,0:T(2,128)(2,1)} %reshape.274), calls=%async_computation | async-start | bytes 262144 | tf_op jit(solution)/shard_map/all_to_all | solution.py:99
  92.1 16.7 %all-to-all-start.2 = ((bf16[32,2,128]{2,1,0:T(2,128)(2,1)}), bf16[32,2,128]{2,1,0:T(2,128)(2,1)}, u32[]{:S(2)}, u32[]{:S(2)}) async-start(bf16[32,2,128]{2,1,0:T(2,128)(2,1)} %bitcast.57), calls=%async_computation.2 | async-start | bytes 32768 | tf_op jit(solution)/shard_map/all_to_all | solution.py:116
  101.7 11.3 %copy-start.2 = (bf16[32,1,64]{2,0,1:T(8,128)(2,1)S(1)}, bf16[32,1,64]{2,0,1:T(8,128)(2,1)}, u32[]{:S(2)}) copy-start(bf16[32,1,64]{2,0,1:T(8,128)(2,1)} %copy-done.1) | copy-start | bytes 12292
  101.7 11.3 %copy-start.4 = (bf16[32,1,64]{2,0,1:T(8,128)(2,1)S(1)}, bf16[32,1,64]{2,0,1:T(8,128)(2,1)}, u32[]{:S(2)}) copy-start(bf16[32,1,64]{2,0,1:T(8,128)(2,1)} %copy-done.3) | copy-start | bytes 12292
where the time goes:
time: 115 us; the launch traced here: 114 us
  blocking collectives  39.4 us (34%)
  starting transfers between devices  29.8 us (26%)
  matrix products  15.6 us (14%)
  other arithmetic  10.3 us (9%)
  waiting for transfers between devices  9.57 us (8%)
  local copies, waits for them, and re-layouts  8.33 us (7%)
    psum x1, blocking collectives, on_device(): rank_reduced = lax.psum(partial_rank, 'tensor').astype(jnp.bfloat16)  25.6 us
    all_gather x1, blocking collectives, on_device(): lax.all_gather(hidden, 'tensor', axis=1, tiled=True)  13.8 us
    all_to_all x1, starting transfers between devices, on_device(): lax.all_to_all(adapter_slots, 'dp', split_axis=0, concat_axis=0, tiled=True)  11.7 us
    all_to_all x1, starting transfers between devices, on_device(): lax.all_to_all(outgoing, 'dp', split_axis=0, concat_axis=0, tiled=True)  9.83 us
    all_to_all x1, starting transfers between devices, on_device(): lax.all_to_all(served.reshape(peer_count, capacity, served.shape[1]), 'dp...  8.32 us
    all_to_all x1, waiting for transfers between devices, on_device(): lax.all_to_all(served.reshape(peer_count, capacity, served.shape[1]), 'dp...  7.05 us
    dot_general x1, matrix products, on_device(): jnp.einsum('hk,lkt->hlt', flattened_rows, adapter_down_maps, preferred_el...  3.34 us
    dot_general x1, matrix products, on_device(): jnp.dot(lax.all_gather(hidden, 'tensor', axis=1, tiled=True), key_value_w...  3 us
  transfers between devices with their start and end apart: 3, of which 2 were waited for; matrix products, arithmetic and copies ran while one was open for 18% of the time, Pallas kernels for 0%

commit v1 on v0

v1 whole, which is shorter than its diff:
```python
import jax
import jax.numpy as jnp
import numpy as np
from jax import lax
from jax.experimental import pallas as pl
from jax.experimental.pallas import tpu as pltpu
from jax.sharding import PartitionSpec as P

HEAD_SIZE = 128
GROUP = 8
CAPACITY = 2
LANES = 128
ROPE_BASE = 500000.0
MIB = 1 << 20

F32, BF16, I32 = jnp.float32, jnp.bfloat16, jnp.int32
VMEM = pl.BlockSpec(memory_space=pltpu.VMEM)
SMEM = pl.BlockSpec(memory_space=pltpu.SMEM)


def iota(shape, dim):
    return lax.broadcasted_iota(I32, shape, dim)


def dot(a, b):
    return jnp.dot(a, b, preferred_element_type=F32)


def dot_t(a, b):
    return lax.dot_general(a, b, (((1,), (1,)), ((), ())), preferred_element_type=F32)


def upright(row):
    n = row.shape[1]
    spread = jnp.broadcast_to(row, (n, n))
    return jnp.sum(jnp.where(iota((n, n), 0) == iota((n, n), 1), spread, 0.0), axis=1, keepdims=True)


def shuffle(chunks, forward):
    wide = 16 * chunks
    row, col = iota((wide, wide), 0), iota((wide, wide), 1)
    chunked, message = (col, row) if forward else (row, col)
    k, s, c = chunked >> 4, (chunked >> 1) & 7, chunked & 1
    return jnp.where(message == s * (2 * chunks) + k * 2 + c, 1.0, 0.0).astype(BF16)


def slots_of(tenant_row, pool):
    n = tenant_row.shape[1]
    owner_row = jnp.floor(tenant_row * (1.0 / pool))
    owner_col = upright(owner_row)
    same = (owner_col == owner_row) & (iota((n, n), 0) < iota((n, n), 1))
    rank = jnp.sum(jnp.where(same, 1.0, 0.0), axis=0, keepdims=True)
    return owner_row * CAPACITY + rank


def place_kernel(pool, tenant_ref, hidden_ref, out_ref):
    rows, width = hidden_ref.shape
    chunks = width // LANES + 1
    slots = out_ref.shape[0] // chunks
    tenant_row = tenant_ref[...].astype(F32)
    slot_row = slots_of(tenant_row, pool)
    place = jnp.where(slot_row == iota((slots, rows), 0).astype(F32), 1.0, 0.0).astype(BF16)
    local = tenant_row - pool * jnp.floor(tenant_row * (1.0 / pool))
    local = jnp.broadcast_to(upright(local), (rows, LANES)).astype(BF16)
    placed = jnp.concatenate([dot(place, hidden_ref[...]), dot(place, local)], axis=1).astype(BF16)
    groups = slots // 16
    side = jnp.concatenate(
        [
            jnp.concatenate(
                [placed[g * 16 : g * 16 + 16, k * LANES : (k + 1) * LANES] for k in range(chunks)], axis=0
            )
            for g in range(groups)
        ],
        axis=1,
    )
    turned = dot(shuffle(chunks, True), side).astype(BF16)
    wide = 16 * chunks
    for g in range(groups):
        out_ref[g * wide : (g + 1) * wide, :] = turned[:, g * LANES : (g + 1) * LANES]


def down_kernel(got_ref, down_ref, partial_ref, ids_ref):
    slots = ids_ref.shape[0]
    chunks = got_ref.shape[0] // slots
    groups, wide = slots // 16, 16 * chunks
    side = jnp.concatenate([got_ref[g * wide : (g + 1) * wide, :] for g in range(groups)], axis=1)
    turned = dot(shuffle(chunks, False), side)
    ids = jnp.concatenate([turned[wide - 16 :, g * LANES : (g + 1) * LANES] for g in range(groups)], axis=0)
    turned = turned.astype(BF16)
    rows = jnp.concatenate(
        [
            jnp.concatenate(
                [turned[k * 16 : k * 16 + 16, g * LANES : (g + 1) * LANES] for k in range(chunks - 1)], axis=1
            )
            for g in range(groups)
        ],
        axis=0,
    )
    full = dot_t(rows, down_ref[...])
    lane = iota((slots, LANES), 1)
    right = (lane >= 64).astype(F32)
    total = jnp.zeros((slots, LANES), F32)
    for q in range(full.shape[1] // LANES):
        total += jnp.where(ids == right + 2.0 * q, full[:, q * LANES : (q + 1) * LANES], 0.0)
    total = total + pltpu.roll(total, 64, 1)
    half = slots // 2
    partial_ref[...] = jnp.where(lane[:half] < 64, total[:half], total[half:])
    ids_ref[...] = ids


def up_kernel(a_ref, b_ref, c_ref, d_ref, ids_ref, up_ref, out_ref):
    total = (a_ref[...] + b_ref[...]) + (c_ref[...] + d_ref[...])
    turned = pltpu.roll(total, 64, 1)
    left = iota(total.shape, 1) < 64
    both = jnp.concatenate([jnp.where(left, total, turned), jnp.where(left, turned, total)], axis=0)
    ids = ids_ref[...]
    right = (iota(ids.shape, 1) >= 64).astype(F32)
    spread = [
        jnp.where(ids == right + 2.0 * q, both, 0.0).astype(BF16) for q in range(up_ref.shape[0] // LANES)
    ]
    out_ref[...] = dot(jnp.concatenate(spread, axis=1), up_ref[...]).astype(BF16)


def cache_kernel(scale, length_ref, query_ref, key_ref, value_ref, sum_ref, top_ref, weight_ref):
    step = pl.program_id(0)
    some, length = key_ref.shape[0], key_ref.shape[1]
    rows = sum_ref.shape[0] // GROUP
    wide = some * GROUP
    by_head = jnp.concatenate(
        [query_ref[:, h * LANES : (h + 1) * LANES] for h in range(GROUP)], axis=0
    )
    row, col = iota((wide, wide), 0), iota((wide, wide), 1)
    turn = jnp.where(col == (row % GROUP) * some + row // GROUP, 1.0, 0.0).astype(BF16)
    by_row = dot(turn, by_head)
    position = iota((GROUP, length), 1)
    for r in range(some):
        query = by_row[r * GROUP : (r + 1) * GROUP].astype(BF16)
        scores = dot_t(query, key_ref[r]) * scale
        scores = jnp.where(position < length_ref[step * some + r], scores, -jnp.inf)
        top = jnp.max(scores, axis=1, keepdims=True)
        weights = jnp.exp(scores - top)
        whole = jnp.sum(weights, axis=1, keepdims=True)
        place = pl.ds(step * some + r, GROUP, stride=rows)
        sum_ref[place, :] = dot(weights.astype(BF16), value_ref[r])
        top_ref[place, :] = jnp.broadcast_to(top, (GROUP, LANES))
        weight_ref[place, :] = jnp.broadcast_to(whole, (GROUP, LANES))


def project_kernel(scale, pool, index_ref, tenant_ref, length_ref, inverse_ref, query_ref, own_ref, core_ref, y1_ref,
                   y2_ref, y3_ref, weight_ref, sum_ref, top_ref, whole_ref, value_ref, key_ref, mixed_ref, share_ref,
                   back_ref):
    rows, depth = own_ref.shape
    me = index_ref[0]

    def part(block, other):
        start = pl.multiple_of(other * depth, depth)
        return dot(block, weight_ref[pl.ds(start, depth), :])

    total = part(own_ref[...], me) + part(core_ref[...], me ^ 1)
    count = weight_ref.shape[0] // depth
    for shift, ref in ((1, y1_ref), (2, y2_ref), (3, y3_ref)):
        other = (me + count - 2 * shift) % count
        total += part(ref[:rows], other) + part(ref[rows:], other ^ 1)
    value_ref[...] = total[:, LANES:]
    angle = upright(length_ref[...].astype(F32)) * inverse_ref[...]
    lane = iota((rows, LANES), 1)
    sine = jnp.sin(angle)
    key = total[:, :LANES]
    key = key * jnp.cos(angle) + pltpu.roll(key, 64, 1) * jnp.where(lane < 64, -sine, sine)
    key = key.astype(BF16)
    key_ref[...] = key
    key = key.astype(F32)
    for h in range(GROUP):
        place = slice(h * rows, (h + 1) * rows)
        query = query_ref[:, h * LANES : (h + 1) * LANES].astype(F32)
        own = jnp.sum(query * key, axis=1, keepdims=True) * scale
        top = top_ref[place, :]
        highest = jnp.maximum(top, own)
        old, new = jnp.exp(top - highest), jnp.exp(own - highest)
        under = 1.0 / (old * whole_ref[place, :] + new)
        mixed_ref[place, :] = sum_ref[place, :] * (old * under)
        share_ref[place, :] = new * under
    slot_col = upright(slots_of(tenant_ref[...].astype(F32), pool))
    back_ref[...] = jnp.where(slot_col == lane.astype(F32), 1.0, 0.0).astype(BF16)


def final_kernel(got_ref, back_ref, value_ref, key_ref, mixed_ref, share_ref, out_ref, entry_ref):
    rows = value_ref.shape[0]
    slots = got_ref.shape[0]
    delta = dot(back_ref[:, :slots], got_ref[...])
    value = (value_ref[...] + delta).astype(BF16)
    entry_ref[:, :LANES] = key_ref[...]
    entry_ref[:, LANES:] = value
    value = value.astype(F32)
    for h in range(GROUP):
        place = slice(h * rows, (h + 1) * rows)
        out_ref[:, h * LANES : (h + 1) * LANES] = (mixed_ref[place, :] + share_ref[place, :] * value).astype(BF16)


def on_device(hidden, queries, key_cache, value_cache, lengths, tenants, weight, down, up):
    rows, depth = hidden.shape
    peers = lax.axis_size("dp")
    count = lax.axis_size("tensor")
    slots = peers * CAPACITY
    pool, _, rank = down.shape
    chunks = depth // LANES + 1
    length = key_cache.shape[1]
    scale = HEAD_SIZE ** -0.5
    shape = jax.ShapeDtypeStruct
    params = lambda size: pltpu.CompilerParams(vmem_limit_bytes=size * MIB)
    cost = lambda flops, size: pl.CostEstimate(flops=flops, bytes_accessed=size, transcendentals=0)

    tenant_row = tenants.reshape(1, rows)
    length_row = lengths.reshape(1, rows)
    me = lax.axis_index("tensor").astype(I32).reshape(1)
    over_core = lambda x: lax.ppermute(x, "tensor", [(i, i ^ 1) for i in range(count)])
    over_y = lambda x, k: lax.ppermute(x, "tensor", [(i, (i + 2 * k) % count) for i in range(count)])

    with jax.named_scope("place"):
        placed = pl.pallas_call(
            lambda *refs: place_kernel(pool, *refs),
            out_shape=shape((slots * chunks, LANES), BF16),
            in_specs=[VMEM] * 2, out_specs=VMEM, compiler_params=params(8),
        )(tenant_row, hidden)
    with jax.named_scope("rows_to_owners"):
        got = lax.all_to_all(
            placed.reshape(peers, chunks, CAPACITY, LANES), "dp", split_axis=0, concat_axis=0, tiled=True
        ).reshape(slots * chunks, LANES)
    with jax.named_scope("gather_hidden"):
        core_hidden = over_core(hidden)
        pair = jnp.concatenate([hidden, core_hidden], axis=0)
        others = [over_y(pair, k) for k in (1, 2, 3)]
    with jax.named_scope("cache"):
        some = 8
        full = lambda n: pl.BlockSpec((GROUP * rows, LANES), lambda i: (0, 0))
        sums, tops, wholes = pl.pallas_call(
            lambda *refs: cache_kernel(scale, *refs),
            grid=(rows // some,),
            out_shape=[shape((GROUP * rows, LANES), F32)] * 3,
            in_specs=[
                SMEM,
                pl.BlockSpec((some, GROUP * LANES), lambda i: (i, 0)),
                pl.BlockSpec((some, length, LANES), lambda i: (i, 0, 0)),
                pl.BlockSpec((some, length, LANES), lambda i: (i, 0, 0)),
            ],
            out_specs=[full(0)] * 3,
            compiler_params=params(16),
            cost_estimate=cost(2 * 2 * rows * GROUP * length * LANES, 2 * rows * length * LANES * 2),
        )(lengths, queries, key_cache, value_cache)
    with jax.named_scope("down"):
        partial, ids = pl.pallas_call(
            down_kernel,
            out_shape=[shape((slots // 2, LANES), F32), shape((slots, LANES), F32)],
            in_specs=[VMEM] * 2, out_specs=[VMEM] * 2, compiler_params=params(16),
        )(got, jnp.swapaxes(down, 1, 2).reshape(pool * rank, depth))
    with jax.named_scope("reduce"):
        pair_sum = partial + over_core(partial)
        sums_y = [over_y(pair_sum, k) for k in (1, 2, 3)]
    with jax.named_scope("project"):
        inverse = ROPE_BASE ** (-(np.arange(HEAD_SIZE // 2, dtype=np.float32) * 2.0) / HEAD_SIZE)
        inverse = jnp.asarray(np.concatenate([inverse, inverse])[None, :], F32)
        value, key, mixed, share, back = pl.pallas_call(
            lambda *refs: project_kernel(scale, pool, *refs),
            out_shape=[
                shape((rows, LANES), F32), shape((rows, LANES), BF16),
                shape((GROUP * rows, LANES), F32), shape((GROUP * rows, LANES), F32),
                shape((rows, LANES), BF16),
            ],
            in_specs=[SMEM] + [VMEM] * 13, out_specs=[VMEM] * 5, compiler_params=params(24),
            cost_estimate=cost(2 * rows * count * depth * 2 * LANES, weight.size * 2),
        )(me, tenant_row, length_row, inverse, queries, hidden, core_hidden, *others, weight, sums, tops, wholes)
    with jax.named_scope("up"):
        served = pl.pallas_call(
            up_kernel, out_shape=shape((slots, LANES), BF16),
            in_specs=[VMEM] * 6, out_specs=VMEM, compiler_params=params(8),
        )(pair_sum, *sums_y, ids, up.reshape(pool * rank, LANES))
    with jax.named_scope("answers"):
        returned = lax.all_to_all(
            served.reshape(peers, CAPACITY, LANES), "dp", split_axis=0, concat_axis=0, tiled=True
        ).reshape(slots, LANES)
    with jax.named_scope("finish"):
        return tuple(pl.pallas_call(
            final_kernel,
            out_shape=[shape((rows, GROUP * LANES), BF16), shape((rows, 2 * LANES), BF16)],
            in_specs=[VMEM] * 6, out_specs=[VMEM] * 2, compiler_params=params(8),
        )(returned, back, value, key, mixed, share))


def solution(mesh):
    in_specs = (
        P("dp", "tensor"),
        P("dp", "tensor"),
        P("dp", None, "tensor"),
        P("dp", None, "tensor"),
        P("dp"),
        P("dp"),
        P(None, "tensor"),
        P("dp", "tensor", None),
        P("dp", None, "tensor"),
    )
    out_specs = (P("dp", "tensor"), P("dp", "tensor"))
    return jax.shard_map(
        on_device, mesh=mesh, in_specs=in_specs, out_specs=out_specs, check_vma=False
    )
```

time: 115 us -> 61.8 us (0.54)
  blocking collectives: 39.4 us -> 0 us
  matrix products: 15.6 us -> 0 us
  Pallas kernels: 0 us -> 14.6 us
  other arithmetic: 10.3 us -> 0.01 us
  starting transfers between devices: 29.8 us -> 27.1 us
  local copies, waits for them, and re-layouts: 8.33 us -> 9.69 us
    psum x1 -> x0, blocking collectives: 25.6 us -> none  [on_device(): rank_reduced = lax.psum(partial_rank, 'tensor').astype(jnp.bfloat16)]
    dot_general x8 -> x0, matrix products: 15.6 us -> none  [the longest x1 3.34 us: on_device(): jnp.einsum('hk,lkt->hlt', flattened_rows, adapter_down_maps, preferred_el...]
    pallas_call x0 -> x6, Pallas kernels: none -> 14.6 us  [the longest x1 8.99 us: on_device(): pl.pallas_call(lambda *refs: cache_kernel(scale, *refs), grid=(rows // so...]
    all_gather x1 -> x0, blocking collectives: 13.8 us -> none  [on_device(): lax.all_gather(hidden, 'tensor', axis=1, tiled=True)]
    all_to_all x3 -> x2, starting transfers between devices: 29.8 us -> 17.8 us  [the longest x1 11.6 us: on_device(): lax.all_to_all(placed.reshape(peers, chunks, CAPACITY, LANES), 'dp', spli...]
    ppermute x0 -> x8, starting transfers between devices: none -> 9.31 us  [the longest x6 9.13 us: on_device(): lax.ppermute(x, 'tensor', [(i, (i + 2 * k) % count) for i in range(count)])]
    unnamed x19 -> x27, local copies, waits for them, and re-layouts: 1.82 us -> 9.06 us
    all_to_all x3 -> x2, waiting for transfers between devices: 9.57 us -> 2.73 us  [the longest x1 2.72 us: on_device(): lax.all_to_all(placed.reshape(peers, chunks, CAPACITY, LANES), 'dp', spli...]
  transfers between devices with their start and end apart: 3 -> 10, of which waited for: 2 -> 5; matrix products, arithmetic and copies ran while one was open for 18% -> 3% of each run, Pallas kernels for 0% -> 22%
where the time goes in v1:
time: 61.8 us; the launch traced here: 61.4 us
  starting transfers between devices  27.1 us (44%)
  Pallas kernels  14.6 us (24%)
  local copies, waits for them, and re-layouts  9.69 us (16%)
  waiting for transfers between devices  9.2 us (15%)
  between operations  0.8 us (1%)
    all_to_all x1, starting transfers between devices, on_device(): lax.all_to_all(placed.reshape(peers, chunks, CAPACITY, LANES), 'dp', spli...  11.6 us
    ppermute x6, starting transfers between devices, on_device(): lax.ppermute(x, 'tensor', [(i, (i + 2 * k) % count) for i in range(count)])  9.13 us
    unnamed x27, local copies, waits for them, and re-layouts  9.06 us
    pallas_call x1, Pallas kernels, on_device(): pl.pallas_call(lambda *refs: cache_kernel(scale, *refs), grid=(rows // so...  8.99 us
    all_to_all x1, starting transfers between devices, on_device(): lax.all_to_all(served.reshape(peers, CAPACITY, LANES), 'dp', split_axis=0...  6.18 us
    ppermute x6, waiting for transfers between devices, on_device(): lax.ppermute(x, 'tensor', [(i, (i + 2 * k) % count) for i in range(count)])  5.3 us
    all_to_all x1, waiting for transfers between devices, on_device(): lax.all_to_all(placed.reshape(peers, chunks, CAPACITY, LANES), 'dp', spli...  2.72 us
    pallas_call x1, Pallas kernels, on_device(): pl.pallas_call(lambda *refs: project_kernel(scale, pool, *refs), out_shap...  1.96 us
  transfers between devices with their start and end apart: 10, of which 5 were waited for; matrix products, arithmetic and copies ran while one was open for 3% of the time, Pallas kernels for 22%

profile of v1, /device:TPU:2, one launch (start us, length us, event | category | flops | bytes accessed | tf_op | source)
XLA Modules:
  0.0 61.4 jit_solution(16606064606954474102)
XLA Ops:
  0.6 0.0 copy-start.1
  0.6 0.1 collective-permute-start.4
  0.7 0.0 copy-start.4
  0.8 1.0 %copy-done.4 = bf16[32,1024]{1,0:T(8,128)(2,1)S(1)} copy-done((bf16[32,1024]{1,0:T(8,128)(2,1)S(1)}, bf16[32,1024]{1,0:T(8,128)(2,1)}, u32[]{:S(2)}) %copy-start.4) | copy-done | bytes 65560
  1.7 0.0 copy-start.9
  1.7 0.7 %copy-done.9 = s32[32]{0:T(128)S(1)} copy-done((s32[32]{0:T(128)S(1)}, s32[32]{0:T(128)}, u32[]{:S(2)}) %copy-start.9) | copy-done | bytes 152
  2.4 1.1 %place.1 = bf16[576,128]{1,0:T(8,128)(2,1)} custom-call(s32[1,32]{1,0:T(1,128)S(1)} %bitcast.15, bf16[32,1024]{1,0:T(8,128)(2,1)S(1)} %copy-done.4), custom_call_target="tpu_custom_call" | custom-call | tf_op jit(solution)/shard_map/place/pallas_call | solution.py:220
  3.5 11.6 %all-to-all-start = ((bf16[32,9,2,128]{3,2,1,0:T(2,128)(2,1)}), bf16[32,9,2,128]{3,2,1,0:T(2,128)(2,1)S(1)}, u32[]{:S(2)}, u32[]{:S(2)}) async-start(bf16[32,9,2,128]{3,2,1,0:T(2,128)(2,1)} %bitcast.1), calls=%async_computation | async-start | bytes 294912 | tf_op jit(solution)/shard_map/rows_to_owners/all_to_all | solution.py:226
  15.1 1.5 %constant_dynamic-update-slice_fusion.1 = bf16[64,1024]{1,0:T(8,128)(2,1)} fusion(bf16[32,1024]{1,0:T(8,128)(2,1)} %refs_5_.1), kind=kLoop, calls=%fused_computation.1 | loop fusion | bytes 131072
  16.6 0.0 collective-permute-done.4.refs_6_
  16.6 0.6 %constant_dynamic-update-slice_fusion = bf16[64,1024]{1,0:T(8,128)(2,1)} fusion(bf16[64,1024]{1,0:T(8,128)(2,1)} %constant_dynamic-update-slice_fusion.1, bf16[32,1024]{1,0:T(8,128)(2,1)S(1)} %collective-permute-done.4.refs_6_), kind=kLoop, calls=%fused_computation | loop fusion | bytes 131072 | tf_op jit(solution)/shard_map/gather_hidden/concatenate | solution.py:231
  17.2 3.0 %collective-permute-start.7 = (bf16[64,1024]{1,0:T(8,128)(2,1)}, bf16[64,1024]{1,0:T(8,128)(2,1)S(1)}, u32[]{:S(2)}, u32[]{:S(2)}) collective-permute-start(bf16[64,1024]{1,0:T(8,128)(2,1)} %constant_dynamic-update-slice_fusion), channel_id=1, source_target_pairs={{0,6},{1,7},{2,0},{3,1},{4,2},{5,3},{6,4},{7,5},{8,14},{9,15},{10,... | collective-permute-start | bytes 393224 | tf_op jit(solution)/shard_map/gather_hidden/ppermute | solution.py:217
  20.2 0.6 %collective-permute-start.6 = (bf16[64,1024]{1,0:T(8,128)(2,1)}, bf16[64,1024]{1,0:T(8,128)(2,1)}, u32[]{:S(2)}, u32[]{:S(2)}) collective-permute-start(bf16[64,1024]{1,0:T(8,128)(2,1)} %constant_dynamic-update-slice_fusion), channel_id=1, source_target_pairs={{0,4},{1,5},{2,6},{3,7},{4,0},{5,1},{6,2},{7,3},{8,12},{9,13},{10,... | collective-permute-start | bytes 393224 | tf_op jit(solution)/shard_map/gather_hidden/ppermute | solution.py:217
  20.9 1.0 %collective-permute-start.5 = (bf16[64,1024]{1,0:T(8,128)(2,1)}, bf16[64,1024]{1,0:T(8,128)(2,1)}, u32[]{:S(2)}, u32[]{:S(2)}) collective-permute-start(bf16[64,1024]{1,0:T(8,128)(2,1)} %constant_dynamic-update-slice_fusion), channel_id=1, source_target_pairs={{0,2},{1,3},{2,4},{3,5},{4,6},{5,7},{6,0},{7,1},{8,10},{9,11},{10,... | collective-permute-start | bytes 393224 | tf_op jit(solution)/shard_map/gather_hidden/ppermute | solution.py:217
  21.8 2.7 %all-to-all-done = bf16[32,9,2,128]{3,2,1,0:T(2,128)(2,1)S(1)} async-done(((bf16[32,9,2,128]{3,2,1,0:T(2,128)(2,1)}), bf16[32,9,2,128]{3,2,1,0:T(2,128)(2,1)S(1)}, u32[]{:S(2)}, u32[]{:S(2)}) %all-to-all-start) | async-done | bytes 147488 | tf_op jit(solution)/shard_map/rows_to_owners/all_to_all | solution.py:226
  24.6 0.0 copy-start.3
  24.6 1.6 %copy-done.3 = bf16[16,1024,64]{1,2,0:T(8,128)(2,1)S(1)} copy-done((bf16[16,1024,64]{1,2,0:T(8,128)(2,1)S(1)}, bf16[16,1024,64]{1,2,0:T(8,128)(2,1)}, u32[]{:S(2)}) %copy-start.3) | copy-done | bytes 2097176
  26.2 0.9 %down.1 = (f32[32,128]{1,0:T(8,128)S(1)}, f32[64,128]{1,0:T(8,128)S(1)}) custom-call(bf16[576,128]{1,0:T(8,128)(2,1)S(1)} %bitcast.12, bf16[1024,1024]{1,0:T(8,128)(2,1)S(1)} %bitcast.11), custom_call_target="tpu_custom_call" | custom-call | tf_op jit(solution)/shard_map/down/pallas_call | solution.py:251
  27.1 0.1 collective-permute-start
  27.2 1.2 %collective-permute-done = f32[32,128]{1,0:T(8,128)S(1)} collective-permute-done((f32[32,128]{1,0:T(8,128)S(1)}, f32[32,128]{1,0:T(8,128)S(1)}, u32[]{:S(2)}, u32[]{:S(2)}) %collective-permute-start) | collective-permute-done | bytes 16416 | tf_op jit(solution)/shard_map/reduce/ppermute | solution.py:216
  28.3 3.0 %collective-permute-start.3 = (f32[32,128]{1,0:T(8,128)S(1)}, f32[32,128]{1,0:T(8,128)S(1)}, u32[]{:S(2)}, u32[]{:S(2)}) collective-permute-start(f32[32,128]{1,0:T(8,128)S(1)} %add.3.a_ref), channel_id=1, source_target_pairs={{0,6},{1,7},{2,0},{3,1},{4,2},{5,3},{6,4},{7,5},{8,14},{9,15},{10,... | collective-permute-start | bytes 49160 | tf_op jit(solution)/shard_map/reduce/ppermute | solution.py:217
  31.3 0.6 %collective-permute-start.2 = (f32[32,128]{1,0:T(8,128)S(1)}, f32[32,128]{1,0:T(8,128)S(1)}, u32[]{:S(2)}, u32[]{:S(2)}) collective-permute-start(f32[32,128]{1,0:T(8,128)S(1)} %add.3.a_ref), channel_id=1, source_target_pairs={{0,4},{1,5},{2,6},{3,7},{4,0},{5,1},{6,2},{7,3},{8,12},{9,13},{10,... | collective-permute-start | bytes 49160 | tf_op jit(solution)/shard_map/reduce/ppermute | solution.py:217
  32.0 0.8 %collective-permute-done.3.d_ref = f32[32,128]{1,0:T(8,128)S(1)} collective-permute-done((f32[32,128]{1,0:T(8,128)S(1)}, f32[32,128]{1,0:T(8,128)S(1)}, u32[]{:S(2)}, u32[]{:S(2)}) %collective-permute-start.3) | collective-permute-done | bytes 16416 | tf_op jit(solution)/shard_map/reduce/ppermute | solution.py:217
  32.8 0.9 %collective-permute-start.1 = (f32[32,128]{1,0:T(8,128)S(1)}, f32[32,128]{1,0:T(8,128)S(1)}, u32[]{:S(2)}, u32[]{:S(2)}) collective-permute-start(f32[32,128]{1,0:T(8,128)S(1)} %add.3.a_ref), channel_id=1, source_target_pairs={{0,2},{1,3},{2,4},{3,5},{4,6},{5,7},{6,0},{7,1},{8,10},{9,11},{10,... | collective-permute-start | bytes 49160 | tf_op jit(solution)/shard_map/reduce/ppermute | solution.py:217
  33.7 2.9 %collective-permute-done.2.c_ref = f32[32,128]{1,0:T(8,128)S(1)} collective-permute-done((f32[32,128]{1,0:T(8,128)S(1)}, f32[32,128]{1,0:T(8,128)S(1)}, u32[]{:S(2)}, u32[]{:S(2)}) %collective-permute-start.2) | collective-permute-done | bytes 16416 | tf_op jit(solution)/shard_map/reduce/ppermute | solution.py:217
  36.6 1.6 %collective-permute-done.1.b_ref = f32[32,128]{1,0:T(8,128)S(1)} collective-permute-done((f32[32,128]{1,0:T(8,128)S(1)}, f32[32,128]{1,0:T(8,128)S(1)}, u32[]{:S(2)}, u32[]{:S(2)}) %collective-permute-start.1) | collective-permute-done | bytes 16416 | tf_op jit(solution)/shard_map/reduce/ppermute | solution.py:217
  38.1 0.0 copy-start.8
  38.1 0.9 %copy-done.8 = bf16[16,64,128]{2,1,0:T(8,128)(2,1)S(1)} copy-done((bf16[16,64,128]{2,1,0:T(8,128)(2,1)S(1)}, bf16[16,64,128]{2,1,0:T(8,128)(2,1)}, u32[]{:S(2)}) %copy-start.8) | copy-done | bytes 262168
  39.1 0.8 %up.1 = bf16[64,128]{1,0:T(8,128)(2,1)} custom-call(f32[32,128]{1,0:T(8,128)S(1)} %add.3.a_ref, f32[32,128]{1,0:T(8,128)S(1)} %collective-permute-done.1.b_ref, f32[32,128]{1,0:T(8,128)S(1)} %collective-permute-done.2.c_ref, f32[32,128]{1,0:T(8,128)S(1)} %collective-permute-done.3.d_ref, f32[64,128]{1,0:T(8,128)S(1)} %get-tuple-element.13.ids_ref, ...), custom_call_target="tpu_custom_call" | custom-call | tf_op jit(solution)/shard_map/up/pallas_call | solution.py:273
  39.9 6.2 %all-to-all-start.1 = ((bf16[32,2,128]{2,1,0:T(2,128)(2,1)}), bf16[32,2,128]{2,1,0:T(2,128)(2,1)S(1)}, u32[]{:S(2)}, u32[]{:S(2)}) async-start(bf16[32,2,128]{2,1,0:T(2,128)(2,1)} %bitcast.6), calls=%async_computation.1 | async-start | bytes 32768 | tf_op jit(solution)/shard_map/answers/all_to_all | solution.py:278
  46.1 0.0 copy-done.1
  46.1 0.0 copy-start.2
  46.2 1.9 %copy-done.2 = bf16[32,384,128]{2,1,0:T(8,128)(2,1)S(1)} copy-done((bf16[32,384,128]{2,1,0:T(8,128)(2,1)S(1)}, bf16[32,384,128]{2,1,0:T(8,128)(2,1)}, u32[]{:S(2)}) %copy-start.2) | copy-done | bytes 3145752
  48.0 0.8 %copy-done.6 = bf16[32,1024]{1,0:T(8,128)(2,1)S(1)} copy-done((bf16[32,1024]{1,0:T(8,128)(2,1)S(1)}, bf16[32,1024]{1,0:T(8,128)(2,1)}, u32[]{:S(2)}) %copy-start.6) | copy-done | bytes 65560
  48.9 0.7 %copy-done.11 = s32[32]{0:T(128)S(1)} copy-done((s32[32]{0:T(128)S(1)}, s32[32]{0:T(128)}, u32[]{:S(2)}) %copy-start.11) | copy-done | bytes 152
  49.5 0.0 copy-start.12
  49.6 9.0 %cache.1 = (f32[256,128]{1,0:T(8,128)S(1)}, f32[256,128]{1,0:T(8,128)S(1)}, f32[256,128]{1,0:T(8,128)S(1)}) custom-call(s32[32]{0:T(128)S(1)} %copy-done.11, bf16[32,1024]{1,0:T(8,128)(2,1)S(1)} %copy-done.6, bf16[32,384,128]{2,1,0:T(8,128)(2,1)S(1)} %copy-done.1, bf16[32,384,128]{2,1,0:T(8,128)(2,1)S(1)} %copy-done.2), custom_call_target="tpu_custom_call" | custom-call | flops 50331648 | bytes 6291456 | tf_op jit(solution)/shard_map/cache/pallas_call | solution.py:236
  58.5 0.0 collective-permute-done.7.refs_9_
  58.6 0.0 collective-permute-done.6.refs_8_
  58.6 0.0 collective-permute-done.5.refs_7_
  58.6 0.0 copy-done
  58.6 0.0 copy-done.5
  58.6 0.0 copy-done.7
  58.6 0.0 copy-done.10
  58.6 0.0 copy-done.12
  58.6 2.0 %project.1 = (f32[32,128]{1,0:T(8,128)S(1)}, bf16[32,128]{1,0:T(8,128)(2,1)S(1)}, f32[256,128]{1,0:T(8,128)S(1)}, f32[256,128]{1,0:T(8,128)S(1)}, bf16[32,128]{1,0:T(8,128)(2,1)S(1)}) custom-call(s32[1]{0:T(128)} %bitcast.8.refs_0_, s32[1,32]{1,0:T(1,128)S(1)} %bitcast.16, s32[1,32]{1,0:T(1,128)S(1)} %bitcast.17, f32[1,128]{1,0:T(1,128)S(1)} %copy-done.12, ...), custom_call_target="tpu_custom_call" | custom-call | flops 134217728 | bytes 4194304 | tf_op jit(solution)/shard_map/project/pallas_call | solution.py:262
  60.6 0.0 all-to-all-done.1
  60.6 0.8 %finish.1 = (bf16[32,1024]{1,0:T(8,128)(2,1)}, bf16[32,256]{1,0:T(8,128)(2,1)}) custom-call(bf16[64,128]{1,0:T(8,128)(2,1)S(1)} %bitcast.14, bf16[32,128]{1,0:T(8,128)(2,1)S(1)} %get-tuple-element.17.back_ref, f32[32,128]{1,0:T(8,128)S(1)} %get-tuple-element.18.value_ref, bf16[32,128]{1,0:T(8,128)(2,1)S(1)} %get-tuple-element.19.key_ref, ...), custom_call_target="tpu_custom_call" | custom-call | tf_op jit(solution)/shard_map/finish/pallas_call | solution.py:282
  (7 shorter events, 0.0 us)
Async XLA Ops:
  0.6 45.5 %copy-start.1 = (bf16[32,384,128]{2,1,0:T(8,128)(2,1)S(1)}, bf16[32,384,128]{2,1,0:T(8,128)(2,1)}, u32[]{:S(2)}) copy-start(bf16[32,384,128]{2,1,0:T(8,128)(2,1)} %refs_2_.1) | copy-start | bytes 9437188
  0.6 15.9 %collective-permute-start.4 = (bf16[32,1024]{1,0:T(8,128)(2,1)}, bf16[32,1024]{1,0:T(8,128)(2,1)S(1)}, u32[]{:S(2)}, u32[]{:S(2)}) collective-permute-start(bf16[32,1024]{1,0:T(8,128)(2,1)} %refs_5_.1), channel_id=1, source_target_pairs={{0,1},{1,0},{2,3},{3,2},{4,5},{5,4},{6,7},{7,6},{8,9},{9,8},{10,11... | collective-permute-start | bytes 196616 | tf_op jit(solution)/shard_map/gather_hidden/ppermute | solution.py:216
  0.7 1.0 %copy-start.4 = (bf16[32,1024]{1,0:T(8,128)(2,1)S(1)}, bf16[32,1024]{1,0:T(8,128)(2,1)}, u32[]{:S(2)}) copy-start(bf16[32,1024]{1,0:T(8,128)(2,1)} %refs_5_.1) | copy-start | bytes 196612
  1.7 0.7 %copy-start.9 = (s32[32]{0:T(128)S(1)}, s32[32]{0:T(128)}, u32[]{:S(2)}) copy-start(s32[32]{0:T(128)} %param.15) | copy-start | bytes 388
  3.5 21.1 %all-to-all-start = ((bf16[32,9,2,128]{3,2,1,0:T(2,128)(2,1)}), bf16[32,9,2,128]{3,2,1,0:T(2,128)(2,1)S(1)}, u32[]{:S(2)}, u32[]{:S(2)}) async-start(bf16[32,9,2,128]{3,2,1,0:T(2,128)(2,1)} %bitcast.1), calls=%async_computation | async-start | bytes 294912 | tf_op jit(solution)/shard_map/rows_to_owners/all_to_all | solution.py:226
  17.2 41.3 %collective-permute-start.7 = (bf16[64,1024]{1,0:T(8,128)(2,1)}, bf16[64,1024]{1,0:T(8,128)(2,1)S(1)}, u32[]{:S(2)}, u32[]{:S(2)}) collective-permute-start(bf16[64,1024]{1,0:T(8,128)(2,1)} %constant_dynamic-update-slice_fusion), channel_id=1, source_target_pairs={{0,6},{1,7},{2,0},{3,1},{4,2},{5,3},{6,4},{7,5},{8,14},{9,15},{10,... | collective-permute-start | bytes 393224 | tf_op jit(solution)/shard_map/gather_hidden/ppermute | solution.py:217
  20.2 38.3 %collective-permute-start.6 = (bf16[64,1024]{1,0:T(8,128)(2,1)}, bf16[64,1024]{1,0:T(8,128)(2,1)}, u32[]{:S(2)}, u32[]{:S(2)}) collective-permute-start(bf16[64,1024]{1,0:T(8,128)(2,1)} %constant_dynamic-update-slice_fusion), channel_id=1, source_target_pairs={{0,4},{1,5},{2,6},{3,7},{4,0},{5,1},{6,2},{7,3},{8,12},{9,13},{10,... | collective-permute-start | bytes 393224 | tf_op jit(solution)/shard_map/gather_hidden/ppermute | solution.py:217
  20.9 37.7 %collective-permute-start.5 = (bf16[64,1024]{1,0:T(8,128)(2,1)}, bf16[64,1024]{1,0:T(8,128)(2,1)}, u32[]{:S(2)}, u32[]{:S(2)}) collective-permute-start(bf16[64,1024]{1,0:T(8,128)(2,1)} %constant_dynamic-update-slice_fusion), channel_id=1, source_target_pairs={{0,2},{1,3},{2,4},{3,5},{4,6},{5,7},{6,0},{7,1},{8,10},{9,11},{10,... | collective-permute-start | bytes 393224 | tf_op jit(solution)/shard_map/gather_hidden/ppermute | solution.py:217
  24.6 1.6 %copy-start.3 = (bf16[16,1024,64]{1,2,0:T(8,128)(2,1)S(1)}, bf16[16,1024,64]{1,2,0:T(8,128)(2,1)}, u32[]{:S(2)}) copy-start(bf16[16,1024,64]{1,2,0:T(8,128)(2,1)} %param.17) | copy-start | bytes 6291460
  27.1 1.3 %collective-permute-start = (f32[32,128]{1,0:T(8,128)S(1)}, f32[32,128]{1,0:T(8,128)S(1)}, u32[]{:S(2)}, u32[]{:S(2)}) collective-permute-start(f32[32,128]{1,0:T(8,128)S(1)} %get-tuple-element.12), channel_id=1, source_target_pairs={{0,1},{1,0},{2,3},{3,2},{4,5},{5,4},{6,7},{7,6},{8,9},{9,8},{10,11... | collective-permute-start | bytes 49160 | tf_op jit(solution)/shard_map/reduce/ppermute | solution.py:216
  28.3 4.5 %collective-permute-start.3 = (f32[32,128]{1,0:T(8,128)S(1)}, f32[32,128]{1,0:T(8,128)S(1)}, u32[]{:S(2)}, u32[]{:S(2)}) collective-permute-start(f32[32,128]{1,0:T(8,128)S(1)} %add.3.a_ref), channel_id=1, source_target_pairs={{0,6},{1,7},{2,0},{3,1},{4,2},{5,3},{6,4},{7,5},{8,14},{9,15},{10,... | collective-permute-start | bytes 49160 | tf_op jit(solution)/shard_map/reduce/ppermute | solution.py:217
  31.3 5.2 %collective-permute-start.2 = (f32[32,128]{1,0:T(8,128)S(1)}, f32[32,128]{1,0:T(8,128)S(1)}, u32[]{:S(2)}, u32[]{:S(2)}) collective-permute-start(f32[32,128]{1,0:T(8,128)S(1)} %add.3.a_ref), channel_id=1, source_target_pairs={{0,4},{1,5},{2,6},{3,7},{4,0},{5,1},{6,2},{7,3},{8,12},{9,13},{10,... | collective-permute-start | bytes 49160 | tf_op jit(solution)/shard_map/reduce/ppermute | solution.py:217
  32.8 5.3 %collective-permute-start.1 = (f32[32,128]{1,0:T(8,128)S(1)}, f32[32,128]{1,0:T(8,128)S(1)}, u32[]{:S(2)}, u32[]{:S(2)}) collective-permute-start(f32[32,128]{1,0:T(8,128)S(1)} %add.3.a_ref), channel_id=1, source_target_pairs={{0,2},{1,3},{2,4},{3,5},{4,6},{5,7},{6,0},{7,1},{8,10},{9,11},{10,... | collective-permute-start | bytes 49160 | tf_op jit(solution)/shard_map/reduce/ppermute | solution.py:217
  38.1 1.0 %copy-start.8 = (bf16[16,64,128]{2,1,0:T(8,128)(2,1)S(1)}, bf16[16,64,128]{2,1,0:T(8,128)(2,1)}, u32[]{:S(2)}) copy-start(bf16[16,64,128]{2,1,0:T(8,128)(2,1)} %param.18) | copy-start | bytes 786436
  39.9 20.7 %all-to-all-start.1 = ((bf16[32,2,128]{2,1,0:T(2,128)(2,1)}), bf16[32,2,128]{2,1,0:T(2,128)(2,1)S(1)}, u32[]{:S(2)}, u32[]{:S(2)}) async-start(bf16[32,2,128]{2,1,0:T(2,128)(2,1)} %bitcast.6), calls=%async_computation.1 | async-start | bytes 32768 | tf_op jit(solution)/shard_map/answers/all_to_all | solution.py:278
  46.1 1.9 %copy-start.2 = (bf16[32,384,128]{2,1,0:T(8,128)(2,1)S(1)}, bf16[32,384,128]{2,1,0:T(8,128)(2,1)}, u32[]{:S(2)}) copy-start(bf16[32,384,128]{2,1,0:T(8,128)(2,1)} %refs_3_.2) | copy-start | bytes 9437188
  48.0 0.8 %copy-start.6 = (bf16[32,1024]{1,0:T(8,128)(2,1)S(1)}, bf16[32,1024]{1,0:T(8,128)(2,1)}, u32[]{:S(2)}) copy-start(bf16[32,1024]{1,0:T(8,128)(2,1)} %refs_4_.1) | copy-start | bytes 196612
  48.9 0.7 %copy-start.11 = (s32[32]{0:T(128)S(1)}, s32[32]{0:T(128)}, u32[]{:S(2)}) copy-start(s32[32]{0:T(128)} %refs_0_.1) | copy-start | bytes 388
  49.5 9.0 %copy-start = (bf16[8192,256]{1,0:T(8,128)(2,1)S(1)}, bf16[8192,256]{1,0:T(8,128)(2,1)}, u32[]{:S(2)}) copy-start(bf16[8192,256]{1,0:T(8,128)(2,1)} %refs_10_.1) | copy-start | bytes 12582916
  49.5 9.1 %copy-start.5 = (bf16[32,1024]{1,0:T(8,128)(2,1)S(1)}, bf16[32,1024]{1,0:T(8,128)(2,1)}, u32[]{:S(2)}) copy-start(bf16[32,1024]{1,0:T(8,128)(2,1)} %refs_5_.1) | copy-start | bytes 196612
  49.5 9.1 %copy-start.7 = (bf16[32,1024]{1,0:T(8,128)(2,1)S(1)}, bf16[32,1024]{1,0:T(8,128)(2,1)}, u32[]{:S(2)}) copy-start(bf16[32,1024]{1,0:T(8,128)(2,1)} %refs_4_.1) | copy-start | bytes 196612
  49.5 9.1 %copy-start.10 = (s32[32]{0:T(128)S(1)}, s32[32]{0:T(128)}, u32[]{:S(2)}) copy-start(s32[32]{0:T(128)} %param.15) | copy-start | bytes 388
  49.5 9.1 %copy-start.12 = (f32[1,128]{1,0:T(1,128)S(1)}, f32[1,128]{1,0:T(1,128)}, u32[]{:S(2)}) copy-start(f32[1,128]{1,0:T(1,128)} %constant.6.clone.refs_3_) | copy-start | bytes 1540

commit v2 on v1

v2 whole, which is shorter than its diff:
```python
import jax
import jax.numpy as jnp
import numpy as np
from jax import lax
from jax.experimental import pallas as pl
from jax.experimental.pallas import tpu as pltpu
from jax.sharding import PartitionSpec as P

HEAD_SIZE = 128
GROUP = 8
CAPACITY = 2
LANES = 128
ROPE_BASE = 500000.0
MIB = 1 << 20
EARLY_ROWS = 16

F32, BF16, I32 = jnp.float32, jnp.bfloat16, jnp.int32
VMEM = pl.BlockSpec(memory_space=pltpu.VMEM)
SMEM = pl.BlockSpec(memory_space=pltpu.SMEM)
HBM = pl.BlockSpec(memory_space=pltpu.HBM)
ANY = pl.BlockSpec(memory_space=pl.ANY)


def iota(shape, dim):
    return lax.broadcasted_iota(I32, shape, dim)


def dot(a, b):
    return jnp.dot(a, b, preferred_element_type=F32)


def dot_t(a, b):
    return lax.dot_general(a, b, (((1,), (1,)), ((), ())), preferred_element_type=F32)


def upright(row):
    n = row.shape[1]
    spread = jnp.broadcast_to(row, (n, n))
    return jnp.sum(jnp.where(iota((n, n), 0) == iota((n, n), 1), spread, 0.0), axis=1, keepdims=True)


def shuffle(chunks, forward):
    wide = 16 * chunks
    row, col = iota((wide, wide), 0), iota((wide, wide), 1)
    chunked, message = (col, row) if forward else (row, col)
    k, s, c = chunked >> 4, (chunked >> 1) & 7, chunked & 1
    return jnp.where(message == s * (2 * chunks) + k * 2 + c, 1.0, 0.0).astype(BF16)


def slots_of(tenant_row, pool):
    n = tenant_row.shape[1]
    owner_row = jnp.floor(tenant_row * (1.0 / pool))
    owner_col = upright(owner_row)
    same = (owner_col == owner_row) & (iota((n, n), 0) < iota((n, n), 1))
    rank = jnp.sum(jnp.where(same, 1.0, 0.0), axis=0, keepdims=True)
    return owner_row * CAPACITY + rank


def place_kernel(pool, tenant_hbm, hidden_hbm, out_ref, tenant_ref, hidden_ref, sems):
    fetch_hidden = pltpu.make_async_copy(hidden_hbm, hidden_ref, sems.at[0])
    fetch_tenant = pltpu.make_async_copy(tenant_hbm, tenant_ref, sems.at[1])
    fetch_tenant.start()
    fetch_hidden.start()
    rows, width = hidden_ref.shape
    chunks = width // LANES + 1
    slots = out_ref.shape[0] // chunks
    mix = shuffle(chunks, True)
    fetch_tenant.wait()
    tenant_row = tenant_ref[...].astype(F32)
    slot_row = slots_of(tenant_row, pool)
    place = jnp.where(slot_row == iota((slots, rows), 0).astype(F32), 1.0, 0.0).astype(BF16)
    local = tenant_row - pool * jnp.floor(tenant_row * (1.0 / pool))
    local = jnp.broadcast_to(upright(local), (rows, LANES)).astype(BF16)
    fetch_hidden.wait()
    placed = jnp.concatenate([dot(place, hidden_ref[...]), dot(place, local)], axis=1).astype(BF16)
    groups = slots // 16
    side = jnp.concatenate(
        [
            jnp.concatenate(
                [placed[g * 16 : g * 16 + 16, k * LANES : (k + 1) * LANES] for k in range(chunks)], axis=0
            )
            for g in range(groups)
        ],
        axis=1,
    )
    turned = dot(mix, side).astype(BF16)
    wide = 16 * chunks
    for g in range(groups):
        out_ref[g * wide : (g + 1) * wide, :] = turned[:, g * LANES : (g + 1) * LANES]


def down_kernel(got_ref, down_ref, up_hbm, after_ref, partial_ref, ids_ref, up_ref, sem):
    fetch_up = pltpu.make_async_copy(up_hbm, up_ref, sem)
    fetch_up.start()
    slots = ids_ref.shape[0]
    chunks = got_ref.shape[0] // slots
    groups, wide = slots // 16, 16 * chunks
    side = jnp.concatenate([got_ref[g * wide : (g + 1) * wide, :] for g in range(groups)], axis=1)
    turned = dot(shuffle(chunks, False), side)
    ids = jnp.concatenate([turned[wide - 16 :, g * LANES : (g + 1) * LANES] for g in range(groups)], axis=0)
    turned = turned.astype(BF16)
    rows = jnp.concatenate(
        [
            jnp.concatenate(
                [turned[k * 16 : k * 16 + 16, g * LANES : (g + 1) * LANES] for k in range(chunks - 1)], axis=1
            )
            for g in range(groups)
        ],
        axis=0,
    )
    full = dot_t(rows, down_ref[...])
    lane = iota((slots, LANES), 1)
    right = (lane >= 64).astype(F32)
    total = jnp.zeros((slots, LANES), F32)
    for q in range(full.shape[1] // LANES):
        total += jnp.where(ids == right + 2.0 * q, full[:, q * LANES : (q + 1) * LANES], 0.0)
    total = total + pltpu.roll(total, 64, 1)
    half = slots // 2
    partial_ref[...] = jnp.where(lane[:half] < 64, total[:half], total[half:])
    ids_ref[...] = ids
    fetch_up.wait()


def up_kernel(a_ref, b_ref, c_ref, d_ref, ids_ref, up_ref, out_ref):
    total = (a_ref[...] + b_ref[...]) + (c_ref[...] + d_ref[...])
    turned = pltpu.roll(total, 64, 1)
    left = iota(total.shape, 1) < 64
    both = jnp.concatenate([jnp.where(left, total, turned), jnp.where(left, turned, total)], axis=0)
    ids = ids_ref[...]
    right = (iota(ids.shape, 1) >= 64).astype(F32)
    spread = [
        jnp.where(ids == right + 2.0 * q, both, 0.0).astype(BF16) for q in range(up_ref.shape[0] // LANES)
    ]
    out_ref[...] = dot(jnp.concatenate(spread, axis=1), up_ref[...]).astype(BF16)


def attend_cache(scale, first, count, rows, length_at, query_ref, key_ref, value_ref, wait_key, wait_value, sum_ref,
                 top_ref, whole_ref):
    length = key_ref.shape[1]
    wide = count * GROUP
    by_head = jnp.concatenate([query_ref[:, h * LANES : (h + 1) * LANES] for h in range(GROUP)], axis=0)
    row, col = iota((wide, GROUP * rows), 0), iota((wide, GROUP * rows), 1)
    turn = jnp.where(col == (row % GROUP) * rows + row // GROUP + first, 1.0, 0.0).astype(BF16)
    by_row = dot(turn, by_head)
    position = iota((GROUP, length), 1)
    wait_key()
    scores = []
    for r in range(count):
        query = by_row[r * GROUP : (r + 1) * GROUP].astype(BF16)
        score = dot_t(query, key_ref[r]) * scale
        scores.append(jnp.where(position < length_at(first + r), score, -jnp.inf))
    scores = jnp.concatenate(scores, axis=0)
    top = jnp.max(scores, axis=1, keepdims=True)
    weights = jnp.exp(scores - top)
    whole = jnp.broadcast_to(jnp.sum(weights, axis=1, keepdims=True), (wide, LANES))
    top = jnp.broadcast_to(top, (wide, LANES))
    wait_value()
    for r in range(count):
        some = slice(r * GROUP, (r + 1) * GROUP)
        place = pl.ds(r, GROUP, stride=count)
        sum_ref[place, :] = dot(weights[some].astype(BF16), value_ref[r])
        top_ref[place, :] = top[some]
        whole_ref[place, :] = whole[some]


def fetches(pairs, sems):
    copies = [pltpu.make_async_copy(source, target, sems.at[i]) for i, (source, target) in enumerate(pairs)]
    for copy in copies:
        copy.start()
    return copies


def early_kernel(scale, count, after_ref, length_hbm, query_hbm, key_hbm, value_hbm, own_hbm, core_hbm, sum_ref,
                 top_ref, whole_ref, pair_ref, length_ref, query_ref, key_ref, value_ref, sems):
    rows = query_ref.shape[0]
    some = pl.ds(0, count)
    copies = fetches(
        [
            (query_hbm, query_ref), (length_hbm, length_ref), (key_hbm.at[some], key_ref),
            (value_hbm.at[some], value_ref), (own_hbm, pair_ref.at[pl.ds(0, rows)]),
            (core_hbm, pair_ref.at[pl.ds(rows, rows)]),
        ],
        sems,
    )
    copies[0].wait()
    copies[1].wait()
    attend_cache(scale, 0, count, rows, lambda r: length_ref[r], query_ref, key_ref, value_ref, copies[2].wait,
                 copies[3].wait, sum_ref, top_ref, whole_ref)
    copies[4].wait()
    copies[5].wait()


def late_kernel(scale, pool, index_ref, after_ref, tenant_hbm, length_hbm, row_hbm, inverse_hbm, query_hbm, key_hbm,
                value_hbm, own_hbm, core_hbm, y1_hbm, y2_hbm, y3_hbm, weight_hbm, sum_ref, top_ref, whole_ref,
                projected_ref, entry_ref, mixed_ref, share_ref, back_ref, tenant_ref, length_ref, row_ref, inverse_ref,
                query_ref, key_ref, value_ref, own_ref, core_ref, y1_ref, y2_ref, y3_ref, weight_ref, sum2_ref, top2_ref,
                whole2_ref, sems, weight_sems):
    rows, depth = own_ref.shape
    count = key_ref.shape[0]
    first = rows - count
    some = pl.ds(first, count)
    me = index_ref[0]
    devices = weight_ref.shape[0] // depth
    copies = fetches(
        [
            (query_hbm, query_ref), (length_hbm, length_ref), (key_hbm.at[some], key_ref),
            (value_hbm.at[some], value_ref), (tenant_hbm, tenant_ref), (row_hbm, row_ref),
            (inverse_hbm, inverse_ref), (own_hbm, own_ref), (core_hbm, core_ref), (y1_hbm, y1_ref), (y2_hbm, y2_ref),
            (y3_hbm, y3_ref),
        ],
        sems,
    )
    blocks = [pl.ds(k * depth, depth) for k in range(devices)]
    weights = fetches([(weight_hbm.at[block], weight_ref.at[block]) for block in blocks], weight_sems)
    copies[0].wait()
    copies[1].wait()
    attend_cache(scale, first, count, rows, lambda r: length_ref[r], query_ref, key_ref, value_ref, copies[2].wait,
                 copies[3].wait, sum2_ref, top2_ref, whole2_ref)
    for copy in copies[4:] + weights:
        copy.wait()

    def part(block, other):
        start = pl.multiple_of(other * depth, depth)
        return dot(block, weight_ref[pl.ds(start, depth), :])

    total = part(own_ref[...], me) + part(core_ref[...], me ^ 1)
    for shift, ref in ((1, y1_ref), (2, y2_ref), (3, y3_ref)):
        other = (me + devices - 2 * shift) % devices
        total += part(ref[:rows], other) + part(ref[rows:], other ^ 1)
    projected_ref[...] = total[:, LANES:]
    angle = upright(row_ref[...].astype(F32)) * inverse_ref[...]
    lane = iota((rows, LANES), 1)
    sine = jnp.sin(angle)
    key = total[:, :LANES]
    key = key * jnp.cos(angle) + pltpu.roll(key, 64, 1) * jnp.where(lane < 64, -sine, sine)
    key = key.astype(BF16)
    entry_ref[...] = key
    key = key.astype(F32)
    halves = ((0, first, sum_ref, top_ref, whole_ref), (first, count, sum2_ref, top2_ref, whole2_ref))
    for h in range(GROUP):
        query = query_ref[:, h * LANES : (h + 1) * LANES].astype(F32)
        own = jnp.sum(query * key, axis=1, keepdims=True) * scale
        for start, many, sums, tops, wholes in halves:
            if many:
                here, place = slice(h * many, (h + 1) * many), slice(h * rows + start, h * rows + start + many)
                mine, top = own[start : start + many], tops[here, :]
                highest = jnp.maximum(top, mine)
                old, new = jnp.exp(top - highest), jnp.exp(mine - highest)
                under = 1.0 / (old * wholes[here, :] + new)
                mixed_ref[place, :] = sums[here, :] * (old * under)
                share_ref[place, :] = new * under
    slot_col = upright(slots_of(tenant_ref[...].astype(F32), pool))
    back_ref[...] = jnp.where(slot_col == lane.astype(F32), 1.0, 0.0).astype(BF16)


def final_kernel(got_ref, back_ref, value_ref, key_ref, mixed_ref, share_ref, out_ref, entry_ref):
    rows = value_ref.shape[0]
    slots = got_ref.shape[0]
    delta = dot(back_ref[:, :slots], got_ref[...])
    value = (value_ref[...] + delta).astype(BF16)
    entry_ref[:, :LANES] = key_ref[...]
    entry_ref[:, LANES:] = value
    value = value.astype(F32)
    for h in range(GROUP):
        place = slice(h * rows, (h + 1) * rows)
        out_ref[:, h * LANES : (h + 1) * LANES] = (mixed_ref[place, :] + share_ref[place, :] * value).astype(BF16)


def on_device(hidden, queries, key_cache, value_cache, lengths, tenants, weight, down, up):
    rows, depth = hidden.shape
    peers = lax.axis_size("dp")
    count = lax.axis_size("tensor")
    slots = peers * CAPACITY
    pool, _, rank = down.shape
    chunks = depth // LANES + 1
    length = key_cache.shape[1]
    scale = HEAD_SIZE ** -0.5
    early = EARLY_ROWS
    late = rows - early
    shape, vmem, dma = jax.ShapeDtypeStruct, pltpu.VMEM, pltpu.SemaphoreType.DMA
    params = lambda size: pltpu.CompilerParams(vmem_limit_bytes=size * MIB)
    far = lambda *arrays: [pltpu.with_memory_space_constraint(x, pltpu.HBM) for x in arrays]
    cost = lambda flops, size: pl.CostEstimate(flops=flops, bytes_accessed=size, transcendentals=0)

    tenant_row = tenants.reshape(1, rows)
    length_row = lengths.reshape(1, rows)
    me = lax.axis_index("tensor").astype(I32).reshape(1)
    over_core = lambda x: lax.ppermute(x, "tensor", [(i, i ^ 1) for i in range(count)])
    over_y = lambda x, k: lax.ppermute(x, "tensor", [(i, (i + 2 * k) % count) for i in range(count)])
    states = lambda n: [shape((GROUP * n, LANES), F32)] * 3
    cache = lambda n: [vmem((n, length, LANES), BF16)] * 2

    with jax.named_scope("place"):
        placed = pl.pallas_call(
            lambda *refs: place_kernel(pool, *refs),
            out_shape=shape((slots * chunks, LANES), BF16),
            in_specs=[HBM] * 2, out_specs=VMEM, compiler_params=params(8),
            scratch_shapes=[vmem((1, rows), I32), vmem((rows, depth), BF16), dma((2,))],
        )(*far(tenant_row, hidden))
    with jax.named_scope("rows_to_owners"):
        got = lax.all_to_all(
            placed.reshape(peers, chunks, CAPACITY, LANES), "dp", split_axis=0, concat_axis=0, tiled=True
        ).reshape(slots * chunks, LANES)
    with jax.named_scope("early"):
        core_hidden = over_core(hidden)
        *first_state, pair = pl.pallas_call(
            lambda *refs: early_kernel(scale, early, *refs),
            out_shape=states(early) + [shape((2 * rows, depth), BF16)],
            in_specs=[ANY] + [HBM] * 6,
            out_specs=[VMEM] * 4,
            scratch_shapes=[pltpu.SMEM((rows,), I32), vmem((rows, GROUP * LANES), BF16)] + cache(early) + [dma((6,))],
            compiler_params=params(12),
            cost_estimate=cost(4 * early * GROUP * length * LANES, 4 * early * length * LANES),
        )(placed, *far(lengths, queries, key_cache, value_cache, hidden, core_hidden))
    with jax.named_scope("gather_hidden"):
        others = [over_y(pair, k) for k in (1, 2, 3)]
    with jax.named_scope("down"):
        partial, ids, up_near = pl.pallas_call(
            down_kernel,
            out_shape=[
                shape((slots // 2, LANES), F32), shape((slots, LANES), F32), shape((pool * rank, LANES), BF16)
            ],
            in_specs=[VMEM] * 2 + [HBM, ANY], out_specs=[VMEM] * 3, compiler_params=params(16),
            scratch_shapes=[dma],
        )(got, jnp.swapaxes(down, 1, 2).reshape(pool * rank, depth), *far(up.reshape(pool * rank, LANES)), first_state[0])
    with jax.named_scope("reduce"):
        pair_sum = partial + over_core(partial)
        sums_y = [over_y(pair_sum, k) for k in (1, 2, 3)]
    with jax.named_scope("up"):
        served = pl.pallas_call(
            up_kernel, out_shape=shape((slots, LANES), BF16),
            in_specs=[VMEM] * 6, out_specs=VMEM, compiler_params=params(8),
        )(pair_sum, *sums_y, ids, up_near)
    with jax.named_scope("answers"):
        returned = lax.all_to_all(
            served.reshape(peers, CAPACITY, LANES), "dp", split_axis=0, concat_axis=0, tiled=True
        ).reshape(slots, LANES)
    with jax.named_scope("late"):
        inverse = ROPE_BASE ** (-(np.arange(HEAD_SIZE // 2, dtype=np.float32) * 2.0) / HEAD_SIZE)
        inverse = jnp.asarray(np.concatenate([inverse, inverse])[None, :], F32)
        block = vmem((rows, depth), BF16)
        value, key, mixed, share, back = pl.pallas_call(
            lambda *refs: late_kernel(scale, pool, *refs),
            out_shape=[
                shape((rows, LANES), F32), shape((rows, LANES), BF16),
                shape((GROUP * rows, LANES), F32), shape((GROUP * rows, LANES), F32),
                shape((rows, LANES), BF16),
            ],
            in_specs=[SMEM, ANY] + [HBM] * 13 + [VMEM] * 3, out_specs=[VMEM] * 5,
            scratch_shapes=[
                vmem((1, rows), I32), pltpu.SMEM((rows,), I32), vmem((1, rows), I32), vmem((1, LANES), F32),
                vmem((rows, GROUP * LANES), BF16),
            ] + cache(late) + [block] * 2 + [vmem((2 * rows, depth), BF16)] * 3 + [
                vmem((count * depth, 2 * LANES), BF16)
            ] + [vmem((GROUP * late, LANES), F32)] * 3 + [dma((12,)), dma((count,))],
            compiler_params=params(20),
            cost_estimate=cost(2 * rows * count * depth * 2 * LANES, weight.size * 2),
        )(me, served, *far(tenant_row, lengths, length_row, inverse, queries, key_cache, value_cache, hidden, core_hidden,
                          *others, weight), *first_state)
    with jax.named_scope("finish"):
        return tuple(pl.pallas_call(
            final_kernel,
            out_shape=[shape((rows, GROUP * LANES), BF16), shape((rows, 2 * LANES), BF16)],
            in_specs=[VMEM] * 6, out_specs=[VMEM] * 2, compiler_params=params(8),
        )(returned, back, value, key, mixed, share))


def solution(mesh):
    in_specs = (
        P("dp", "tensor"),
        P("dp", "tensor"),
        P("dp", None, "tensor"),
        P("dp", None, "tensor"),
        P("dp"),
        P("dp"),
        P(None, "tensor"),
        P("dp", "tensor", None),
        P("dp", None, "tensor"),
    )
    out_specs = (P("dp", "tensor"), P("dp", "tensor"))
    return jax.shard_map(
        on_device, mesh=mesh, in_specs=in_specs, out_specs=out_specs, check_vma=False
    )
```

time: 61.8 us -> 56.1 us (0.908)
  local copies, waits for them, and re-layouts: 9.69 us -> 1.33 us
  starting transfers between devices: 27.1 us -> 30.1 us
  Pallas kernels: 14.6 us -> 12.2 us
  waiting for transfers between devices: 9.2 us -> 11.4 us
    unnamed x27 -> x10, local copies, waits for them, and re-layouts: 9.06 us -> 1.33 us
    all_to_all x1, starting transfers between devices: 6.18 us -> 9.78 us  [on_device(): lax.all_to_all(served.reshape(peers, CAPACITY, LANES), 'dp', split_axis=0...]
    pallas_call x2, Pallas kernels: 11 us -> 7.78 us  [the longest x1 5.03 us: on_device(): pl.pallas_call(lambda *refs: late_kernel(scale, pool, *refs), out_shape=[...]
    all_to_all x1, waiting for transfers between devices: 2.72 us -> 0.01 us  [on_device(): lax.all_to_all(placed.reshape(peers, chunks, CAPACITY, LANES), 'dp', spli...]
    all_to_all x1, waiting for transfers between devices: 0.01 us -> 2.65 us  [on_device(): lax.all_to_all(served.reshape(peers, CAPACITY, LANES), 'dp', split_axis=0...]
    ppermute x2, waiting for transfers between devices: 1.17 us -> 2.62 us  [on_device(): lax.ppermute(x, 'tensor', [(i, i ^ 1) for i in range(count)])]
    ppermute x6, waiting for transfers between devices: 5.3 us -> 6.14 us  [on_device(): lax.ppermute(x, 'tensor', [(i, (i + 2 * k) % count) for i in range(count)])]
    pallas_call x1, Pallas kernels: 1.1 us -> 1.87 us  [on_device(): pl.pallas_call(lambda *refs: place_kernel(pool, *refs), out_shape=shape((...]
  transfers between devices with their start and end apart: 10 -> 10, of which waited for: 5 -> 6; matrix products, arithmetic and copies ran while one was open for 3% -> 0% of each run, Pallas kernels for 22% -> 17%
where the time goes in v2:
time: 56.1 us; the launch traced here: 55.9 us
  starting transfers between devices  30.1 us (54%)
  Pallas kernels  12.2 us (22%)
  waiting for transfers between devices  11.4 us (20%)
  local copies, waits for them, and re-layouts  1.33 us (2%)
  between operations  0.76 us (1%)
    all_to_all x1, starting transfers between devices, on_device(): lax.all_to_all(placed.reshape(peers, chunks, CAPACITY, LANES), 'dp', spli...  11.6 us
    all_to_all x1, starting transfers between devices, on_device(): lax.all_to_all(served.reshape(peers, CAPACITY, LANES), 'dp', split_axis=0...  9.78 us
    ppermute x6, starting transfers between devices, on_device(): lax.ppermute(x, 'tensor', [(i, (i + 2 * k) % count) for i in range(count)])  8.51 us
    ppermute x6, waiting for transfers between devices, on_device(): lax.ppermute(x, 'tensor', [(i, (i + 2 * k) % count) for i in range(count)])  6.14 us
    pallas_call x1, Pallas kernels, on_device(): pl.pallas_call(lambda *refs: late_kernel(scale, pool, *refs), out_shape=[...  5.03 us
    pallas_call x1, Pallas kernels, on_device(): pl.pallas_call(lambda *refs: early_kernel(scale, early, *refs), out_shape...  2.76 us
    all_to_all x1, waiting for transfers between devices, on_device(): lax.all_to_all(served.reshape(peers, CAPACITY, LANES), 'dp', split_axis=0...  2.65 us
    ppermute x2, waiting for transfers between devices, on_device(): lax.ppermute(x, 'tensor', [(i, i ^ 1) for i in range(count)])  2.62 us
  transfers between devices with their start and end apart: 10, of which 6 were waited for; matrix products, arithmetic and copies ran while one was open for 0% of the time, Pallas kernels for 17%

profile of v2, /device:TPU:2, one launch (start us, length us, event | category | flops | bytes accessed | tf_op | source)
XLA Modules:
  0.0 55.9 jit_solution(13839494196485661596)
XLA Ops:
  0.6 1.9 %place.1.refs_0_ = bf16[576,128]{1,0:T(8,128)(2,1)} custom-call(s32[1,32]{1,0:T(1,128)} %bitcast.16, bf16[32,1024]{1,0:T(8,128)(2,1)} %refs_9_.1), custom_call_target="tpu_custom_call" | custom-call | tf_op jit(solution)/shard_map/place/pallas_call | solution.py:294
  2.5 11.6 %all-to-all-start = ((bf16[32,9,2,128]{3,2,1,0:T(2,128)(2,1)}), bf16[32,9,2,128]{3,2,1,0:T(2,128)(2,1)S(1)}, u32[]{:S(2)}, u32[]{:S(2)}) async-start(bf16[32,9,2,128]{3,2,1,0:T(2,128)(2,1)} %bitcast.1), calls=%async_computation | async-start | bytes 294912 | tf_op jit(solution)/shard_map/rows_to_owners/all_to_all | solution.py:301
  14.1 0.0 copy-start
  14.2 0.1 collective-permute-start
  14.3 1.4 %collective-permute-done.refs_6_.refs_10_ = bf16[32,1024]{1,0:T(8,128)(2,1)S(1)} collective-permute-done((bf16[32,1024]{1,0:T(8,128)(2,1)}, bf16[32,1024]{1,0:T(8,128)(2,1)S(1)}, u32[]{:S(2)}, u32[]{:S(2)}) %collective-permute-start) | collective-permute-done | bytes 65568 | tf_op jit(solution)/shard_map/early/ppermute | solution.py:288
  15.7 0.0 copy-start.1
  15.7 0.6 %copy-done.1 = bf16[32,1024]{1,0:T(8,128)(2,1)} copy-done((bf16[32,1024]{1,0:T(8,128)(2,1)}, bf16[32,1024]{1,0:T(8,128)(2,1)S(1)}, u32[]{:S(2)}) %copy-start.1) | copy-done | bytes 65560
  16.3 2.8 %early.1 = (f32[128,128]{1,0:T(8,128)S(1)}, f32[128,128]{1,0:T(8,128)S(1)}, f32[128,128]{1,0:T(8,128)S(1)}, bf16[64,1024]{1,0:T(8,128)(2,1)S(1)}) custom-call(bf16[576,128]{1,0:T(8,128)(2,1)} %place.1.refs_0_, s32[32]{0:T(128)} %refs_3_.3, bf16[32,1024]{1,0:T(8,128)(2,1)} %refs_6_.1, bf16[32,384,128]{2,1,0:T(8,128)(2,1)} %refs_7_.1, ...), custom_call_target="tpu_custom_call" | custom-call | flops 25165824 | bytes 3145728 | tf_op jit(solution)/shard_map/early/pallas_call | solution.py:306
  19.1 1.7 %collective-permute-start.5 = (bf16[64,1024]{1,0:T(8,128)(2,1)S(1)}, bf16[64,1024]{1,0:T(8,128)(2,1)S(1)}, u32[]{:S(2)}, u32[]{:S(2)}) collective-permute-start(bf16[64,1024]{1,0:T(8,128)(2,1)S(1)} %get-tuple-element.18), channel_id=1, source_target_pairs={{0,2},{1,3},{2,4},{3,5},{4,6},{5,7},{6,0},{7,1},{8,10},{9,11},{10,... | collective-permute-start | bytes 393224 | tf_op jit(solution)/shard_map/gather_hidden/ppermute | solution.py:289
  20.8 2.9 %collective-permute-start.6 = (bf16[64,1024]{1,0:T(8,128)(2,1)S(1)}, bf16[64,1024]{1,0:T(8,128)(2,1)S(1)}, u32[]{:S(2)}, u32[]{:S(2)}) collective-permute-start(bf16[64,1024]{1,0:T(8,128)(2,1)S(1)} %get-tuple-element.18), channel_id=1, source_target_pairs={{0,4},{1,5},{2,6},{3,7},{4,0},{5,1},{6,2},{7,3},{8,12},{9,13},{10,... | collective-permute-start | bytes 393224 | tf_op jit(solution)/shard_map/gather_hidden/ppermute | solution.py:289
  23.6 1.3 %collective-permute-start.7 = (bf16[64,1024]{1,0:T(8,128)(2,1)S(1)}, bf16[64,1024]{1,0:T(8,128)(2,1)S(1)}, u32[]{:S(2)}, u32[]{:S(2)}) collective-permute-start(bf16[64,1024]{1,0:T(8,128)(2,1)S(1)} %get-tuple-element.18), channel_id=1, source_target_pairs={{0,6},{1,7},{2,0},{3,1},{4,2},{5,3},{6,4},{7,5},{8,14},{9,15},{10,... | collective-permute-start | bytes 393224 | tf_op jit(solution)/shard_map/gather_hidden/ppermute | solution.py:289
  25.0 0.0 all-to-all-done
  25.0 0.0 copy-done
  25.0 1.0 %down.1 = (f32[32,128]{1,0:T(8,128)S(1)}, f32[64,128]{1,0:T(8,128)S(1)}, bf16[1024,128]{1,0:T(8,128)(2,1)S(1)}) custom-call(bf16[576,128]{1,0:T(8,128)(2,1)S(1)} %bitcast.12, bf16[1024,1024]{1,0:T(8,128)(2,1)S(1)} %bitcast.11, bf16[1024,128]{1,0:T(8,128)(2,1)} %bitcast.14, f32[128,128]{1,0:T(8,128)S(1)} %get-tuple-element.14.after_ref.refs_15_), custom_call_target="tpu_custom_call" | custom-call | tf_op jit(solution)/shard_map/down/pallas_call | solution.py:318
  26.0 0.1 collective-permute-start.1
  26.1 1.2 %collective-permute-done.1 = f32[32,128]{1,0:T(8,128)S(1)} collective-permute-done((f32[32,128]{1,0:T(8,128)S(1)}, f32[32,128]{1,0:T(8,128)S(1)}, u32[]{:S(2)}, u32[]{:S(2)}) %collective-permute-start.1) | collective-permute-done | bytes 16416 | tf_op jit(solution)/shard_map/reduce/ppermute | solution.py:288
  27.2 0.7 %collective-permute-start.2 = (f32[32,128]{1,0:T(8,128)S(1)}, f32[32,128]{1,0:T(8,128)S(1)}, u32[]{:S(2)}, u32[]{:S(2)}) collective-permute-start(f32[32,128]{1,0:T(8,128)S(1)} %add.3.a_ref), channel_id=1, source_target_pairs={{0,2},{1,3},{2,4},{3,5},{4,6},{5,7},{6,0},{7,1},{8,10},{9,11},{10,... | collective-permute-start | bytes 49160 | tf_op jit(solution)/shard_map/reduce/ppermute | solution.py:289
  27.9 1.9 %collective-permute-start.3 = (f32[32,128]{1,0:T(8,128)S(1)}, f32[32,128]{1,0:T(8,128)S(1)}, u32[]{:S(2)}, u32[]{:S(2)}) collective-permute-start(f32[32,128]{1,0:T(8,128)S(1)} %add.3.a_ref), channel_id=1, source_target_pairs={{0,4},{1,5},{2,6},{3,7},{4,0},{5,1},{6,2},{7,3},{8,12},{9,13},{10,... | collective-permute-start | bytes 49160 | tf_op jit(solution)/shard_map/reduce/ppermute | solution.py:289
  29.9 2.4 %collective-permute-done.2.b_ref = f32[32,128]{1,0:T(8,128)S(1)} collective-permute-done((f32[32,128]{1,0:T(8,128)S(1)}, f32[32,128]{1,0:T(8,128)S(1)}, u32[]{:S(2)}, u32[]{:S(2)}) %collective-permute-start.2) | collective-permute-done | bytes 16416 | tf_op jit(solution)/shard_map/reduce/ppermute | solution.py:289
  32.3 0.0 collective-permute-start.4
  32.3 0.9 %collective-permute-done.3.c_ref = f32[32,128]{1,0:T(8,128)S(1)} collective-permute-done((f32[32,128]{1,0:T(8,128)S(1)}, f32[32,128]{1,0:T(8,128)S(1)}, u32[]{:S(2)}, u32[]{:S(2)}) %collective-permute-start.3) | collective-permute-done | bytes 16416 | tf_op jit(solution)/shard_map/reduce/ppermute | solution.py:289
  33.2 2.8 %collective-permute-done.4.d_ref = f32[32,128]{1,0:T(8,128)S(1)} collective-permute-done((f32[32,128]{1,0:T(8,128)S(1)}, f32[32,128]{1,0:T(8,128)S(1)}, u32[]{:S(2)}, u32[]{:S(2)}) %collective-permute-start.4) | collective-permute-done | bytes 16416 | tf_op jit(solution)/shard_map/reduce/ppermute | solution.py:289
  36.0 0.8 %up.1.refs_1_ = bf16[64,128]{1,0:T(8,128)(2,1)} custom-call(f32[32,128]{1,0:T(8,128)S(1)} %add.3.a_ref, f32[32,128]{1,0:T(8,128)S(1)} %collective-permute-done.2.b_ref, f32[32,128]{1,0:T(8,128)S(1)} %collective-permute-done.3.c_ref, f32[32,128]{1,0:T(8,128)S(1)} %collective-permute-done.4.d_ref, f32[64,128]{1,0:T(8,128)S(1)} %get-tuple-element.16.ids_ref, ...), custom_call_target="tpu_custom_call" | custom-call | tf_op jit(solution)/shard_map/up/pallas_call | solution.py:330
  36.8 9.8 %all-to-all-start.1 = ((bf16[32,2,128]{2,1,0:T(2,128)(2,1)}), bf16[32,2,128]{2,1,0:T(2,128)(2,1)S(1)}, u32[]{:S(2)}, u32[]{:S(2)}) async-start(bf16[32,2,128]{2,1,0:T(2,128)(2,1)} %bitcast.6), calls=%async_computation.1 | async-start | bytes 32768 | tf_op jit(solution)/shard_map/answers/all_to_all | solution.py:335
  46.6 0.0 collective-permute-done.5.refs_11_
  46.6 0.0 copy-start.2
  46.7 0.0 collective-permute-done.6.refs_12_
  46.7 0.0 copy-start.3
  46.7 0.0 collective-permute-done.7.refs_13_
  46.7 0.0 copy-start.4
  46.7 0.6 %copy-done.2 = bf16[64,1024]{1,0:T(8,128)(2,1)} copy-done((bf16[64,1024]{1,0:T(8,128)(2,1)}, bf16[64,1024]{1,0:T(8,128)(2,1)S(1)}, u32[]{:S(2)}) %copy-start.2) | copy-done | bytes 131096
  47.3 0.0 copy-done.3
  47.3 0.1 copy-done.4
  47.4 5.0 %late.1 = (f32[32,128]{1,0:T(8,128)S(1)}, bf16[32,128]{1,0:T(8,128)(2,1)S(1)}, f32[256,128]{1,0:T(8,128)S(1)}, f32[256,128]{1,0:T(8,128)S(1)}, bf16[32,128]{1,0:T(8,128)(2,1)S(1)}) custom-call(s32[1]{0:T(128)} %bitcast.8.refs_0_, bf16[64,128]{1,0:T(8,128)(2,1)} %up.1.refs_1_, s32[1,32]{1,0:T(1,128)} %bitcast.17, s32[32]{0:T(128)} %refs_3_.3, ...), custom_call_target="tpu_custom_call" | custom-call | flops 134217728 | bytes 4194304 | tf_op jit(solution)/shard_map/late/pallas_call | solution.py:342
  52.4 2.7 %all-to-all-done.1 = bf16[32,2,128]{2,1,0:T(2,128)(2,1)S(1)} async-done(((bf16[32,2,128]{2,1,0:T(2,128)(2,1)}), bf16[32,2,128]{2,1,0:T(2,128)(2,1)S(1)}, u32[]{:S(2)}, u32[]{:S(2)}) %all-to-all-start.1) | async-done | bytes 16416 | tf_op jit(solution)/shard_map/answers/all_to_all | solution.py:335
  55.1 0.8 %finish.1 = (bf16[32,1024]{1,0:T(8,128)(2,1)}, bf16[32,256]{1,0:T(8,128)(2,1)}) custom-call(bf16[64,128]{1,0:T(8,128)(2,1)S(1)} %bitcast.13, bf16[32,128]{1,0:T(8,128)(2,1)S(1)} %get-tuple-element.21.back_ref, f32[32,128]{1,0:T(8,128)S(1)} %get-tuple-element.22.value_ref, bf16[32,128]{1,0:T(8,128)(2,1)S(1)} %get-tuple-element.23.key_ref, ...), custom_call_target="tpu_custom_call" | custom-call | tf_op jit(solution)/shard_map/finish/pallas_call | solution.py:361
  (1 shorter events, 0.0 us)
Async XLA Ops:
  2.5 22.5 %all-to-all-start = ((bf16[32,9,2,128]{3,2,1,0:T(2,128)(2,1)}), bf16[32,9,2,128]{3,2,1,0:T(2,128)(2,1)S(1)}, u32[]{:S(2)}, u32[]{:S(2)}) async-start(bf16[32,9,2,128]{3,2,1,0:T(2,128)(2,1)} %bitcast.1), calls=%async_computation | async-start | bytes 294912 | tf_op jit(solution)/shard_map/rows_to_owners/all_to_all | solution.py:301
  14.1 10.9 %copy-start = (bf16[16,1024,64]{1,2,0:T(8,128)(2,1)S(1)}, bf16[16,1024,64]{1,2,0:T(8,128)(2,1)}, u32[]{:S(2)}) copy-start(bf16[16,1024,64]{1,2,0:T(8,128)(2,1)} %param.17) | copy-start | bytes 6291460
  14.2 1.6 %collective-permute-start = (bf16[32,1024]{1,0:T(8,128)(2,1)}, bf16[32,1024]{1,0:T(8,128)(2,1)S(1)}, u32[]{:S(2)}, u32[]{:S(2)}) collective-permute-start(bf16[32,1024]{1,0:T(8,128)(2,1)} %refs_9_.1), channel_id=1, source_target_pairs={{0,1},{1,0},{2,3},{3,2},{4,5},{5,4},{6,7},{7,6},{8,9},{9,8},{10,11... | collective-permute-start | bytes 196616 | tf_op jit(solution)/shard_map/early/ppermute | solution.py:288
  15.7 0.6 %copy-start.1 = (bf16[32,1024]{1,0:T(8,128)(2,1)}, bf16[32,1024]{1,0:T(8,128)(2,1)S(1)}, u32[]{:S(2)}) copy-start(bf16[32,1024]{1,0:T(8,128)(2,1)S(1)} %collective-permute-done.refs_6_.refs_10_) | copy-start | bytes 196612
  19.1 27.5 %collective-permute-start.5 = (bf16[64,1024]{1,0:T(8,128)(2,1)S(1)}, bf16[64,1024]{1,0:T(8,128)(2,1)S(1)}, u32[]{:S(2)}, u32[]{:S(2)}) collective-permute-start(bf16[64,1024]{1,0:T(8,128)(2,1)S(1)} %get-tuple-element.18), channel_id=1, source_target_pairs={{0,2},{1,3},{2,4},{3,5},{4,6},{5,7},{6,0},{7,1},{8,10},{9,11},{10,... | collective-permute-start | bytes 393224 | tf_op jit(solution)/shard_map/gather_hidden/ppermute | solution.py:289
  20.8 25.9 %collective-permute-start.6 = (bf16[64,1024]{1,0:T(8,128)(2,1)S(1)}, bf16[64,1024]{1,0:T(8,128)(2,1)S(1)}, u32[]{:S(2)}, u32[]{:S(2)}) collective-permute-start(bf16[64,1024]{1,0:T(8,128)(2,1)S(1)} %get-tuple-element.18), channel_id=1, source_target_pairs={{0,4},{1,5},{2,6},{3,7},{4,0},{5,1},{6,2},{7,3},{8,12},{9,13},{10,... | collective-permute-start | bytes 393224 | tf_op jit(solution)/shard_map/gather_hidden/ppermute | solution.py:289
  23.6 23.0 %collective-permute-start.7 = (bf16[64,1024]{1,0:T(8,128)(2,1)S(1)}, bf16[64,1024]{1,0:T(8,128)(2,1)S(1)}, u32[]{:S(2)}, u32[]{:S(2)}) collective-permute-start(bf16[64,1024]{1,0:T(8,128)(2,1)S(1)} %get-tuple-element.18), channel_id=1, source_target_pairs={{0,6},{1,7},{2,0},{3,1},{4,2},{5,3},{6,4},{7,5},{8,14},{9,15},{10,... | collective-permute-start | bytes 393224 | tf_op jit(solution)/shard_map/gather_hidden/ppermute | solution.py:289
  26.0 1.3 %collective-permute-start.1 = (f32[32,128]{1,0:T(8,128)S(1)}, f32[32,128]{1,0:T(8,128)S(1)}, u32[]{:S(2)}, u32[]{:S(2)}) collective-permute-start(f32[32,128]{1,0:T(8,128)S(1)} %get-tuple-element.15), channel_id=1, source_target_pairs={{0,1},{1,0},{2,3},{3,2},{4,5},{5,4},{6,7},{7,6},{8,9},{9,8},{10,11... | collective-permute-start | bytes 49160 | tf_op jit(solution)/shard_map/reduce/ppermute | solution.py:288
  27.2 5.0 %collective-permute-start.2 = (f32[32,128]{1,0:T(8,128)S(1)}, f32[32,128]{1,0:T(8,128)S(1)}, u32[]{:S(2)}, u32[]{:S(2)}) collective-permute-start(f32[32,128]{1,0:T(8,128)S(1)} %add.3.a_ref), channel_id=1, source_target_pairs={{0,2},{1,3},{2,4},{3,5},{4,6},{5,7},{6,0},{7,1},{8,10},{9,11},{10,... | collective-permute-start | bytes 49160 | tf_op jit(solution)/shard_map/reduce/ppermute | solution.py:289
  27.9 5.2 %collective-permute-start.3 = (f32[32,128]{1,0:T(8,128)S(1)}, f32[32,128]{1,0:T(8,128)S(1)}, u32[]{:S(2)}, u32[]{:S(2)}) collective-permute-start(f32[32,128]{1,0:T(8,128)S(1)} %add.3.a_ref), channel_id=1, source_target_pairs={{0,4},{1,5},{2,6},{3,7},{4,0},{5,1},{6,2},{7,3},{8,12},{9,13},{10,... | collective-permute-start | bytes 49160 | tf_op jit(solution)/shard_map/reduce/ppermute | solution.py:289
  32.3 3.7 %collective-permute-start.4 = (f32[32,128]{1,0:T(8,128)S(1)}, f32[32,128]{1,0:T(8,128)S(1)}, u32[]{:S(2)}, u32[]{:S(2)}) collective-permute-start(f32[32,128]{1,0:T(8,128)S(1)} %add.3.a_ref), channel_id=1, source_target_pairs={{0,6},{1,7},{2,0},{3,1},{4,2},{5,3},{6,4},{7,5},{8,14},{9,15},{10,... | collective-permute-start | bytes 49160 | tf_op jit(solution)/shard_map/reduce/ppermute | solution.py:289
  36.8 18.2 %all-to-all-start.1 = ((bf16[32,2,128]{2,1,0:T(2,128)(2,1)}), bf16[32,2,128]{2,1,0:T(2,128)(2,1)S(1)}, u32[]{:S(2)}, u32[]{:S(2)}) async-start(bf16[32,2,128]{2,1,0:T(2,128)(2,1)} %bitcast.6), calls=%async_computation.1 | async-start | bytes 32768 | tf_op jit(solution)/shard_map/answers/all_to_all | solution.py:335
  46.6 0.7 %copy-start.2 = (bf16[64,1024]{1,0:T(8,128)(2,1)}, bf16[64,1024]{1,0:T(8,128)(2,1)S(1)}, u32[]{:S(2)}) copy-start(bf16[64,1024]{1,0:T(8,128)(2,1)S(1)} %collective-permute-done.5.refs_11_) | copy-start | bytes 393220
  46.7 0.7 %copy-start.3 = (bf16[64,1024]{1,0:T(8,128)(2,1)}, bf16[64,1024]{1,0:T(8,128)(2,1)S(1)}, u32[]{:S(2)}) copy-start(bf16[64,1024]{1,0:T(8,128)(2,1)S(1)} %collective-permute-done.6.refs_12_) | copy-start | bytes 393220
  46.7 0.7 %copy-start.4 = (bf16[64,1024]{1,0:T(8,128)(2,1)}, bf16[64,1024]{1,0:T(8,128)(2,1)S(1)}, u32[]{:S(2)}) copy-start(bf16[64,1024]{1,0:T(8,128)(2,1)S(1)} %collective-permute-done.7.refs_13_) | copy-start | bytes 393220

commit v3 on v2

--- a/solution.py
+++ b/solution.py
@@ -56,7 +56,14 @@
     return owner_row * CAPACITY + rank
 
 
-def place_kernel(pool, tenant_hbm, hidden_hbm, out_ref, tenant_ref, hidden_ref, sems):
+def fetches(pairs, sems):
+    copies = [pltpu.make_async_copy(source, target, sems.at[i]) for i, (source, target) in enumerate(pairs)]
+    for copy in copies:
+        copy.start()
+    return copies
+
+
+def place_kernel(pool, tenant_hbm, hidden_hbm, out_ref, hidden_ref, tenant_ref, sems):
     fetch_hidden = pltpu.make_async_copy(hidden_hbm, hidden_ref, sems.at[0])
     fetch_tenant = pltpu.make_async_copy(tenant_hbm, tenant_ref, sems.at[1])
     fetch_tenant.start()
@@ -89,9 +96,14 @@
         out_ref[g * wide : (g + 1) * wide, :] = turned[:, g * LANES : (g + 1) * LANES]
 
 
-def down_kernel(got_ref, down_ref, up_hbm, after_ref, partial_ref, ids_ref, up_ref, sem):
-    fetch_up = pltpu.make_async_copy(up_hbm, up_ref, sem)
-    fetch_up.start()
+def down_kernel(got_ref, down_ref, up_hbm, after_ref, own_any, y1_any, y2_any, y3_any, partial_ref, ids_ref, up_ref,
+                quad_hbm, sems):
+    rows = own_any.shape[0]
+    copies = fetches(
+        [(up_hbm, up_ref)]
+        + [(block, quad_hbm.at[pl.ds(k * rows, rows)]) for k, block in enumerate((own_any, y1_any, y2_any, y3_any))],
+        sems,
+    )
     slots = ids_ref.shape[0]
     chunks = got_ref.shape[0] // slots
     groups, wide = slots // 16, 16 * chunks
@@ -118,10 +130,11 @@
     half = slots // 2
     partial_ref[...] = jnp.where(lane[:half] < 64, total[:half], total[half:])
     ids_ref[...] = ids
-    fetch_up.wait()
-
-
-def up_kernel(a_ref, b_ref, c_ref, d_ref, ids_ref, up_ref, out_ref):
+    for copy in copies:
+        copy.wait()
+
+
+def up_kernel(after_ref, a_ref, b_ref, c_ref, d_ref, ids_ref, up_ref, out_ref):
     total = (a_ref[...] + b_ref[...]) + (c_ref[...] + d_ref[...])
     turned = pltpu.roll(total, 64, 1)
     left = iota(total.shape, 1) < 64
@@ -163,94 +176,78 @@
         whole_ref[place, :] = whole[some]
 
 
-def fetches(pairs, sems):
-    copies = [pltpu.make_async_copy(source, target, sems.at[i]) for i, (source, target) in enumerate(pairs)]
-    for copy in copies:
-        copy.start()
-    return copies
-
-
-def early_kernel(scale, count, after_ref, length_hbm, query_hbm, key_hbm, value_hbm, own_hbm, core_hbm, sum_ref,
-                 top_ref, whole_ref, pair_ref, length_ref, query_ref, key_ref, value_ref, sems):
-    rows = query_ref.shape[0]
-    some = pl.ds(0, count)
+def cache_kernel(scale, first, after_ref, length_hbm, query_hbm, key_hbm, value_hbm, sum_ref, top_ref, whole_ref,
+                 length_ref, query_ref, key_ref, value_ref, sems):
+    rows, count = query_ref.shape[0], key_ref.shape[0]
+    some = pl.ds(first, count)
     copies = fetches(
         [
             (query_hbm, query_ref), (length_hbm, length_ref), (key_hbm.at[some], key_ref),
-            (value_hbm.at[some], value_ref), (own_hbm, pair_ref.at[pl.ds(0, rows)]),
-            (core_hbm, pair_ref.at[pl.ds(rows, rows)]),
+            (value_hbm.at[some], value_ref),
         ],
         sems,
     )
     copies[0].wait()
     copies[1].wait()
-    attend_cache(scale, 0, count, rows, lambda r: length_ref[r], query_ref, key_ref, value_ref, copies[2].wait,
+    attend_cache(scale, first, count, rows, lambda r: length_ref[r], query_ref, key_ref, value_ref, copies[2].wait,
                  copies[3].wait, sum_ref, top_ref, whole_ref)
-    copies[4].wait()
-    copies[5].wait()
-
-
-def late_kernel(scale, pool, index_ref, after_ref, tenant_hbm, length_hbm, row_hbm, inverse_hbm, query_hbm, key_hbm,
-                value_hbm, own_hbm, core_hbm, y1_hbm, y2_hbm, y3_hbm, weight_hbm, sum_ref, top_ref, whole_ref,
-                projected_ref, entry_ref, mixed_ref, share_ref, back_ref, tenant_ref, length_ref, row_ref, inverse_ref,
-                query_ref, key_ref, value_ref, own_ref, core_ref, y1_ref, y2_ref, y3_ref, weight_ref, sum2_ref, top2_ref,
-                whole2_ref, sems, weight_sems):
-    rows, depth = own_ref.shape
-    count = key_ref.shape[0]
-    first = rows - count
-    some = pl.ds(first, count)
+
+
+def late_kernel(scale, pool, index_ref, after_ref, tenant_hbm, row_hbm, inverse_hbm, query_hbm, near_hbm, far_hbm,
+                weight_hbm, *refs):
+    state_refs, refs = refs[:6], refs[6:]
+    (projected_ref, entry_ref, mixed_ref, share_ref, back_ref, tenant_ref, row_ref, inverse_ref, query_ref, near_ref,
+     far_ref, weight_ref, sems, weight_sems) = refs
+    rows, depth = query_ref.shape[0], near_ref.shape[1]
+    first = state_refs[0].shape[0] // GROUP
     me = index_ref[0]
     devices = weight_ref.shape[0] // depth
     copies = fetches(
         [
-            (query_hbm, query_ref), (length_hbm, length_ref), (key_hbm.at[some], key_ref),
-            (value_hbm.at[some], value_ref), (tenant_hbm, tenant_ref), (row_hbm, row_ref),
-            (inverse_hbm, inverse_ref), (own_hbm, own_ref), (core_hbm, core_ref), (y1_hbm, y1_ref), (y2_hbm, y2_ref),
-            (y3_hbm, y3_ref),
+            (near_hbm, near_ref), (far_hbm, far_ref), (query_hbm, query_ref), (tenant_hbm, tenant_ref),
+            (row_hbm, row_ref), (inverse_hbm, inverse_ref),
         ],
         sems,
     )
     blocks = [pl.ds(k * depth, depth) for k in range(devices)]
     weights = fetches([(weight_hbm.at[block], weight_ref.at[block]) for block in blocks], weight_sems)
-    copies[0].wait()
-    copies[1].wait()
-    attend_cache(scale, first, count, rows, lambda r: length_ref[r], query_ref, key_ref, value_ref, copies[2].wait,
-                 copies[3].wait, sum2_ref, top2_ref, whole2_ref)
-    for copy in copies[4:] + weights:
+    for copy in copies:
+        copy.wait()
+    slot_col = upright(slots_of(tenant_ref[...].astype(F32), pool))
+    lane = iota((rows, LANES), 1)
+    back_ref[...] = jnp.where(slot_col == lane.astype(F32), 1.0, 0.0).astype(BF16)
+    angle = upright(row_ref[...].astype(F32)) * inverse_ref[...]
+    sine, cosine = jnp.sin(angle), jnp.cos(angle)
+    for copy in weights:
         copy.wait()
 
     def part(block, other):
         start = pl.multiple_of(other * depth, depth)
         return dot(block, weight_ref[pl.ds(start, depth), :])
 
-    total = part(own_ref[...], me) + part(core_ref[...], me ^ 1)
-    for shift, ref in ((1, y1_ref), (2, y2_ref), (3, y3_ref)):
+    total = jnp.zeros((rows, 2 * LANES), F32)
+    for shift in range(devices // 2):
         other = (me + devices - 2 * shift) % devices
-        total += part(ref[:rows], other) + part(ref[rows:], other ^ 1)
+        block = slice(shift * rows, (shift + 1) * rows)
+        total += part(near_ref[block], other) + part(far_ref[block], other ^ 1)
     projected_ref[...] = total[:, LANES:]
-    angle = upright(row_ref[...].astype(F32)) * inverse_ref[...]
-    lane = iota((rows, LANES), 1)
-    sine = jnp.sin(angle)
     key = total[:, :LANES]
-    key = key * jnp.cos(angle) + pltpu.roll(key, 64, 1) * jnp.where(lane < 64, -sine, sine)
+    key = key * cosine + pltpu.roll(key, 64, 1) * jnp.where(lane < 64, -sine, sine)
     key = key.astype(BF16)
     entry_ref[...] = key
     key = key.astype(F32)
-    halves = ((0, first, sum_ref, top_ref, whole_ref), (first, count, sum2_ref, top2_ref, whole2_ref))
+    halves = ((0, first, state_refs[:3]), (first, rows - first, state_refs[3:]))
     for h in range(GROUP):
         query = query_ref[:, h * LANES : (h + 1) * LANES].astype(F32)
         own = jnp.sum(query * key, axis=1, keepdims=True) * scale
-        for start, many, sums, tops, wholes in halves:
-            if many:
-                here, place = slice(h * many, (h + 1) * many), slice(h * rows + start, h * rows + start + many)
-                mine, top = own[start : start + many], tops[here, :]
-                highest = jnp.maximum(top, mine)
-                old, new = jnp.exp(top - highest), jnp.exp(mine - highest)
-                under = 1.0 / (old * wholes[here, :] + new)
-                mixed_ref[place, :] = sums[here, :] * (old * under)
-                share_ref[place, :] = new * under
-    slot_col = upright(slots_of(tenant_ref[...].astype(F32), pool))
-    back_ref[...] = jnp.where(slot_col == lane.astype(F32), 1.0, 0.0).astype(BF16)
+        for start, many, (sums, tops, wholes) in halves:
+            here, place = slice(h * many, (h + 1) * many), slice(h * rows + start, h * rows + start + many)
+            mine, top = own[start : start + many], tops[here, :]
+            highest = jnp.maximum(top, mine)
+            old, new = jnp.exp(top - highest), jnp.exp(mine - highest)
+            under = 1.0 / (old * wholes[here, :] + new)
+            mixed_ref[place, :] = sums[here, :] * (old * under)
+            share_ref[place, :] = new * under
 
 
 def final_kernel(got_ref, back_ref, value_ref, key_ref, mixed_ref, share_ref, out_ref, entry_ref):
@@ -288,49 +285,57 @@
     over_core = lambda x: lax.ppermute(x, "tensor", [(i, i ^ 1) for i in range(count)])
     over_y = lambda x, k: lax.ppermute(x, "tensor", [(i, (i + 2 * k) % count) for i in range(count)])
     states = lambda n: [shape((GROUP * n, LANES), F32)] * 3
-    cache = lambda n: [vmem((n, length, LANES), BF16)] * 2
+
+    def attend(first, many, after):
+        return pl.pallas_call(
+            lambda *refs: cache_kernel(scale, first, *refs),
+            out_shape=states(many),
+            in_specs=[ANY] + [HBM] * 4,
+            out_specs=[VMEM] * 3,
+            scratch_shapes=[pltpu.SMEM((rows,), I32), vmem((rows, GROUP * LANES), BF16)]
+            + [vmem((many, length, LANES), BF16)] * 2 + [dma((4,))],
+            compiler_params=params(12),
+            cost_estimate=cost(4 * many * GROUP * length * LANES, 4 * many * length * LANES),
+        )(after, *far(lengths, queries, key_cache, value_cache))
 
     with jax.named_scope("place"):
-        placed = pl.pallas_call(
+        placed, handed = pl.pallas_call(
             lambda *refs: place_kernel(pool, *refs),
-            out_shape=shape((slots * chunks, LANES), BF16),
-            in_specs=[HBM] * 2, out_specs=VMEM, compiler_params=params(8),
-            scratch_shapes=[vmem((1, rows), I32), vmem((rows, depth), BF16), dma((2,))],
+            out_shape=[shape((slots * chunks, LANES), BF16), shape((rows, depth), BF16)],
+            in_specs=[HBM] * 2, out_specs=[VMEM] * 2, compiler_params=params(8),
+            scratch_shapes=[vmem((1, rows), I32), dma((2,))],
         )(*far(tenant_row, hidden))
     with jax.named_scope("rows_to_owners"):
         got = lax.all_to_all(
             placed.reshape(peers, chunks, CAPACITY, LANES), "dp", split_axis=0, concat_axis=0, tiled=True
         ).reshape(slots * chunks, LANES)
+    with jax.named_scope("gather_hidden"):
+        others = [over_y(handed, k) for k in (1, 2, 3)]
     with jax.named_scope("early"):
-        core_hidden = over_core(hidden)
-        *first_state, pair = pl.pallas_call(
-            lambda *refs: early_kernel(scale, early, *refs),
-            out_shape=states(early) + [shape((2 * rows, depth), BF16)],
-            in_specs=[ANY] + [HBM] * 6,
-            out_specs=[VMEM] * 4,
-            scratch_shapes=[pltpu.SMEM((rows,), I32), vmem((rows, GROUP * LANES), BF16)] + cache(early) + [dma((6,))],
-            compiler_params=params(12),
-            cost_estimate=cost(4 * early * GROUP * length * LANES, 4 * early * length * LANES),
-        )(placed, *far(lengths, queries, key_cache, value_cache, hidden, core_hidden))
-    with jax.named_scope("gather_hidden"):
-        others = [over_y(pair, k) for k in (1, 2, 3)]
+        first_state = attend(0, early, placed)
     with jax.named_scope("down"):
-        partial, ids, up_near = pl.pallas_call(
+        partial, ids, up_near, near = pl.pallas_call(
             down_kernel,
             out_shape=[
-                shape((slots // 2, LANES), F32), shape((slots, LANES), F32), shape((pool * rank, LANES), BF16)
+                shape((slots // 2, LANES), F32), shape((slots, LANES), F32), shape((pool * rank, LANES), BF16),
+                shape((4 * rows, depth), BF16),
             ],
-            in_specs=[VMEM] * 2 + [HBM, ANY], out_specs=[VMEM] * 3, compiler_params=params(16),
-            scratch_shapes=[dma],
-        )(got, jnp.swapaxes(down, 1, 2).reshape(pool * rank, depth), *far(up.reshape(pool * rank, LANES)), first_state[0])
+            in_specs=[VMEM] * 2 + [HBM] + [ANY] * 5, out_specs=[VMEM] * 3 + [ANY], compiler_params=params(16),
+            scratch_shapes=[dma((5,))],
+        )(got, jnp.swapaxes(down, 1, 2).reshape(pool * rank, depth), *far(up.reshape(pool * rank, LANES)),
+          first_state[0], handed, *others)
     with jax.named_scope("reduce"):
         pair_sum = partial + over_core(partial)
         sums_y = [over_y(pair_sum, k) for k in (1, 2, 3)]
+    with jax.named_scope("middle"):
+        second_state = attend(early, late, pair_sum)
+    with jax.named_scope("gather_core"):
+        other = over_core(near)
     with jax.named_scope("up"):
         served = pl.pallas_call(
             up_kernel, out_shape=shape((slots, LANES), BF16),
-            in_specs=[VMEM] * 6, out_specs=VMEM, compiler_params=params(8),
-        )(pair_sum, *sums_y, ids, up_near)
+            in_specs=[ANY] + [VMEM] * 6, out_specs=VMEM, compiler_params=params(8),
+        )(second_state[0], pair_sum, *sums_y, ids, up_near)
     with jax.named_scope("answers"):
         returned = lax.all_to_all(
             served.reshape(peers, CAPACITY, LANES), "dp", split_axis=0, concat_axis=0, tiled=True
@@ -338,7 +343,6 @@
     with jax.named_scope("late"):
         inverse = ROPE_BASE ** (-(np.arange(HEAD_SIZE // 2, dtype=np.float32) * 2.0) / HEAD_SIZE)
         inverse = jnp.asarray(np.concatenate([inverse, inverse])[None, :], F32)
-        block = vmem((rows, depth), BF16)
         value, key, mixed, share, back = pl.pallas_call(
             lambda *refs: late_kernel(scale, pool, *refs),
             out_shape=[
@@ -346,17 +350,16 @@
                 shape((GROUP * rows, LANES), F32), shape((GROUP * rows, LANES), F32),
                 shape((rows, LANES), BF16),
             ],
-            in_specs=[SMEM, ANY] + [HBM] * 13 + [VMEM] * 3, out_specs=[VMEM] * 5,
+            in_specs=[SMEM, ANY] + [HBM] * 4 + [ANY] * 2 + [HBM] + [VMEM] * 6, out_specs=[VMEM] * 5,
             scratch_shapes=[
-                vmem((1, rows), I32), pltpu.SMEM((rows,), I32), vmem((1, rows), I32), vmem((1, LANES), F32),
-                vmem((rows, GROUP * LANES), BF16),
-            ] + cache(late) + [block] * 2 + [vmem((2 * rows, depth), BF16)] * 3 + [
-                vmem((count * depth, 2 * LANES), BF16)
-            ] + [vmem((GROUP * late, LANES), F32)] * 3 + [dma((12,)), dma((count,))],
-            compiler_params=params(20),
+                vmem((1, rows), I32), vmem((1, rows), I32), vmem((1, LANES), F32),
+                vmem((rows, GROUP * LANES), BF16), vmem((4 * rows, depth), BF16), vmem((4 * rows, depth), BF16),
+                vmem((count * depth, 2 * LANES), BF16), dma((6,)), dma((count,)),
+            ],
+            compiler_params=params(12),
             cost_estimate=cost(2 * rows * count * depth * 2 * LANES, weight.size * 2),
-        )(me, served, *far(tenant_row, lengths, length_row, inverse, queries, key_cache, value_cache, hidden, core_hidden,
-                          *others, weight), *first_state)
+        )(me, served, *far(tenant_row, length_row, inverse, queries), near, other, *far(weight), *first_state,
+          *second_state)
     with jax.named_scope("finish"):
         return tuple(pl.pallas_call(
             final_kernel,

time: 56.1 us -> 54.2 us (0.966)
  waiting for transfers between devices: 11.4 us -> 6.43 us
  starting transfers between devices: 30.1 us -> 32.7 us
  Pallas kernels: 12.2 us -> 13.7 us
  local copies, waits for them, and re-layouts: 1.33 us -> 0.01 us
    ppermute x6, waiting for transfers between devices: 6.14 us -> 0.17 us  [on_device(): lax.ppermute(x, 'tensor', [(i, (i + 2 * k) % count) for i in range(count)])]
    ppermute x6, starting transfers between devices: 8.51 us -> 11.7 us  [on_device(): lax.ppermute(x, 'tensor', [(i, (i + 2 * k) % count) for i in range(count)])]
    pallas_call x2 -> x3, Pallas kernels: 4.63 us -> 7.36 us  [the longest x2 5.47 us: attend(): pl.pallas_call(lambda *refs: cache_kernel(scale, first, *refs), out_shape...]
    all_to_all x1, waiting for transfers between devices: 2.65 us -> 5.03 us  [on_device(): lax.all_to_all(served.reshape(peers, CAPACITY, LANES), 'dp', split_axis=0...]
    pallas_call x1, Pallas kernels: 5.03 us -> 3.39 us  [on_device(): pl.pallas_call(lambda *refs: late_kernel(scale, pool, *refs), out_shape=[...]
    ppermute x2, waiting for transfers between devices: 2.62 us -> 1.05 us  [on_device(): lax.ppermute(x, 'tensor', [(i, i ^ 1) for i in range(count)])]
    unnamed x10 -> x2, local copies, waits for them, and re-layouts: 1.33 us -> 0.01 us
    all_to_all x1, starting transfers between devices: 9.78 us -> 8.77 us  [on_device(): lax.all_to_all(served.reshape(peers, CAPACITY, LANES), 'dp', split_axis=0...]
  transfers between devices with their start and end apart: 10 -> 10, of which waited for: 6 -> 4; matrix products, arithmetic and copies ran while one was open for 0% -> 0% of each run, Pallas kernels for 17% -> 18%
where the time goes in v3:
time: 54.2 us; the launch traced here: 53.6 us
  starting transfers between devices  32.7 us (60%)
  Pallas kernels  13.7 us (25%)
  waiting for transfers between devices  6.43 us (12%)
  between operations  0.76 us (1%)
    ppermute x6, starting transfers between devices, on_device(): lax.ppermute(x, 'tensor', [(i, (i + 2 * k) % count) for i in range(count)])  11.7 us
    all_to_all x1, starting transfers between devices, on_device(): lax.all_to_all(placed.reshape(peers, chunks, CAPACITY, LANES), 'dp', spli...  11.6 us
    all_to_all x1, starting transfers between devices, on_device(): lax.all_to_all(served.reshape(peers, CAPACITY, LANES), 'dp', split_axis=0...  8.77 us
    pallas_call x2, Pallas kernels, attend(): pl.pallas_call(lambda *refs: cache_kernel(scale, first, *refs), out_shape...  5.47 us
    all_to_all x1, waiting for transfers between devices, on_device(): lax.all_to_all(served.reshape(peers, CAPACITY, LANES), 'dp', split_axis=0...  5.03 us
    pallas_call x1, Pallas kernels, on_device(): pl.pallas_call(lambda *refs: late_kernel(scale, pool, *refs), out_shape=[...  3.39 us
    pallas_call x1, Pallas kernels, on_device(): pl.pallas_call(lambda *refs: place_kernel(pool, *refs), out_shape=[shape(...  1.89 us
    pallas_call x1, Pallas kernels, on_device(): pl.pallas_call(down_kernel, out_shape=[shape((slots // 2, LANES), F32), s...  1.29 us
  transfers between devices with their start and end apart: 10, of which 4 were waited for; matrix products, arithmetic and copies ran while one was open for 0% of the time, Pallas kernels for 18%

profile of v3, /device:TPU:2, one launch (start us, length us, event | category | flops | bytes accessed | tf_op | source)
XLA Modules:
  0.0 53.6 jit_solution(1267159918167569681)
XLA Ops:
  0.6 1.9 %place.1 = (bf16[576,128]{1,0:T(8,128)(2,1)}, bf16[32,1024]{1,0:T(8,128)(2,1)S(1)}) custom-call(s32[1,32]{1,0:T(1,128)} %bitcast.16, bf16[32,1024]{1,0:T(8,128)(2,1)} %refs_1_.3), custom_call_target="tpu_custom_call" | custom-call | tf_op jit(solution)/shard_map/place/pallas_call | solution.py:302
  2.5 11.6 %all-to-all-start = ((bf16[32,9,2,128]{3,2,1,0:T(2,128)(2,1)}), bf16[32,9,2,128]{3,2,1,0:T(2,128)(2,1)S(1)}, u32[]{:S(2)}, u32[]{:S(2)}) async-start(bf16[32,9,2,128]{3,2,1,0:T(2,128)(2,1)} %bitcast.1), calls=%async_computation | async-start | bytes 294912 | tf_op jit(solution)/shard_map/rows_to_owners/all_to_all | solution.py:309
  14.2 0.0 copy-start
  14.2 1.7 %collective-permute-start = (bf16[32,1024]{1,0:T(8,128)(2,1)S(1)}, bf16[32,1024]{1,0:T(8,128)(2,1)S(1)}, u32[]{:S(2)}, u32[]{:S(2)}) collective-permute-start(bf16[32,1024]{1,0:T(8,128)(2,1)S(1)} %get-tuple-element.21.own_any), channel_id=1, source_target_pairs={{0,2},{1,3},{2,4},{3,5},{4,6},{5,7},{6,0},{7,1},{8,10},{9,11},{10,... | collective-permute-start | bytes 196616 | tf_op jit(solution)/shard_map/gather_hidden/ppermute | solution.py:286
  15.8 2.9 %collective-permute-start.1 = (bf16[32,1024]{1,0:T(8,128)(2,1)S(1)}, bf16[32,1024]{1,0:T(8,128)(2,1)S(1)}, u32[]{:S(2)}, u32[]{:S(2)}) collective-permute-start(bf16[32,1024]{1,0:T(8,128)(2,1)S(1)} %get-tuple-element.21.own_any), channel_id=1, source_target_pairs={{0,4},{1,5},{2,6},{3,7},{4,0},{5,1},{6,2},{7,3},{8,12},{9,13},{10,... | collective-permute-start | bytes 196616 | tf_op jit(solution)/shard_map/gather_hidden/ppermute | solution.py:286
  18.7 1.3 %collective-permute-start.2 = (bf16[32,1024]{1,0:T(8,128)(2,1)S(1)}, bf16[32,1024]{1,0:T(8,128)(2,1)S(1)}, u32[]{:S(2)}, u32[]{:S(2)}) collective-permute-start(bf16[32,1024]{1,0:T(8,128)(2,1)S(1)} %get-tuple-element.21.own_any), channel_id=1, source_target_pairs={{0,6},{1,7},{2,0},{3,1},{4,2},{5,3},{6,4},{7,5},{8,14},{9,15},{10,... | collective-permute-start | bytes 196616 | tf_op jit(solution)/shard_map/gather_hidden/ppermute | solution.py:286
  20.1 2.7 %early.1 = (f32[128,128]{1,0:T(8,128)S(1)}, f32[128,128]{1,0:T(8,128)S(1)}, f32[128,128]{1,0:T(8,128)S(1)}) custom-call(bf16[576,128]{1,0:T(8,128)(2,1)} %get-tuple-element.19.refs_0_, s32[32]{0:T(128)} %refs_1_.5, bf16[32,1024]{1,0:T(8,128)(2,1)} %refs_5_.1, bf16[32,384,128]{2,1,0:T(8,128)(2,1)} %refs_3_.3, bf16[32,384,128]{2,1,0:T(8,128)(2,1)} %refs_4_.4), custom_call_target="tpu_custom_call" | custom-call | flops 25165824 | bytes 3145728 | tf_op jit(solution)/shard_map/early/pallas_call | solution.py:290
  22.8 0.0 collective-permute-done.y1_any
  22.8 0.0 collective-permute-done.1.y2_any
  22.8 0.2 collective-permute-done.2.y3_any
  23.0 0.2 all-to-all-done
  23.2 0.0 copy-done
  23.2 1.3 %down.1 = (f32[32,128]{1,0:T(8,128)S(1)}, f32[64,128]{1,0:T(8,128)S(1)}, bf16[1024,128]{1,0:T(8,128)(2,1)S(1)}, bf16[128,1024]{1,0:T(8,128)(2,1)S(1)}) custom-call(bf16[576,128]{1,0:T(8,128)(2,1)S(1)} %bitcast.12, bf16[1024,1024]{1,0:T(8,128)(2,1)S(1)} %bitcast.11, bf16[1024,128]{1,0:T(8,128)(2,1)} %bitcast.14, ...), custom_call_target="tpu_custom_call" | custom-call | tf_op jit(solution)/shard_map/down/pallas_call | solution.py:317
  24.5 0.1 collective-permute-start.7
  24.6 0.5 collective-permute-start.3
  25.1 1.0 %collective-permute-done.3 = f32[32,128]{1,0:T(8,128)S(1)} collective-permute-done((f32[32,128]{1,0:T(8,128)S(1)}, f32[32,128]{1,0:T(8,128)S(1)}, u32[]{:S(2)}, u32[]{:S(2)}) %collective-permute-start.3) | collective-permute-done | bytes 16416 | tf_op jit(solution)/shard_map/reduce/ppermute | solution.py:285
  26.1 1.6 %collective-permute-start.4 = (f32[32,128]{1,0:T(8,128)S(1)}, f32[32,128]{1,0:T(8,128)S(1)}, u32[]{:S(2)}, u32[]{:S(2)}) collective-permute-start(f32[32,128]{1,0:T(8,128)S(1)} %add.3.refs_0_.a_ref), channel_id=1, source_target_pairs={{0,2},{1,3},{2,4},{3,5},{4,6},{5,7},{6,0},{7,1},{8,10},{9,11},{10,... | collective-permute-start | bytes 49160 | tf_op jit(solution)/shard_map/reduce/ppermute | solution.py:286
  27.7 2.9 %collective-permute-start.5 = (f32[32,128]{1,0:T(8,128)S(1)}, f32[32,128]{1,0:T(8,128)S(1)}, u32[]{:S(2)}, u32[]{:S(2)}) collective-permute-start(f32[32,128]{1,0:T(8,128)S(1)} %add.3.refs_0_.a_ref), channel_id=1, source_target_pairs={{0,4},{1,5},{2,6},{3,7},{4,0},{5,1},{6,2},{7,3},{8,12},{9,13},{10,... | collective-permute-start | bytes 49160 | tf_op jit(solution)/shard_map/reduce/ppermute | solution.py:286
  30.6 1.3 %collective-permute-start.6 = (f32[32,128]{1,0:T(8,128)S(1)}, f32[32,128]{1,0:T(8,128)S(1)}, u32[]{:S(2)}, u32[]{:S(2)}) collective-permute-start(f32[32,128]{1,0:T(8,128)S(1)} %add.3.refs_0_.a_ref), channel_id=1, source_target_pairs={{0,6},{1,7},{2,0},{3,1},{4,2},{5,3},{6,4},{7,5},{8,14},{9,15},{10,... | collective-permute-start | bytes 49160 | tf_op jit(solution)/shard_map/reduce/ppermute | solution.py:286
  31.9 2.7 %middle.1 = (f32[128,128]{1,0:T(8,128)S(1)}, f32[128,128]{1,0:T(8,128)S(1)}, f32[128,128]{1,0:T(8,128)S(1)}) custom-call(f32[32,128]{1,0:T(8,128)S(1)} %add.3.refs_0_.a_ref, s32[32]{0:T(128)} %refs_1_.5, bf16[32,1024]{1,0:T(8,128)(2,1)} %refs_5_.1, bf16[32,384,128]{2,1,0:T(8,128)(2,1)} %refs_3_.3, bf16[32,384,128]{2,1,0:T(8,128)(2,1)} %refs_4_.4), custom_call_target="tpu_custom_call" | custom-call | flops 25165824 | bytes 3145728 | tf_op jit(solution)/shard_map/middle/pallas_call | solution.py:290
  34.7 0.0 collective-permute-done.4.b_ref
  34.7 0.0 collective-permute-done.5.c_ref
  34.7 0.0 collective-permute-done.6.d_ref
  34.7 0.8 %up.1.refs_1_ = bf16[64,128]{1,0:T(8,128)(2,1)} custom-call(f32[128,128]{1,0:T(8,128)S(1)} %get-tuple-element.23.after_ref.refs_12_, f32[32,128]{1,0:T(8,128)S(1)} %add.3.refs_0_.a_ref, f32[32,128]{1,0:T(8,128)S(1)} %collective-permute-done.4.b_ref, f32[32,128]{1,0:T(8,128)S(1)} %collective-permute-done.5.c_ref, f32[32,128]{1,0:T(8,128)S(1)} %collective-permute-done.6.d_ref, ...), custom_call_target="tpu_custom_call" | custom-call | tf_op jit(solution)/shard_map/up/pallas_call | solution.py:335
  35.6 8.8 %all-to-all-start.1 = ((bf16[32,2,128]{2,1,0:T(2,128)(2,1)}), bf16[32,2,128]{2,1,0:T(2,128)(2,1)S(1)}, u32[]{:S(2)}, u32[]{:S(2)}) async-start(bf16[32,2,128]{2,1,0:T(2,128)(2,1)} %bitcast.6), calls=%async_computation.1 | async-start | bytes 32768 | tf_op jit(solution)/shard_map/answers/all_to_all | solution.py:340
  44.3 0.0 collective-permute-done.7.refs_7_
  44.4 3.4 %late.1 = (f32[32,128]{1,0:T(8,128)S(1)}, bf16[32,128]{1,0:T(8,128)(2,1)S(1)}, f32[256,128]{1,0:T(8,128)S(1)}, f32[256,128]{1,0:T(8,128)S(1)}, bf16[32,128]{1,0:T(8,128)(2,1)S(1)}) custom-call(s32[1]{0:T(128)} %bitcast.8.refs_0_, bf16[64,128]{1,0:T(8,128)(2,1)} %up.1.refs_1_, s32[1,32]{1,0:T(1,128)} %bitcast.17, s32[1,32]{1,0:T(1,128)} %bitcast.15, ...), custom_call_target="tpu_custom_call" | custom-call | flops 134217728 | bytes 4194304 | tf_op jit(solution)/shard_map/late/pallas_call | solution.py:346
  47.8 5.0 %all-to-all-done.1 = bf16[32,2,128]{2,1,0:T(2,128)(2,1)S(1)} async-done(((bf16[32,2,128]{2,1,0:T(2,128)(2,1)}), bf16[32,2,128]{2,1,0:T(2,128)(2,1)S(1)}, u32[]{:S(2)}, u32[]{:S(2)}) %all-to-all-start.1) | async-done | bytes 16416 | tf_op jit(solution)/shard_map/answers/all_to_all | solution.py:340
  52.8 0.8 %finish.1 = (bf16[32,1024]{1,0:T(8,128)(2,1)}, bf16[32,256]{1,0:T(8,128)(2,1)}) custom-call(bf16[64,128]{1,0:T(8,128)(2,1)S(1)} %bitcast.13, bf16[32,128]{1,0:T(8,128)(2,1)S(1)} %get-tuple-element.31.back_ref, f32[32,128]{1,0:T(8,128)S(1)} %get-tuple-element.32.value_ref, bf16[32,128]{1,0:T(8,128)(2,1)S(1)} %get-tuple-element.33.key_ref, ...), custom_call_target="tpu_custom_call" | custom-call | tf_op jit(solution)/shard_map/finish/pallas_call | solution.py:364
  (1 shorter events, 0.0 us)
Async XLA Ops:
  2.5 20.6 %all-to-all-start = ((bf16[32,9,2,128]{3,2,1,0:T(2,128)(2,1)}), bf16[32,9,2,128]{3,2,1,0:T(2,128)(2,1)S(1)}, u32[]{:S(2)}, u32[]{:S(2)}) async-start(bf16[32,9,2,128]{3,2,1,0:T(2,128)(2,1)} %bitcast.1), calls=%async_computation | async-start | bytes 294912 | tf_op jit(solution)/shard_map/rows_to_owners/all_to_all | solution.py:309
  14.2 9.0 %copy-start = (bf16[16,1024,64]{1,2,0:T(8,128)(2,1)S(1)}, bf16[16,1024,64]{1,2,0:T(8,128)(2,1)}, u32[]{:S(2)}) copy-start(bf16[16,1024,64]{1,2,0:T(8,128)(2,1)} %param.17) | copy-start | bytes 6291460
  14.2 8.6 %collective-permute-start = (bf16[32,1024]{1,0:T(8,128)(2,1)S(1)}, bf16[32,1024]{1,0:T(8,128)(2,1)S(1)}, u32[]{:S(2)}, u32[]{:S(2)}) collective-permute-start(bf16[32,1024]{1,0:T(8,128)(2,1)S(1)} %get-tuple-element.21.own_any), channel_id=1, source_target_pairs={{0,2},{1,3},{2,4},{3,5},{4,6},{5,7},{6,0},{7,1},{8,10},{9,11},{10,... | collective-permute-start | bytes 196616 | tf_op jit(solution)/shard_map/gather_hidden/ppermute | solution.py:286
  15.8 7.0 %collective-permute-start.1 = (bf16[32,1024]{1,0:T(8,128)(2,1)S(1)}, bf16[32,1024]{1,0:T(8,128)(2,1)S(1)}, u32[]{:S(2)}, u32[]{:S(2)}) collective-permute-start(bf16[32,1024]{1,0:T(8,128)(2,1)S(1)} %get-tuple-element.21.own_any), channel_id=1, source_target_pairs={{0,4},{1,5},{2,6},{3,7},{4,0},{5,1},{6,2},{7,3},{8,12},{9,13},{10,... | collective-permute-start | bytes 196616 | tf_op jit(solution)/shard_map/gather_hidden/ppermute | solution.py:286
  18.7 4.3 %collective-permute-start.2 = (bf16[32,1024]{1,0:T(8,128)(2,1)S(1)}, bf16[32,1024]{1,0:T(8,128)(2,1)S(1)}, u32[]{:S(2)}, u32[]{:S(2)}) collective-permute-start(bf16[32,1024]{1,0:T(8,128)(2,1)S(1)} %get-tuple-element.21.own_any), channel_id=1, source_target_pairs={{0,6},{1,7},{2,0},{3,1},{4,2},{5,3},{6,4},{7,5},{8,14},{9,15},{10,... | collective-permute-start | bytes 196616 | tf_op jit(solution)/shard_map/gather_hidden/ppermute | solution.py:286
  24.5 19.9 %collective-permute-start.7 = (bf16[128,1024]{1,0:T(8,128)(2,1)S(1)}, bf16[128,1024]{1,0:T(8,128)(2,1)S(1)}, u32[]{:S(2)}, u32[]{:S(2)}) collective-permute-start(bf16[128,1024]{1,0:T(8,128)(2,1)S(1)} %get-tuple-element.26.refs_6_), channel_id=1, source_target_pairs={{0,1},{1,0},{2,3},{3,2},{4,5},{5,4},{6,7},{7,6},{8,9},{9,8},{10,11... | collective-permute-start | bytes 786440 | tf_op jit(solution)/shard_map/gather_core/ppermute | solution.py:285
  24.6 1.5 %collective-permute-start.3 = (f32[32,128]{1,0:T(8,128)S(1)}, f32[32,128]{1,0:T(8,128)S(1)}, u32[]{:S(2)}, u32[]{:S(2)}) collective-permute-start(f32[32,128]{1,0:T(8,128)S(1)} %get-tuple-element.22), channel_id=1, source_target_pairs={{0,1},{1,0},{2,3},{3,2},{4,5},{5,4},{6,7},{7,6},{8,9},{9,8},{10,11... | collective-permute-start | bytes 49160 | tf_op jit(solution)/shard_map/reduce/ppermute | solution.py:285
  26.1 8.6 %collective-permute-start.4 = (f32[32,128]{1,0:T(8,128)S(1)}, f32[32,128]{1,0:T(8,128)S(1)}, u32[]{:S(2)}, u32[]{:S(2)}) collective-permute-start(f32[32,128]{1,0:T(8,128)S(1)} %add.3.refs_0_.a_ref), channel_id=1, source_target_pairs={{0,2},{1,3},{2,4},{3,5},{4,6},{5,7},{6,0},{7,1},{8,10},{9,11},{10,... | collective-permute-start | bytes 49160 | tf_op jit(solution)/shard_map/reduce/ppermute | solution.py:286
  27.7 7.0 %collective-permute-start.5 = (f32[32,128]{1,0:T(8,128)S(1)}, f32[32,128]{1,0:T(8,128)S(1)}, u32[]{:S(2)}, u32[]{:S(2)}) collective-permute-start(f32[32,128]{1,0:T(8,128)S(1)} %add.3.refs_0_.a_ref), channel_id=1, source_target_pairs={{0,4},{1,5},{2,6},{3,7},{4,0},{5,1},{6,2},{7,3},{8,12},{9,13},{10,... | collective-permute-start | bytes 49160 | tf_op jit(solution)/shard_map/reduce/ppermute | solution.py:286
  30.6 4.1 %collective-permute-start.6 = (f32[32,128]{1,0:T(8,128)S(1)}, f32[32,128]{1,0:T(8,128)S(1)}, u32[]{:S(2)}, u32[]{:S(2)}) collective-permute-start(f32[32,128]{1,0:T(8,128)S(1)} %add.3.refs_0_.a_ref), channel_id=1, source_target_pairs={{0,6},{1,7},{2,0},{3,1},{4,2},{5,3},{6,4},{7,5},{8,14},{9,15},{10,... | collective-permute-start | bytes 49160 | tf_op jit(solution)/shard_map/reduce/ppermute | solution.py:286
  35.6 17.2 %all-to-all-start.1 = ((bf16[32,2,128]{2,1,0:T(2,128)(2,1)}), bf16[32,2,128]{2,1,0:T(2,128)(2,1)S(1)}, u32[]{:S(2)}, u32[]{:S(2)}) async-start(bf16[32,2,128]{2,1,0:T(2,128)(2,1)} %bitcast.6), calls=%async_computation.1 | async-start | bytes 32768 | tf_op jit(solution)/shard_map/answers/all_to_all | solution.py:340

commit v4 on v3

--- a/solution.py
+++ b/solution.py
@@ -96,14 +96,9 @@
         out_ref[g * wide : (g + 1) * wide, :] = turned[:, g * LANES : (g + 1) * LANES]
 
 
-def down_kernel(got_ref, down_ref, up_hbm, after_ref, own_any, y1_any, y2_any, y3_any, partial_ref, ids_ref, up_ref,
-                quad_hbm, sems):
-    rows = own_any.shape[0]
-    copies = fetches(
-        [(up_hbm, up_ref)]
-        + [(block, quad_hbm.at[pl.ds(k * rows, rows)]) for k, block in enumerate((own_any, y1_any, y2_any, y3_any))],
-        sems,
-    )
+def down_kernel(got_ref, down_ref, up_hbm, after_ref, partial_ref, ids_ref, up_ref, sem):
+    fetch_up = pltpu.make_async_copy(up_hbm, up_ref, sem)
+    fetch_up.start()
     slots = ids_ref.shape[0]
     chunks = got_ref.shape[0] // slots
     groups, wide = slots // 16, 16 * chunks
@@ -130,8 +125,7 @@
     half = slots // 2
     partial_ref[...] = jnp.where(lane[:half] < 64, total[:half], total[half:])
     ids_ref[...] = ids
-    for copy in copies:
-        copy.wait()
+    fetch_up.wait()
 
 
 def up_kernel(after_ref, a_ref, b_ref, c_ref, d_ref, ids_ref, up_ref, out_ref):
@@ -176,10 +170,10 @@
         whole_ref[place, :] = whole[some]
 
 
-def cache_kernel(scale, first, after_ref, length_hbm, query_hbm, key_hbm, value_hbm, sum_ref, top_ref, whole_ref,
-                 length_ref, query_ref, key_ref, value_ref, sems):
+def early_kernel(scale, after_ref, length_hbm, query_hbm, key_hbm, value_hbm, sum_ref, top_ref, whole_ref, length_ref,
+                 query_ref, key_ref, value_ref, sems):
     rows, count = query_ref.shape[0], key_ref.shape[0]
-    some = pl.ds(first, count)
+    some = pl.ds(0, count)
     copies = fetches(
         [
             (query_hbm, query_ref), (length_hbm, length_ref), (key_hbm.at[some], key_ref),
@@ -189,37 +183,52 @@
     )
     copies[0].wait()
     copies[1].wait()
-    attend_cache(scale, first, count, rows, lambda r: length_ref[r], query_ref, key_ref, value_ref, copies[2].wait,
+    attend_cache(scale, 0, count, rows, lambda r: length_ref[r], query_ref, key_ref, value_ref, copies[2].wait,
                  copies[3].wait, sum_ref, top_ref, whole_ref)
 
 
-def late_kernel(scale, pool, index_ref, after_ref, tenant_hbm, row_hbm, inverse_hbm, query_hbm, near_hbm, far_hbm,
-                weight_hbm, *refs):
-    state_refs, refs = refs[:6], refs[6:]
-    (projected_ref, entry_ref, mixed_ref, share_ref, back_ref, tenant_ref, row_ref, inverse_ref, query_ref, near_ref,
-     far_ref, weight_ref, sems, weight_sems) = refs
+def middle_kernel(scale, pool, after_ref, length_hbm, query_hbm, key_hbm, value_hbm, tenant_hbm, row_hbm, inverse_hbm,
+                  weight_hbm, sum_ref, top_ref, whole_ref, weight_ref,
+                  query_ref, cosine_ref, sine_ref, back_ref, length_ref, key_ref, value_ref, tenant_ref, row_ref,
+                  inverse_ref, sems):
+    rows, count = query_ref.shape[0], key_ref.shape[0]
+    some = pl.ds(rows - count, count)
+    copies = fetches(
+        [
+            (query_hbm, query_ref), (length_hbm, length_ref), (tenant_hbm, tenant_ref), (row_hbm, row_ref),
+            (inverse_hbm, inverse_ref), (key_hbm.at[some], key_ref), (value_hbm.at[some], value_ref),
+            (weight_hbm, weight_ref),
+        ],
+        sems,
+    )
+    for copy in copies[:5]:
+        copy.wait()
+    lane = iota((rows, LANES), 1)
+    slot_col = upright(slots_of(tenant_ref[...].astype(F32), pool))
+    back_ref[...] = jnp.where(slot_col == lane.astype(F32), 1.0, 0.0).astype(BF16)
+    angle = upright(row_ref[...].astype(F32)) * inverse_ref[...]
+    sine = jnp.sin(angle)
+    cosine_ref[...] = jnp.cos(angle)
+    sine_ref[...] = jnp.where(lane < 64, -sine, sine)
+    attend_cache(scale, rows - count, count, rows, lambda r: length_ref[r], query_ref, key_ref, value_ref,
+                 copies[5].wait, copies[6].wait, sum_ref, top_ref, whole_ref)
+    for copy in copies[7:]:
+        copy.wait()
+
+
+def join_kernel(after_ref, own_any, y1_any, y2_any, y3_any, near_ref, sems):
+    rows = own_any.shape[0]
+    blocks = enumerate((own_any, y1_any, y2_any, y3_any))
+    for copy in fetches([(block, near_ref.at[pl.ds(k * rows, rows)]) for k, block in blocks], sems):
+        copy.wait()
+
+
+def late_kernel(scale, index_ref, near_ref, far_ref, weight_ref, query_ref, cosine_ref, sine_ref, *refs):
+    state_refs, (projected_ref, entry_ref, mixed_ref, share_ref) = refs[:6], refs[6:]
     rows, depth = query_ref.shape[0], near_ref.shape[1]
     first = state_refs[0].shape[0] // GROUP
     me = index_ref[0]
     devices = weight_ref.shape[0] // depth
-    copies = fetches(
-        [
-            (near_hbm, near_ref), (far_hbm, far_ref), (query_hbm, query_ref), (tenant_hbm, tenant_ref),
-            (row_hbm, row_ref), (inverse_hbm, inverse_ref),
-        ],
-        sems,
-    )
-    blocks = [pl.ds(k * depth, depth) for k in range(devices)]
-    weights = fetches([(weight_hbm.at[block], weight_ref.at[block]) for block in blocks], weight_sems)
-    for copy in copies:
-        copy.wait()
-    slot_col = upright(slots_of(tenant_ref[...].astype(F32), pool))
-    lane = iota((rows, LANES), 1)
-    back_ref[...] = jnp.where(slot_col == lane.astype(F32), 1.0, 0.0).astype(BF16)
-    angle = upright(row_ref[...].astype(F32)) * inverse_ref[...]
-    sine, cosine = jnp.sin(angle), jnp.cos(angle)
-    for copy in weights:
-        copy.wait()
 
     def part(block, other):
         start = pl.multiple_of(other * depth, depth)
@@ -232,8 +241,7 @@
         total += part(near_ref[block], other) + part(far_ref[block], other ^ 1)
     projected_ref[...] = total[:, LANES:]
     key = total[:, :LANES]
-    key = key * cosine + pltpu.roll(key, 64, 1) * jnp.where(lane < 64, -sine, sine)
-    key = key.astype(BF16)
+    key = (key * cosine_ref[...] + pltpu.roll(key, 64, 1) * sine_ref[...]).astype(BF16)
     entry_ref[...] = key
     key = key.astype(F32)
     halves = ((0, first, state_refs[:3]), (first, rows - first, state_refs[3:]))
@@ -272,8 +280,6 @@
     chunks = depth // LANES + 1
     length = key_cache.shape[1]
     scale = HEAD_SIZE ** -0.5
-    early = EARLY_ROWS
-    late = rows - early
     shape, vmem, dma = jax.ShapeDtypeStruct, pltpu.VMEM, pltpu.SemaphoreType.DMA
     params = lambda size: pltpu.CompilerParams(vmem_limit_bytes=size * MIB)
     far = lambda *arrays: [pltpu.with_memory_space_constraint(x, pltpu.HBM) for x in arrays]
@@ -284,19 +290,13 @@
     me = lax.axis_index("tensor").astype(I32).reshape(1)
     over_core = lambda x: lax.ppermute(x, "tensor", [(i, i ^ 1) for i in range(count)])
     over_y = lambda x, k: lax.ppermute(x, "tensor", [(i, (i + 2 * k) % count) for i in range(count)])
+
+    early = EARLY_ROWS
+    late = rows - early
     states = lambda n: [shape((GROUP * n, LANES), F32)] * 3
-
-    def attend(first, many, after):
-        return pl.pallas_call(
-            lambda *refs: cache_kernel(scale, first, *refs),
-            out_shape=states(many),
-            in_specs=[ANY] + [HBM] * 4,
-            out_specs=[VMEM] * 3,
-            scratch_shapes=[pltpu.SMEM((rows,), I32), vmem((rows, GROUP * LANES), BF16)]
-            + [vmem((many, length, LANES), BF16)] * 2 + [dma((4,))],
-            compiler_params=params(12),
-            cost_estimate=cost(4 * many * GROUP * length * LANES, 4 * many * length * LANES),
-        )(after, *far(lengths, queries, key_cache, value_cache))
+    effort = lambda n: cost(4 * n * GROUP * length * LANES, 4 * n * length * LANES)
+    inverse = ROPE_BASE ** (-(np.arange(HEAD_SIZE // 2, dtype=np.float32) * 2.0) / HEAD_SIZE)
+    inverse = jnp.asarray(np.concatenate([inverse, inverse])[None, :], F32)
 
     with jax.named_scope("place"):
         placed, handed = pl.pallas_call(
@@ -312,54 +312,62 @@
     with jax.named_scope("gather_hidden"):
         others = [over_y(handed, k) for k in (1, 2, 3)]
     with jax.named_scope("early"):
-        first_state = attend(0, early, placed)
+        first_state = pl.pallas_call(
+            lambda *refs: early_kernel(scale, *refs),
+            out_shape=states(early),
+            in_specs=[ANY] + [HBM] * 4, out_specs=[VMEM] * 3,
+            scratch_shapes=[pltpu.SMEM((rows,), I32), vmem((rows, GROUP * LANES), BF16)]
+            + [vmem((early, length, LANES), BF16)] * 2 + [dma((4,))],
+            compiler_params=params(12), cost_estimate=effort(early),
+        )(placed, *far(lengths, queries, key_cache, value_cache))
     with jax.named_scope("down"):
-        partial, ids, up_near, near = pl.pallas_call(
+        partial, ids, up_near = pl.pallas_call(
             down_kernel,
             out_shape=[
-                shape((slots // 2, LANES), F32), shape((slots, LANES), F32), shape((pool * rank, LANES), BF16),
-                shape((4 * rows, depth), BF16),
+                shape((slots // 2, LANES), F32), shape((slots, LANES), F32), shape((pool * rank, LANES), BF16)
             ],
-            in_specs=[VMEM] * 2 + [HBM] + [ANY] * 5, out_specs=[VMEM] * 3 + [ANY], compiler_params=params(16),
-            scratch_shapes=[dma((5,))],
+            in_specs=[VMEM] * 2 + [HBM, ANY], out_specs=[VMEM] * 3, compiler_params=params(16),
+            scratch_shapes=[dma],
         )(got, jnp.swapaxes(down, 1, 2).reshape(pool * rank, depth), *far(up.reshape(pool * rank, LANES)),
-          first_state[0], handed, *others)
+          first_state[0])
     with jax.named_scope("reduce"):
         pair_sum = partial + over_core(partial)
         sums_y = [over_y(pair_sum, k) for k in (1, 2, 3)]
-    with jax.named_scope("middle"):
-        second_state = attend(early, late, pair_sum)
+    with jax.named_scope("join"):
+        near = pl.pallas_call(
+            join_kernel, out_shape=shape((4 * rows, depth), BF16), in_specs=[ANY] * 5, out_specs=VMEM,
+            scratch_shapes=[dma((4,))], compiler_params=params(4),
+        )(pair_sum, handed, *others)
     with jax.named_scope("gather_core"):
         other = over_core(near)
     with jax.named_scope("up"):
         served = pl.pallas_call(
             up_kernel, out_shape=shape((slots, LANES), BF16),
             in_specs=[ANY] + [VMEM] * 6, out_specs=VMEM, compiler_params=params(8),
-        )(second_state[0], pair_sum, *sums_y, ids, up_near)
+        )(near, pair_sum, *sums_y, ids, up_near)
     with jax.named_scope("answers"):
         returned = lax.all_to_all(
             served.reshape(peers, CAPACITY, LANES), "dp", split_axis=0, concat_axis=0, tiled=True
         ).reshape(slots, LANES)
+    with jax.named_scope("middle"):
+        *second_state, weight_near, queries_near, cosine, sine, back = pl.pallas_call(
+            lambda *refs: middle_kernel(scale, pool, *refs),
+            out_shape=states(late) + [
+                shape(weight.shape, BF16), shape(queries.shape, BF16),
+                shape((rows, LANES), F32), shape((rows, LANES), F32), shape((rows, LANES), BF16),
+            ],
+            in_specs=[ANY] + [HBM] * 8, out_specs=[VMEM] * 8,
+            scratch_shapes=[pltpu.SMEM((rows,), I32)] + [vmem((late, length, LANES), BF16)] * 2
+            + [vmem((1, rows), I32), vmem((1, rows), I32), vmem((1, LANES), F32), dma((8,))],
+            compiler_params=params(12), cost_estimate=effort(late),
+        )(served, *far(lengths, queries, key_cache, value_cache, tenant_row, length_row, inverse, weight))
     with jax.named_scope("late"):
-        inverse = ROPE_BASE ** (-(np.arange(HEAD_SIZE // 2, dtype=np.float32) * 2.0) / HEAD_SIZE)
-        inverse = jnp.asarray(np.concatenate([inverse, inverse])[None, :], F32)
-        value, key, mixed, share, back = pl.pallas_call(
-            lambda *refs: late_kernel(scale, pool, *refs),
-            out_shape=[
-                shape((rows, LANES), F32), shape((rows, LANES), BF16),
-                shape((GROUP * rows, LANES), F32), shape((GROUP * rows, LANES), F32),
-                shape((rows, LANES), BF16),
-            ],
-            in_specs=[SMEM, ANY] + [HBM] * 4 + [ANY] * 2 + [HBM] + [VMEM] * 6, out_specs=[VMEM] * 5,
-            scratch_shapes=[
-                vmem((1, rows), I32), vmem((1, rows), I32), vmem((1, LANES), F32),
-                vmem((rows, GROUP * LANES), BF16), vmem((4 * rows, depth), BF16), vmem((4 * rows, depth), BF16),
-                vmem((count * depth, 2 * LANES), BF16), dma((6,)), dma((count,)),
-            ],
-            compiler_params=params(12),
+        value, key, mixed, share = pl.pallas_call(
+            lambda *refs: late_kernel(scale, *refs),
+            out_shape=[shape((rows, LANES), F32), shape((rows, LANES), BF16)] + [shape((GROUP * rows, LANES), F32)] * 2,
+            in_specs=[SMEM] + [VMEM] * 12, out_specs=[VMEM] * 4, compiler_params=params(8),
             cost_estimate=cost(2 * rows * count * depth * 2 * LANES, weight.size * 2),
-        )(me, served, *far(tenant_row, length_row, inverse, queries), near, other, *far(weight), *first_state,
-          *second_state)
+        )(me, near, other, weight_near, queries_near, cosine, sine, *first_state, *second_state)
     with jax.named_scope("finish"):
         return tuple(pl.pallas_call(
             final_kernel,

time: 54.2 us -> 53 us (0.978)
  the two profiles are of different devices: /device:TPU:2 before, /device:TPU:8 now
where the time goes in v4:
time: 53 us; the launch traced here: 52.8 us
  starting transfers between devices  28.7 us (54%)
  Pallas kernels  12 us (23%)
  waiting for transfers between devices  11.4 us (22%)
  between operations  0.75 us (1%)
    all_to_all x1, starting transfers between devices, on_device(): lax.all_to_all(placed.reshape(peers, chunks, CAPACITY, LANES), 'dp', spli...  11.3 us
    ppermute x6, starting transfers between devices, on_device(): lax.ppermute(x, 'tensor', [(i, (i + 2 * k) % count) for i in range(count)])  9.92 us
    all_to_all x1, starting transfers between devices, on_device(): lax.all_to_all(served.reshape(peers, CAPACITY, LANES), 'dp', split_axis=0...  7.09 us
    all_to_all x1, waiting for transfers between devices, on_device(): lax.all_to_all(served.reshape(peers, CAPACITY, LANES), 'dp', split_axis=0...  5.26 us
    pallas_call x1, Pallas kernels, on_device(): pl.pallas_call(lambda *refs: middle_kernel(scale, pool, *refs), out_shape...  3.31 us
    all_to_all x1, waiting for transfers between devices, on_device(): lax.all_to_all(placed.reshape(peers, chunks, CAPACITY, LANES), 'dp', spli...  3.03 us
    pallas_call x1, Pallas kernels, on_device(): pl.pallas_call(lambda *refs: early_kernel(scale, *refs), out_shape=states...  2.74 us
    ppermute x6, waiting for transfers between devices, on_device(): lax.ppermute(x, 'tensor', [(i, (i + 2 * k) % count) for i in range(count)])  1.9 us
  transfers between devices with their start and end apart: 10, of which 4 were waited for; matrix products, arithmetic and copies ran while one was open for 0% of the time, Pallas kernels for 17%

profile of v4, /device:TPU:8, one launch (start us, length us, event | category | flops | bytes accessed | tf_op | source)
XLA Modules:
  0.0 52.8 jit_solution(5304368546808593265)
XLA Ops:
  0.6 1.9 %place.1 = (bf16[576,128]{1,0:T(8,128)(2,1)}, bf16[32,1024]{1,0:T(8,128)(2,1)S(1)}) custom-call(s32[1,32]{1,0:T(1,128)} %bitcast.16, bf16[32,1024]{1,0:T(8,128)(2,1)} %refs_1_.3), custom_call_target="tpu_custom_call" | custom-call | tf_op jit(solution)/shard_map/place/pallas_call | solution.py:302
  2.5 11.3 %all-to-all-start = ((bf16[32,9,2,128]{3,2,1,0:T(2,128)(2,1)}), bf16[32,9,2,128]{3,2,1,0:T(2,128)(2,1)S(1)}, u32[]{:S(2)}, u32[]{:S(2)}) async-start(bf16[32,9,2,128]{3,2,1,0:T(2,128)(2,1)} %bitcast.1), calls=%async_computation | async-start | bytes 294912 | tf_op jit(solution)/shard_map/rows_to_owners/all_to_all | solution.py:309
  13.9 0.0 copy-start
  13.9 1.6 %collective-permute-start.1 = (bf16[32,1024]{1,0:T(8,128)(2,1)S(1)}, bf16[32,1024]{1,0:T(8,128)(2,1)S(1)}, u32[]{:S(2)}, u32[]{:S(2)}) collective-permute-start(bf16[32,1024]{1,0:T(8,128)(2,1)S(1)} %get-tuple-element.25.own_any), channel_id=1, source_target_pairs={{0,2},{1,3},{2,4},{3,5},{4,6},{5,7},{6,0},{7,1},{8,10},{9,11},{10,... | collective-permute-start | bytes 196616 | tf_op jit(solution)/shard_map/gather_hidden/ppermute | solution.py:292
  15.5 0.9 %collective-permute-start.2 = (bf16[32,1024]{1,0:T(8,128)(2,1)S(1)}, bf16[32,1024]{1,0:T(8,128)(2,1)S(1)}, u32[]{:S(2)}, u32[]{:S(2)}) collective-permute-start(bf16[32,1024]{1,0:T(8,128)(2,1)S(1)} %get-tuple-element.25.own_any), channel_id=1, source_target_pairs={{0,4},{1,5},{2,6},{3,7},{4,0},{5,1},{6,2},{7,3},{8,12},{9,13},{10,... | collective-permute-start | bytes 196616 | tf_op jit(solution)/shard_map/gather_hidden/ppermute | solution.py:292
  16.5 2.4 %collective-permute-start.3 = (bf16[32,1024]{1,0:T(8,128)(2,1)S(1)}, bf16[32,1024]{1,0:T(8,128)(2,1)S(1)}, u32[]{:S(2)}, u32[]{:S(2)}) collective-permute-start(bf16[32,1024]{1,0:T(8,128)(2,1)S(1)} %get-tuple-element.25.own_any), channel_id=1, source_target_pairs={{0,6},{1,7},{2,0},{3,1},{4,2},{5,3},{6,4},{7,5},{8,14},{9,15},{10,... | collective-permute-start | bytes 196616 | tf_op jit(solution)/shard_map/gather_hidden/ppermute | solution.py:292
  18.9 2.7 %early.1 = (f32[128,128]{1,0:T(8,128)S(1)}, f32[128,128]{1,0:T(8,128)S(1)}, f32[128,128]{1,0:T(8,128)S(1)}) custom-call(bf16[576,128]{1,0:T(8,128)(2,1)} %get-tuple-element.22.refs_0_, s32[32]{0:T(128)} %refs_1_.5, bf16[32,1024]{1,0:T(8,128)(2,1)} %refs_2_.3, bf16[32,384,128]{2,1,0:T(8,128)(2,1)} %refs_3_.3, bf16[32,384,128]{2,1,0:T(8,128)(2,1)} %refs_4_.3), custom_call_target="tpu_custom_call" | custom-call | flops 25165824 | bytes 3145728 | tf_op jit(solution)/shard_map/early/pallas_call | solution.py:315
  21.6 3.0 %all-to-all-done = bf16[32,9,2,128]{3,2,1,0:T(2,128)(2,1)S(1)} async-done(((bf16[32,9,2,128]{3,2,1,0:T(2,128)(2,1)}), bf16[32,9,2,128]{3,2,1,0:T(2,128)(2,1)S(1)}, u32[]{:S(2)}, u32[]{:S(2)}) %all-to-all-start) | async-done | bytes 147488 | tf_op jit(solution)/shard_map/rows_to_owners/all_to_all | solution.py:309
  24.6 0.0 copy-done
  24.6 1.0 %down.1 = (f32[32,128]{1,0:T(8,128)S(1)}, f32[64,128]{1,0:T(8,128)S(1)}, bf16[1024,128]{1,0:T(8,128)(2,1)S(1)}) custom-call(bf16[576,128]{1,0:T(8,128)(2,1)S(1)} %bitcast.12, bf16[1024,1024]{1,0:T(8,128)(2,1)S(1)} %bitcast.11, bf16[1024,128]{1,0:T(8,128)(2,1)} %bitcast.14, f32[128,128]{1,0:T(8,128)S(1)} %get-tuple-element.23.after_ref.refs_7_), custom_call_target="tpu_custom_call" | custom-call | tf_op jit(solution)/shard_map/down/pallas_call | solution.py:324
  25.6 0.1 collective-permute-start
  25.7 1.2 %collective-permute-done = f32[32,128]{1,0:T(8,128)S(1)} collective-permute-done((f32[32,128]{1,0:T(8,128)S(1)}, f32[32,128]{1,0:T(8,128)S(1)}, u32[]{:S(2)}, u32[]{:S(2)}) %collective-permute-start) | collective-permute-done | bytes 16416 | tf_op jit(solution)/shard_map/reduce/ppermute | solution.py:291
  26.9 0.0 collective-permute-done.1.y1_any
  26.9 0.0 collective-permute-done.2.y2_any
  26.9 0.0 collective-permute-done.3.y3_any
  26.9 0.4 join.1.after_ref.refs_1_
  27.3 0.2 collective-permute-start.7
  27.6 1.6 %collective-permute-start.4 = (f32[32,128]{1,0:T(8,128)S(1)}, f32[32,128]{1,0:T(8,128)S(1)}, u32[]{:S(2)}, u32[]{:S(2)}) collective-permute-start(f32[32,128]{1,0:T(8,128)S(1)} %add.3.after_ref.a_ref), channel_id=1, source_target_pairs={{0,2},{1,3},{2,4},{3,5},{4,6},{5,7},{6,0},{7,1},{8,10},{9,11},{10,... | collective-permute-start | bytes 49160 | tf_op jit(solution)/shard_map/reduce/ppermute | solution.py:292
  29.1 0.9 %collective-permute-start.5 = (f32[32,128]{1,0:T(8,128)S(1)}, f32[32,128]{1,0:T(8,128)S(1)}, u32[]{:S(2)}, u32[]{:S(2)}) collective-permute-start(f32[32,128]{1,0:T(8,128)S(1)} %add.3.after_ref.a_ref), channel_id=1, source_target_pairs={{0,4},{1,5},{2,6},{3,7},{4,0},{5,1},{6,2},{7,3},{8,12},{9,13},{10,... | collective-permute-start | bytes 49160 | tf_op jit(solution)/shard_map/reduce/ppermute | solution.py:292
  30.1 2.4 %collective-permute-start.6 = (f32[32,128]{1,0:T(8,128)S(1)}, f32[32,128]{1,0:T(8,128)S(1)}, u32[]{:S(2)}, u32[]{:S(2)}) collective-permute-start(f32[32,128]{1,0:T(8,128)S(1)} %add.3.after_ref.a_ref), channel_id=1, source_target_pairs={{0,6},{1,7},{2,0},{3,1},{4,2},{5,3},{6,4},{7,5},{8,14},{9,15},{10,... | collective-permute-start | bytes 49160 | tf_op jit(solution)/shard_map/reduce/ppermute | solution.py:292
  32.5 0.0 collective-permute-done.4.b_ref
  32.5 1.9 %collective-permute-done.5.c_ref = f32[32,128]{1,0:T(8,128)S(1)} collective-permute-done((f32[32,128]{1,0:T(8,128)S(1)}, f32[32,128]{1,0:T(8,128)S(1)}, u32[]{:S(2)}, u32[]{:S(2)}) %collective-permute-start.5) | collective-permute-done | bytes 16416 | tf_op jit(solution)/shard_map/reduce/ppermute | solution.py:292
  34.4 0.0 collective-permute-done.6.d_ref
  34.4 0.8 %up.1.refs_0_ = bf16[64,128]{1,0:T(8,128)(2,1)} custom-call(bf16[128,1024]{1,0:T(8,128)(2,1)S(1)} %join.1.after_ref.refs_1_, f32[32,128]{1,0:T(8,128)S(1)} %add.3.after_ref.a_ref, f32[32,128]{1,0:T(8,128)S(1)} %collective-permute-done.4.b_ref, f32[32,128]{1,0:T(8,128)S(1)} %collective-permute-done.5.c_ref, f32[32,128]{1,0:T(8,128)S(1)} %collective-permute-done.6.d_ref, ...), custom_call_target="tpu_custom_call" | custom-call | tf_op jit(solution)/shard_map/up/pallas_call | solution.py:344
  35.2 7.1 %all-to-all-start.1 = ((bf16[32,2,128]{2,1,0:T(2,128)(2,1)}), bf16[32,2,128]{2,1,0:T(2,128)(2,1)S(1)}, u32[]{:S(2)}, u32[]{:S(2)}) async-start(bf16[32,2,128]{2,1,0:T(2,128)(2,1)} %bitcast.6), calls=%async_computation.1 | async-start | bytes 32768 | tf_op jit(solution)/shard_map/answers/all_to_all | solution.py:349
  42.3 3.3 %middle.1 = (f32[128,128]{1,0:T(8,128)S(1)}, f32[128,128]{1,0:T(8,128)S(1)}, f32[128,128]{1,0:T(8,128)S(1)}, bf16[8192,256]{1,0:T(8,128)(2,1)S(1)}, bf16[32,1024...) custom-call(bf16[64,128]{1,0:T(8,128)(2,1)} %up.1.refs_0_, ...), custom_call_target="tpu_custom_call" | custom-call | flops 25165824 | bytes 3145728 | tf_op jit(solution)/shard_map/middle/pallas_call | solution.py:353
  45.7 0.0 collective-permute-done.7.refs_2_
  45.7 1.1 %late.1 = (f32[32,128]{1,0:T(8,128)S(1)}, bf16[32,128]{1,0:T(8,128)(2,1)S(1)}, f32[256,128]{1,0:T(8,128)S(1)}, f32[256,128]{1,0:T(8,128)S(1)}) custom-call(s32[1]{0:T(128)} %bitcast.9.refs_0_, bf16[128,1024]{1,0:T(8,128)(2,1)S(1)} %join.1.after_ref.refs_1_, bf16[128,1024]{1,0:T(8,128)(2,1)S(1)} %collective-permute-done.7.refs_2_, ...), custom_call_target="tpu_custom_call" | custom-call | flops 134217728 | bytes 4194304 | tf_op jit(solution)/shard_map/late/pallas_call | solution.py:365
  46.7 5.3 %all-to-all-done.1 = bf16[32,2,128]{2,1,0:T(2,128)(2,1)S(1)} async-done(((bf16[32,2,128]{2,1,0:T(2,128)(2,1)}), bf16[32,2,128]{2,1,0:T(2,128)(2,1)S(1)}, u32[]{:S(2)}, u32[]{:S(2)}) %all-to-all-start.1) | async-done | bytes 16416 | tf_op jit(solution)/shard_map/answers/all_to_all | solution.py:349
  52.0 0.8 %finish.1 = (bf16[32,1024]{1,0:T(8,128)(2,1)}, bf16[32,256]{1,0:T(8,128)(2,1)}) custom-call(bf16[64,128]{1,0:T(8,128)(2,1)S(1)} %bitcast.13, bf16[32,128]{1,0:T(8,128)(2,1)S(1)} %get-tuple-element.28.back_ref, f32[32,128]{1,0:T(8,128)S(1)} %get-tuple-element.38.value_ref, bf16[32,128]{1,0:T(8,128)(2,1)S(1)} %get-tuple-element.39.key_ref, ...), custom_call_target="tpu_custom_call" | custom-call | tf_op jit(solution)/shard_map/finish/pallas_call | solution.py:372
  (1 shorter events, 0.0 us)
Async XLA Ops:
  2.5 22.1 %all-to-all-start = ((bf16[32,9,2,128]{3,2,1,0:T(2,128)(2,1)}), bf16[32,9,2,128]{3,2,1,0:T(2,128)(2,1)S(1)}, u32[]{:S(2)}, u32[]{:S(2)}) async-start(bf16[32,9,2,128]{3,2,1,0:T(2,128)(2,1)} %bitcast.1), calls=%async_computation | async-start | bytes 294912 | tf_op jit(solution)/shard_map/rows_to_owners/all_to_all | solution.py:309
  13.9 10.8 %copy-start = (bf16[16,1024,64]{1,2,0:T(8,128)(2,1)S(1)}, bf16[16,1024,64]{1,2,0:T(8,128)(2,1)}, u32[]{:S(2)}) copy-start(bf16[16,1024,64]{1,2,0:T(8,128)(2,1)} %param.17) | copy-start | bytes 6291460
  13.9 13.0 %collective-permute-start.1 = (bf16[32,1024]{1,0:T(8,128)(2,1)S(1)}, bf16[32,1024]{1,0:T(8,128)(2,1)S(1)}, u32[]{:S(2)}, u32[]{:S(2)}) collective-permute-start(bf16[32,1024]{1,0:T(8,128)(2,1)S(1)} %get-tuple-element.25.own_any), channel_id=1, source_target_pairs={{0,2},{1,3},{2,4},{3,5},{4,6},{5,7},{6,0},{7,1},{8,10},{9,11},{10,... | collective-permute-start | bytes 196616 | tf_op jit(solution)/shard_map/gather_hidden/ppermute | solution.py:292
  15.5 11.4 %collective-permute-start.2 = (bf16[32,1024]{1,0:T(8,128)(2,1)S(1)}, bf16[32,1024]{1,0:T(8,128)(2,1)S(1)}, u32[]{:S(2)}, u32[]{:S(2)}) collective-permute-start(bf16[32,1024]{1,0:T(8,128)(2,1)S(1)} %get-tuple-element.25.own_any), channel_id=1, source_target_pairs={{0,4},{1,5},{2,6},{3,7},{4,0},{5,1},{6,2},{7,3},{8,12},{9,13},{10,... | collective-permute-start | bytes 196616 | tf_op jit(solution)/shard_map/gather_hidden/ppermute | solution.py:292
  16.5 10.4 %collective-permute-start.3 = (bf16[32,1024]{1,0:T(8,128)(2,1)S(1)}, bf16[32,1024]{1,0:T(8,128)(2,1)S(1)}, u32[]{:S(2)}, u32[]{:S(2)}) collective-permute-start(bf16[32,1024]{1,0:T(8,128)(2,1)S(1)} %get-tuple-element.25.own_any), channel_id=1, source_target_pairs={{0,6},{1,7},{2,0},{3,1},{4,2},{5,3},{6,4},{7,5},{8,14},{9,15},{10,... | collective-permute-start | bytes 196616 | tf_op jit(solution)/shard_map/gather_hidden/ppermute | solution.py:292
  25.6 1.3 %collective-permute-start = (f32[32,128]{1,0:T(8,128)S(1)}, f32[32,128]{1,0:T(8,128)S(1)}, u32[]{:S(2)}, u32[]{:S(2)}) collective-permute-start(f32[32,128]{1,0:T(8,128)S(1)} %get-tuple-element.24), channel_id=1, source_target_pairs={{0,1},{1,0},{2,3},{3,2},{4,5},{5,4},{6,7},{7,6},{8,9},{9,8},{10,11... | collective-permute-start | bytes 49160 | tf_op jit(solution)/shard_map/reduce/ppermute | solution.py:291
  27.3 18.3 %collective-permute-start.7 = (bf16[128,1024]{1,0:T(8,128)(2,1)S(1)}, bf16[128,1024]{1,0:T(8,128)(2,1)S(1)}, u32[]{:S(2)}, u32[]{:S(2)}) collective-permute-start(bf16[128,1024]{1,0:T(8,128)(2,1)S(1)} %join.1.after_ref.refs_1_), channel_id=1, source_target_pairs={{0,1},{1,0},{2,3},{3,2},{4,5},{5,4},{6,7},{7,6},{8,9},{9,8},{10,11... | collective-permute-start | bytes 786440 | tf_op jit(solution)/shard_map/gather_core/ppermute | solution.py:291
  27.6 4.9 %collective-permute-start.4 = (f32[32,128]{1,0:T(8,128)S(1)}, f32[32,128]{1,0:T(8,128)S(1)}, u32[]{:S(2)}, u32[]{:S(2)}) collective-permute-start(f32[32,128]{1,0:T(8,128)S(1)} %add.3.after_ref.a_ref), channel_id=1, source_target_pairs={{0,2},{1,3},{2,4},{3,5},{4,6},{5,7},{6,0},{7,1},{8,10},{9,11},{10,... | collective-permute-start | bytes 49160 | tf_op jit(solution)/shard_map/reduce/ppermute | solution.py:292
  29.1 5.2 %collective-permute-start.5 = (f32[32,128]{1,0:T(8,128)S(1)}, f32[32,128]{1,0:T(8,128)S(1)}, u32[]{:S(2)}, u32[]{:S(2)}) collective-permute-start(f32[32,128]{1,0:T(8,128)S(1)} %add.3.after_ref.a_ref), channel_id=1, source_target_pairs={{0,4},{1,5},{2,6},{3,7},{4,0},{5,1},{6,2},{7,3},{8,12},{9,13},{10,... | collective-permute-start | bytes 49160 | tf_op jit(solution)/shard_map/reduce/ppermute | solution.py:292
  30.1 4.3 %collective-permute-start.6 = (f32[32,128]{1,0:T(8,128)S(1)}, f32[32,128]{1,0:T(8,128)S(1)}, u32[]{:S(2)}, u32[]{:S(2)}) collective-permute-start(f32[32,128]{1,0:T(8,128)S(1)} %add.3.after_ref.a_ref), channel_id=1, source_target_pairs={{0,6},{1,7},{2,0},{3,1},{4,2},{5,3},{6,4},{7,5},{8,14},{9,15},{10,... | collective-permute-start | bytes 49160 | tf_op jit(solution)/shard_map/reduce/ppermute | solution.py:292
  35.2 16.8 %all-to-all-start.1 = ((bf16[32,2,128]{2,1,0:T(2,128)(2,1)}), bf16[32,2,128]{2,1,0:T(2,128)(2,1)S(1)}, u32[]{:S(2)}, u32[]{:S(2)}) async-start(bf16[32,2,128]{2,1,0:T(2,128)(2,1)} %bitcast.6), calls=%async_computation.1 | async-start | bytes 32768 | tf_op jit(solution)/shard_map/answers/all_to_all | solution.py:349

commit v5 on v4

--- a/solution.py
+++ b/solution.py
@@ -13,6 +13,7 @@
 ROPE_BASE = 500000.0
 MIB = 1 << 20
 EARLY_ROWS = 16
+TURN = 26
 
 F32, BF16, I32 = jnp.float32, jnp.bfloat16, jnp.int32
 VMEM = pl.BlockSpec(memory_space=pltpu.VMEM)
@@ -47,9 +48,10 @@
     return jnp.where(message == s * (2 * chunks) + k * 2 + c, 1.0, 0.0).astype(BF16)
 
 
-def slots_of(tenant_row, pool):
+def slots_of(tenant_row, pool, peers, turn):
     n = tenant_row.shape[1]
-    owner_row = jnp.floor(tenant_row * (1.0 / pool))
+    owner_row = jnp.floor(tenant_row * (1.0 / pool)) - turn
+    owner_row = jnp.where(owner_row < 0.0, owner_row + peers, owner_row)
     owner_col = upright(owner_row)
     same = (owner_col == owner_row) & (iota((n, n), 0) < iota((n, n), 1))
     rank = jnp.sum(jnp.where(same, 1.0, 0.0), axis=0, keepdims=True)
@@ -74,7 +76,7 @@
     mix = shuffle(chunks, True)
     fetch_tenant.wait()
     tenant_row = tenant_ref[...].astype(F32)
-    slot_row = slots_of(tenant_row, pool)
+    slot_row = slots_of(tenant_row, pool, slots // CAPACITY, TURN)
     place = jnp.where(slot_row == iota((slots, rows), 0).astype(F32), 1.0, 0.0).astype(BF16)
     local = tenant_row - pool * jnp.floor(tenant_row * (1.0 / pool))
     local = jnp.broadcast_to(upright(local), (rows, LANES)).astype(BF16)
@@ -187,7 +189,7 @@
                  copies[3].wait, sum_ref, top_ref, whole_ref)
 
 
-def middle_kernel(scale, pool, after_ref, length_hbm, query_hbm, key_hbm, value_hbm, tenant_hbm, row_hbm, inverse_hbm,
+def middle_kernel(scale, pool, peers, after_ref, length_hbm, query_hbm, key_hbm, value_hbm, tenant_hbm, row_hbm, inverse_hbm,
                   weight_hbm, sum_ref, top_ref, whole_ref, weight_ref,
                   query_ref, cosine_ref, sine_ref, back_ref, length_ref, key_ref, value_ref, tenant_ref, row_ref,
                   inverse_ref, sems):
@@ -204,7 +206,7 @@
     for copy in copies[:5]:
         copy.wait()
     lane = iota((rows, LANES), 1)
-    slot_col = upright(slots_of(tenant_ref[...].astype(F32), pool))
+    slot_col = upright(slots_of(tenant_ref[...].astype(F32), pool, peers, TURN))
     back_ref[...] = jnp.where(slot_col == lane.astype(F32), 1.0, 0.0).astype(BF16)
     angle = upright(row_ref[...].astype(F32)) * inverse_ref[...]
     sine = jnp.sin(angle)
@@ -292,6 +294,7 @@
     over_y = lambda x, k: lax.ppermute(x, "tensor", [(i, (i + 2 * k) % count) for i in range(count)])
 
     early = EARLY_ROWS
+    ring = [[(k + TURN) % peers for k in range(peers)]]
     late = rows - early
     states = lambda n: [shape((GROUP * n, LANES), F32)] * 3
     effort = lambda n: cost(4 * n * GROUP * length * LANES, 4 * n * length * LANES)
@@ -307,7 +310,7 @@
         )(*far(tenant_row, hidden))
     with jax.named_scope("rows_to_owners"):
         got = lax.all_to_all(
-            placed.reshape(peers, chunks, CAPACITY, LANES), "dp", split_axis=0, concat_axis=0, tiled=True
+            placed.reshape(peers, chunks, CAPACITY, LANES), "dp", split_axis=0, concat_axis=0, tiled=True, axis_index_groups=ring
         ).reshape(slots * chunks, LANES)
     with jax.named_scope("gather_hidden"):
         others = [over_y(handed, k) for k in (1, 2, 3)]
@@ -347,11 +350,11 @@
         )(near, pair_sum, *sums_y, ids, up_near)
     with jax.named_scope("answers"):
         returned = lax.all_to_all(
-            served.reshape(peers, CAPACITY, LANES), "dp", split_axis=0, concat_axis=0, tiled=True
+            served.reshape(peers, CAPACITY, LANES), "dp", split_axis=0, concat_axis=0, tiled=True, axis_index_groups=ring
         ).reshape(slots, LANES)
     with jax.named_scope("middle"):
         *second_state, weight_near, queries_near, cosine, sine, back = pl.pallas_call(
-            lambda *refs: middle_kernel(scale, pool, *refs),
+            lambda *refs: middle_kernel(scale, pool, peers, *refs),
             out_shape=states(late) + [
                 shape(weight.shape, BF16), shape(queries.shape, BF16),
                 shape((rows, LANES), F32), shape((rows, LANES), F32), shape((rows, LANES), BF16),

time: 53 us -> 48.8 us (0.921)
  the two profiles are of different devices: /device:TPU:8 before, /device:TPU:2 now
where the time goes in v5:
time: 48.8 us; the launch traced here: 47.9 us
  starting transfers between devices  30.4 us (62%)
  Pallas kernels  12 us (25%)
  waiting for transfers between devices  4.72 us (10%)
  between operations  0.76 us (2%)
    all_to_all x1, starting transfers between devices, on_device(): lax.all_to_all(placed.reshape(peers, chunks, CAPACITY, LANES), 'dp', spli...  10.8 us
    ppermute x6, starting transfers between devices, on_device(): lax.ppermute(x, 'tensor', [(i, (i + 2 * k) % count) for i in range(count)])  10.3 us
    all_to_all x1, starting transfers between devices, on_device(): lax.all_to_all(served.reshape(peers, CAPACITY, LANES), 'dp', split_axis=0...  9.04 us
    pallas_call x1, Pallas kernels, on_device(): pl.pallas_call(lambda *refs: middle_kernel(scale, pool, peers, *refs), ou...  3.31 us
    pallas_call x1, Pallas kernels, on_device(): pl.pallas_call(lambda *refs: early_kernel(scale, *refs), out_shape=states...  2.74 us
    ppermute x6, waiting for transfers between devices, on_device(): lax.ppermute(x, 'tensor', [(i, (i + 2 * k) % count) for i in range(count)])  2.4 us
    pallas_call x1, Pallas kernels, on_device(): pl.pallas_call(lambda *refs: place_kernel(pool, *refs), out_shape=[shape(...  1.89 us
    ppermute x2, waiting for transfers between devices, on_device(): lax.ppermute(x, 'tensor', [(i, i ^ 1) for i in range(count)])  1.17 us
  transfers between devices with their start and end apart: 10, of which 5 were waited for; matrix products, arithmetic and copies ran while one was open for 0% of the time, Pallas kernels for 19%

profile of v5, /device:TPU:2, one launch (start us, length us, event | category | flops | bytes accessed | tf_op | source)
XLA Modules:
  0.0 47.9 jit_solution(13974478628983682017)
XLA Ops:
  0.6 1.9 %place.1 = (bf16[576,128]{1,0:T(8,128)(2,1)}, bf16[32,1024]{1,0:T(8,128)(2,1)S(1)}) custom-call(s32[1,32]{1,0:T(1,128)} %bitcast.16, bf16[32,1024]{1,0:T(8,128)(2,1)} %refs_1_.3), custom_call_target="tpu_custom_call" | custom-call | tf_op jit(solution)/shard_map/place/pallas_call | solution.py:305
  2.5 10.8 %all-to-all-start = ((bf16[32,9,2,128]{3,2,1,0:T(2,128)(2,1)}), bf16[32,9,2,128]{3,2,1,0:T(2,128)(2,1)S(1)}, u32[]{:S(2)}, u32[]{:S(2)}) async-start(bf16[32,9,2,128]{3,2,1,0:T(2,128)(2,1)} %bitcast.1), calls=%async_computation | async-start | bytes 294912 | tf_op jit(solution)/shard_map/rows_to_owners/all_to_all | solution.py:312
  13.3 0.0 copy-start
  13.3 1.7 %collective-permute-start.1 = (bf16[32,1024]{1,0:T(8,128)(2,1)S(1)}, bf16[32,1024]{1,0:T(8,128)(2,1)S(1)}, u32[]{:S(2)}, u32[]{:S(2)}) collective-permute-start(bf16[32,1024]{1,0:T(8,128)(2,1)S(1)} %get-tuple-element.25.own_any), channel_id=1, source_target_pairs={{0,2},{1,3},{2,4},{3,5},{4,6},{5,7},{6,0},{7,1},{8,10},{9,11},{10,... | collective-permute-start | bytes 196616 | tf_op jit(solution)/shard_map/gather_hidden/ppermute | solution.py:294
  15.0 2.9 %collective-permute-start.2 = (bf16[32,1024]{1,0:T(8,128)(2,1)S(1)}, bf16[32,1024]{1,0:T(8,128)(2,1)S(1)}, u32[]{:S(2)}, u32[]{:S(2)}) collective-permute-start(bf16[32,1024]{1,0:T(8,128)(2,1)S(1)} %get-tuple-element.25.own_any), channel_id=1, source_target_pairs={{0,4},{1,5},{2,6},{3,7},{4,0},{5,1},{6,2},{7,3},{8,12},{9,13},{10,... | collective-permute-start | bytes 196616 | tf_op jit(solution)/shard_map/gather_hidden/ppermute | solution.py:294
  17.9 1.3 %collective-permute-start.3 = (bf16[32,1024]{1,0:T(8,128)(2,1)S(1)}, bf16[32,1024]{1,0:T(8,128)(2,1)S(1)}, u32[]{:S(2)}, u32[]{:S(2)}) collective-permute-start(bf16[32,1024]{1,0:T(8,128)(2,1)S(1)} %get-tuple-element.25.own_any), channel_id=1, source_target_pairs={{0,6},{1,7},{2,0},{3,1},{4,2},{5,3},{6,4},{7,5},{8,14},{9,15},{10,... | collective-permute-start | bytes 196616 | tf_op jit(solution)/shard_map/gather_hidden/ppermute | solution.py:294
  19.2 2.7 %early.1 = (f32[128,128]{1,0:T(8,128)S(1)}, f32[128,128]{1,0:T(8,128)S(1)}, f32[128,128]{1,0:T(8,128)S(1)}) custom-call(bf16[576,128]{1,0:T(8,128)(2,1)} %get-tuple-element.22.refs_0_, s32[32]{0:T(128)} %refs_1_.5, bf16[32,1024]{1,0:T(8,128)(2,1)} %refs_2_.3, bf16[32,384,128]{2,1,0:T(8,128)(2,1)} %refs_3_.3, bf16[32,384,128]{2,1,0:T(8,128)(2,1)} %refs_4_.3), custom_call_target="tpu_custom_call" | custom-call | flops 25165824 | bytes 3145728 | tf_op jit(solution)/shard_map/early/pallas_call | solution.py:318
  22.0 0.0 all-to-all-done
  22.0 0.0 copy-done
  22.0 1.0 %down.1 = (f32[32,128]{1,0:T(8,128)S(1)}, f32[64,128]{1,0:T(8,128)S(1)}, bf16[1024,128]{1,0:T(8,128)(2,1)S(1)}) custom-call(bf16[576,128]{1,0:T(8,128)(2,1)S(1)} %bitcast.12, bf16[1024,1024]{1,0:T(8,128)(2,1)S(1)} %bitcast.11, bf16[1024,128]{1,0:T(8,128)(2,1)} %bitcast.14, f32[128,128]{1,0:T(8,128)S(1)} %get-tuple-element.23.after_ref.refs_7_), custom_call_target="tpu_custom_call" | custom-call | tf_op jit(solution)/shard_map/down/pallas_call | solution.py:327
  23.0 0.1 collective-permute-start
  23.1 1.2 %collective-permute-done = f32[32,128]{1,0:T(8,128)S(1)} collective-permute-done((f32[32,128]{1,0:T(8,128)S(1)}, f32[32,128]{1,0:T(8,128)S(1)}, u32[]{:S(2)}, u32[]{:S(2)}) %collective-permute-start) | collective-permute-done | bytes 16416 | tf_op jit(solution)/shard_map/reduce/ppermute | solution.py:293
  24.3 0.0 collective-permute-done.1.y1_any
  24.3 0.0 collective-permute-done.2.y2_any
  24.3 0.0 collective-permute-done.3.y3_any
  24.3 0.4 join.1.after_ref.refs_1_
  24.7 0.2 collective-permute-start.7
  24.9 0.7 %collective-permute-start.4 = (f32[32,128]{1,0:T(8,128)S(1)}, f32[32,128]{1,0:T(8,128)S(1)}, u32[]{:S(2)}, u32[]{:S(2)}) collective-permute-start(f32[32,128]{1,0:T(8,128)S(1)} %add.3.after_ref.a_ref), channel_id=1, source_target_pairs={{0,2},{1,3},{2,4},{3,5},{4,6},{5,7},{6,0},{7,1},{8,10},{9,11},{10,... | collective-permute-start | bytes 49160 | tf_op jit(solution)/shard_map/reduce/ppermute | solution.py:294
  25.6 2.3 %collective-permute-start.5 = (f32[32,128]{1,0:T(8,128)S(1)}, f32[32,128]{1,0:T(8,128)S(1)}, u32[]{:S(2)}, u32[]{:S(2)}) collective-permute-start(f32[32,128]{1,0:T(8,128)S(1)} %add.3.after_ref.a_ref), channel_id=1, source_target_pairs={{0,4},{1,5},{2,6},{3,7},{4,0},{5,1},{6,2},{7,3},{8,12},{9,13},{10,... | collective-permute-start | bytes 49160 | tf_op jit(solution)/shard_map/reduce/ppermute | solution.py:294
  27.9 1.3 %collective-permute-start.6 = (f32[32,128]{1,0:T(8,128)S(1)}, f32[32,128]{1,0:T(8,128)S(1)}, u32[]{:S(2)}, u32[]{:S(2)}) collective-permute-start(f32[32,128]{1,0:T(8,128)S(1)} %add.3.after_ref.a_ref), channel_id=1, source_target_pairs={{0,6},{1,7},{2,0},{3,1},{4,2},{5,3},{6,4},{7,5},{8,14},{9,15},{10,... | collective-permute-start | bytes 49160 | tf_op jit(solution)/shard_map/reduce/ppermute | solution.py:294
  29.3 0.6 %collective-permute-done.4.b_ref = f32[32,128]{1,0:T(8,128)S(1)} collective-permute-done((f32[32,128]{1,0:T(8,128)S(1)}, f32[32,128]{1,0:T(8,128)S(1)}, u32[]{:S(2)}, u32[]{:S(2)}) %collective-permute-start.4) | collective-permute-done | bytes 16416 | tf_op jit(solution)/shard_map/reduce/ppermute | solution.py:294
  29.9 1.0 %collective-permute-done.5.c_ref = f32[32,128]{1,0:T(8,128)S(1)} collective-permute-done((f32[32,128]{1,0:T(8,128)S(1)}, f32[32,128]{1,0:T(8,128)S(1)}, u32[]{:S(2)}, u32[]{:S(2)}) %collective-permute-start.5) | collective-permute-done | bytes 16416 | tf_op jit(solution)/shard_map/reduce/ppermute | solution.py:294
  30.8 0.8 %collective-permute-done.6.d_ref = f32[32,128]{1,0:T(8,128)S(1)} collective-permute-done((f32[32,128]{1,0:T(8,128)S(1)}, f32[32,128]{1,0:T(8,128)S(1)}, u32[]{:S(2)}, u32[]{:S(2)}) %collective-permute-start.6) | collective-permute-done | bytes 16416 | tf_op jit(solution)/shard_map/reduce/ppermute | solution.py:294
  31.7 0.8 %up.1.refs_0_ = bf16[64,128]{1,0:T(8,128)(2,1)} custom-call(bf16[128,1024]{1,0:T(8,128)(2,1)S(1)} %join.1.after_ref.refs_1_, f32[32,128]{1,0:T(8,128)S(1)} %add.3.after_ref.a_ref, f32[32,128]{1,0:T(8,128)S(1)} %collective-permute-done.4.b_ref, f32[32,128]{1,0:T(8,128)S(1)} %collective-permute-done.5.c_ref, f32[32,128]{1,0:T(8,128)S(1)} %collective-permute-done.6.d_ref, ...), custom_call_target="tpu_custom_call" | custom-call | tf_op jit(solution)/shard_map/up/pallas_call | solution.py:347
  32.5 9.0 %all-to-all-start.1 = ((bf16[32,2,128]{2,1,0:T(2,128)(2,1)}), bf16[32,2,128]{2,1,0:T(2,128)(2,1)S(1)}, u32[]{:S(2)}, u32[]{:S(2)}) async-start(bf16[32,2,128]{2,1,0:T(2,128)(2,1)} %bitcast.6), calls=%async_computation.1 | async-start | bytes 32768 | tf_op jit(solution)/shard_map/answers/all_to_all | solution.py:352
  41.6 3.3 %middle.1 = (f32[128,128]{1,0:T(8,128)S(1)}, f32[128,128]{1,0:T(8,128)S(1)}, f32[128,128]{1,0:T(8,128)S(1)}, bf16[8192,256]{1,0:T(8,128)(2,1)S(1)}, bf16[32,1024...) custom-call(bf16[64,128]{1,0:T(8,128)(2,1)} %up.1.refs_0_, ...), custom_call_target="tpu_custom_call" | custom-call | flops 25165824 | bytes 3145728 | tf_op jit(solution)/shard_map/middle/pallas_call | solution.py:356
  44.9 0.0 collective-permute-done.7.refs_2_
  44.9 1.1 %late.1 = (f32[32,128]{1,0:T(8,128)S(1)}, bf16[32,128]{1,0:T(8,128)(2,1)S(1)}, f32[256,128]{1,0:T(8,128)S(1)}, f32[256,128]{1,0:T(8,128)S(1)}) custom-call(s32[1]{0:T(128)} %bitcast.9.refs_0_, bf16[128,1024]{1,0:T(8,128)(2,1)S(1)} %join.1.after_ref.refs_1_, bf16[128,1024]{1,0:T(8,128)(2,1)S(1)} %collective-permute-done.7.refs_2_, ...), custom_call_target="tpu_custom_call" | custom-call | flops 134217728 | bytes 4194304 | tf_op jit(solution)/shard_map/late/pallas_call | solution.py:368
  46.0 1.2 %all-to-all-done.1 = bf16[32,2,128]{2,1,0:T(2,128)(2,1)S(1)} async-done(((bf16[32,2,128]{2,1,0:T(2,128)(2,1)}), bf16[32,2,128]{2,1,0:T(2,128)(2,1)S(1)}, u32[]{:S(2)}, u32[]{:S(2)}) %all-to-all-start.1) | async-done | bytes 16416 | tf_op jit(solution)/shard_map/answers/all_to_all | solution.py:352
  47.1 0.8 %finish.1 = (bf16[32,1024]{1,0:T(8,128)(2,1)}, bf16[32,256]{1,0:T(8,128)(2,1)}) custom-call(bf16[64,128]{1,0:T(8,128)(2,1)S(1)} %bitcast.13, bf16[32,128]{1,0:T(8,128)(2,1)S(1)} %get-tuple-element.28.back_ref, f32[32,128]{1,0:T(8,128)S(1)} %get-tuple-element.38.value_ref, bf16[32,128]{1,0:T(8,128)(2,1)S(1)} %get-tuple-element.39.key_ref, ...), custom_call_target="tpu_custom_call" | custom-call | tf_op jit(solution)/shard_map/finish/pallas_call | solution.py:375
  (1 shorter events, 0.0 us)
Async XLA Ops:
  2.5 19.5 %all-to-all-start = ((bf16[32,9,2,128]{3,2,1,0:T(2,128)(2,1)}), bf16[32,9,2,128]{3,2,1,0:T(2,128)(2,1)S(1)}, u32[]{:S(2)}, u32[]{:S(2)}) async-start(bf16[32,9,2,128]{3,2,1,0:T(2,128)(2,1)} %bitcast.1), calls=%async_computation | async-start | bytes 294912 | tf_op jit(solution)/shard_map/rows_to_owners/all_to_all | solution.py:312
  13.3 8.7 %copy-start = (bf16[16,1024,64]{1,2,0:T(8,128)(2,1)S(1)}, bf16[16,1024,64]{1,2,0:T(8,128)(2,1)}, u32[]{:S(2)}) copy-start(bf16[16,1024,64]{1,2,0:T(8,128)(2,1)} %param.17) | copy-start | bytes 6291460
  13.3 10.9 %collective-permute-start.1 = (bf16[32,1024]{1,0:T(8,128)(2,1)S(1)}, bf16[32,1024]{1,0:T(8,128)(2,1)S(1)}, u32[]{:S(2)}, u32[]{:S(2)}) collective-permute-start(bf16[32,1024]{1,0:T(8,128)(2,1)S(1)} %get-tuple-element.25.own_any), channel_id=1, source_target_pairs={{0,2},{1,3},{2,4},{3,5},{4,6},{5,7},{6,0},{7,1},{8,10},{9,11},{10,... | collective-permute-start | bytes 196616 | tf_op jit(solution)/shard_map/gather_hidden/ppermute | solution.py:294
  15.0 9.3 %collective-permute-start.2 = (bf16[32,1024]{1,0:T(8,128)(2,1)S(1)}, bf16[32,1024]{1,0:T(8,128)(2,1)S(1)}, u32[]{:S(2)}, u32[]{:S(2)}) collective-permute-start(bf16[32,1024]{1,0:T(8,128)(2,1)S(1)} %get-tuple-element.25.own_any), channel_id=1, source_target_pairs={{0,4},{1,5},{2,6},{3,7},{4,0},{5,1},{6,2},{7,3},{8,12},{9,13},{10,... | collective-permute-start | bytes 196616 | tf_op jit(solution)/shard_map/gather_hidden/ppermute | solution.py:294
  17.9 6.4 %collective-permute-start.3 = (bf16[32,1024]{1,0:T(8,128)(2,1)S(1)}, bf16[32,1024]{1,0:T(8,128)(2,1)S(1)}, u32[]{:S(2)}, u32[]{:S(2)}) collective-permute-start(bf16[32,1024]{1,0:T(8,128)(2,1)S(1)} %get-tuple-element.25.own_any), channel_id=1, source_target_pairs={{0,6},{1,7},{2,0},{3,1},{4,2},{5,3},{6,4},{7,5},{8,14},{9,15},{10,... | collective-permute-start | bytes 196616 | tf_op jit(solution)/shard_map/gather_hidden/ppermute | solution.py:294
  23.0 1.3 %collective-permute-start = (f32[32,128]{1,0:T(8,128)S(1)}, f32[32,128]{1,0:T(8,128)S(1)}, u32[]{:S(2)}, u32[]{:S(2)}) collective-permute-start(f32[32,128]{1,0:T(8,128)S(1)} %get-tuple-element.24), channel_id=1, source_target_pairs={{0,1},{1,0},{2,3},{3,2},{4,5},{5,4},{6,7},{7,6},{8,9},{9,8},{10,11... | collective-permute-start | bytes 49160 | tf_op jit(solution)/shard_map/reduce/ppermute | solution.py:293
  24.7 20.2 %collective-permute-start.7 = (bf16[128,1024]{1,0:T(8,128)(2,1)S(1)}, bf16[128,1024]{1,0:T(8,128)(2,1)S(1)}, u32[]{:S(2)}, u32[]{:S(2)}) collective-permute-start(bf16[128,1024]{1,0:T(8,128)(2,1)S(1)} %join.1.after_ref.refs_1_), channel_id=1, source_target_pairs={{0,1},{1,0},{2,3},{3,2},{4,5},{5,4},{6,7},{7,6},{8,9},{9,8},{10,11... | collective-permute-start | bytes 786440 | tf_op jit(solution)/shard_map/gather_core/ppermute | solution.py:293
  24.9 5.0 %collective-permute-start.4 = (f32[32,128]{1,0:T(8,128)S(1)}, f32[32,128]{1,0:T(8,128)S(1)}, u32[]{:S(2)}, u32[]{:S(2)}) collective-permute-start(f32[32,128]{1,0:T(8,128)S(1)} %add.3.after_ref.a_ref), channel_id=1, source_target_pairs={{0,2},{1,3},{2,4},{3,5},{4,6},{5,7},{6,0},{7,1},{8,10},{9,11},{10,... | collective-permute-start | bytes 49160 | tf_op jit(solution)/shard_map/reduce/ppermute | solution.py:294
  25.6 5.2 %collective-permute-start.5 = (f32[32,128]{1,0:T(8,128)S(1)}, f32[32,128]{1,0:T(8,128)S(1)}, u32[]{:S(2)}, u32[]{:S(2)}) collective-permute-start(f32[32,128]{1,0:T(8,128)S(1)} %add.3.after_ref.a_ref), channel_id=1, source_target_pairs={{0,4},{1,5},{2,6},{3,7},{4,0},{5,1},{6,2},{7,3},{8,12},{9,13},{10,... | collective-permute-start | bytes 49160 | tf_op jit(solution)/shard_map/reduce/ppermute | solution.py:294
  27.9 3.7 %collective-permute-start.6 = (f32[32,128]{1,0:T(8,128)S(1)}, f32[32,128]{1,0:T(8,128)S(1)}, u32[]{:S(2)}, u32[]{:S(2)}) collective-permute-start(f32[32,128]{1,0:T(8,128)S(1)} %add.3.after_ref.a_ref), channel_id=1, source_target_pairs={{0,6},{1,7},{2,0},{3,1},{4,2},{5,3},{6,4},{7,5},{8,14},{9,15},{10,... | collective-permute-start | bytes 49160 | tf_op jit(solution)/shard_map/reduce/ppermute | solution.py:294
  32.5 14.6 %all-to-all-start.1 = ((bf16[32,2,128]{2,1,0:T(2,128)(2,1)}), bf16[32,2,128]{2,1,0:T(2,128)(2,1)S(1)}, u32[]{:S(2)}, u32[]{:S(2)}) async-start(bf16[32,2,128]{2,1,0:T(2,128)(2,1)} %bitcast.6), calls=%async_computation.1 | async-start | bytes 32768 | tf_op jit(solution)/shard_map/answers/all_to_all | solution.py:352

commit v6 on v5

--- a/solution.py
+++ b/solution.py
@@ -12,7 +12,8 @@
 LANES = 128
 ROPE_BASE = 500000.0
 MIB = 1 << 20
-EARLY_ROWS = 16
+EARLY_ROWS = 8
+INNER_ROWS = 16
 TURN = 26
 
 F32, BF16, I32 = jnp.float32, jnp.bfloat16, jnp.int32
@@ -130,7 +131,7 @@
     fetch_up.wait()
 
 
-def up_kernel(after_ref, a_ref, b_ref, c_ref, d_ref, ids_ref, up_ref, out_ref):
+def up_kernel(after_ref, after2_ref, a_ref, b_ref, c_ref, d_ref, ids_ref, up_ref, out_ref):
     total = (a_ref[...] + b_ref[...]) + (c_ref[...] + d_ref[...])
     turned = pltpu.roll(total, 64, 1)
     left = iota(total.shape, 1) < 64
@@ -172,10 +173,10 @@
         whole_ref[place, :] = whole[some]
 
 
-def early_kernel(scale, after_ref, length_hbm, query_hbm, key_hbm, value_hbm, sum_ref, top_ref, whole_ref, length_ref,
+def cache_kernel(scale, first, after_ref, length_hbm, query_hbm, key_hbm, value_hbm, sum_ref, top_ref, whole_ref, length_ref,
                  query_ref, key_ref, value_ref, sems):
     rows, count = query_ref.shape[0], key_ref.shape[0]
-    some = pl.ds(0, count)
+    some = pl.ds(first, count)
     copies = fetches(
         [
             (query_hbm, query_ref), (length_hbm, length_ref), (key_hbm.at[some], key_ref),
@@ -185,22 +186,23 @@
     )
     copies[0].wait()
     copies[1].wait()
-    attend_cache(scale, 0, count, rows, lambda r: length_ref[r], query_ref, key_ref, value_ref, copies[2].wait,
+    attend_cache(scale, first, count, rows, lambda r: length_ref[r], query_ref, key_ref, value_ref, copies[2].wait,
                  copies[3].wait, sum_ref, top_ref, whole_ref)
 
 
-def middle_kernel(scale, pool, peers, after_ref, length_hbm, query_hbm, key_hbm, value_hbm, tenant_hbm, row_hbm, inverse_hbm,
-                  weight_hbm, sum_ref, top_ref, whole_ref, weight_ref,
-                  query_ref, cosine_ref, sine_ref, back_ref, length_ref, key_ref, value_ref, tenant_ref, row_ref,
-                  inverse_ref, sems):
-    rows, count = query_ref.shape[0], key_ref.shape[0]
+def tables_kernel(scale, pool, peers, after_ref, length_hbm, query_hbm, key_hbm, value_hbm, tenant_hbm, row_hbm,
+                  inverse_hbm, weight_hbm, *refs):
+    *state_refs, weight_ref, query_ref, cosine_ref, sine_ref, back_ref = refs[:-7]
+    length_ref, key_ref, value_ref, tenant_ref, row_ref, inverse_ref, sems = refs[-7:]
+    rows = query_ref.shape[0]
+    count = key_ref.shape[0] if state_refs else 0
     some = pl.ds(rows - count, count)
     copies = fetches(
         [
             (query_hbm, query_ref), (length_hbm, length_ref), (tenant_hbm, tenant_ref), (row_hbm, row_ref),
-            (inverse_hbm, inverse_ref), (key_hbm.at[some], key_ref), (value_hbm.at[some], value_ref),
-            (weight_hbm, weight_ref),
-        ],
+            (inverse_hbm, inverse_ref), (weight_hbm, weight_ref),
+        ][: 5 if count else 6]
+        + ([(key_hbm.at[some], key_ref), (value_hbm.at[some], value_ref), (weight_hbm, weight_ref)] if count else []),
         sems,
     )
     for copy in copies[:5]:
@@ -212,10 +214,10 @@
     sine = jnp.sin(angle)
     cosine_ref[...] = jnp.cos(angle)
     sine_ref[...] = jnp.where(lane < 64, -sine, sine)
-    attend_cache(scale, rows - count, count, rows, lambda r: length_ref[r], query_ref, key_ref, value_ref,
-                 copies[5].wait, copies[6].wait, sum_ref, top_ref, whole_ref)
-    for copy in copies[7:]:
-        copy.wait()
+    if count:
+        attend_cache(scale, rows - count, count, rows, lambda r: length_ref[r], query_ref, key_ref, value_ref,
+                     copies[5].wait, copies[6].wait, *state_refs)
+    copies[-1].wait()
 
 
 def join_kernel(after_ref, own_any, y1_any, y2_any, y3_any, near_ref, sems):
@@ -226,9 +228,8 @@
 
 
 def late_kernel(scale, index_ref, near_ref, far_ref, weight_ref, query_ref, cosine_ref, sine_ref, *refs):
-    state_refs, (projected_ref, entry_ref, mixed_ref, share_ref) = refs[:6], refs[6:]
+    state_refs, (projected_ref, entry_ref, mixed_ref, share_ref) = refs[:-4], refs[-4:]
     rows, depth = query_ref.shape[0], near_ref.shape[1]
-    first = state_refs[0].shape[0] // GROUP
     me = index_ref[0]
     devices = weight_ref.shape[0] // depth
 
@@ -246,11 +247,15 @@
     key = (key * cosine_ref[...] + pltpu.roll(key, 64, 1) * sine_ref[...]).astype(BF16)
     entry_ref[...] = key
     key = key.astype(F32)
-    halves = ((0, first, state_refs[:3]), (first, rows - first, state_refs[3:]))
+    parts, start = [], 0
+    for k in range(0, len(state_refs), 3):
+        many = state_refs[k].shape[0] // GROUP
+        parts.append((start, many, state_refs[k : k + 3]))
+        start += many
     for h in range(GROUP):
         query = query_ref[:, h * LANES : (h + 1) * LANES].astype(F32)
         own = jnp.sum(query * key, axis=1, keepdims=True) * scale
-        for start, many, (sums, tops, wholes) in halves:
+        for start, many, (sums, tops, wholes) in parts:
             here, place = slice(h * many, (h + 1) * many), slice(h * rows + start, h * rows + start + many)
             mine, top = own[start : start + many], tops[here, :]
             highest = jnp.maximum(top, mine)
@@ -295,11 +300,22 @@
 
     early = EARLY_ROWS
     ring = [[(k + TURN) % peers for k in range(peers)]]
-    late = rows - early
+    inner = INNER_ROWS
+    late = rows - early - inner
     states = lambda n: [shape((GROUP * n, LANES), F32)] * 3
     effort = lambda n: cost(4 * n * GROUP * length * LANES, 4 * n * length * LANES)
     inverse = ROPE_BASE ** (-(np.arange(HEAD_SIZE // 2, dtype=np.float32) * 2.0) / HEAD_SIZE)
     inverse = jnp.asarray(np.concatenate([inverse, inverse])[None, :], F32)
+
+    def attend(first, many, after):
+        return pl.pallas_call(
+            lambda *refs: cache_kernel(scale, first, *refs),
+            out_shape=states(many),
+            in_specs=[ANY] + [HBM] * 4, out_specs=[VMEM] * 3,
+            scratch_shapes=[pltpu.SMEM((rows,), I32), vmem((rows, GROUP * LANES), BF16)]
+            + [vmem((many, length, LANES), BF16)] * 2 + [dma((4,))],
+            compiler_params=params(14), cost_estimate=effort(many),
+        )(after, *far(lengths, queries, key_cache, value_cache))
 
     with jax.named_scope("place"):
         placed, handed = pl.pallas_call(
@@ -315,14 +331,7 @@
     with jax.named_scope("gather_hidden"):
         others = [over_y(handed, k) for k in (1, 2, 3)]
     with jax.named_scope("early"):
-        first_state = pl.pallas_call(
-            lambda *refs: early_kernel(scale, *refs),
-            out_shape=states(early),
-            in_specs=[ANY] + [HBM] * 4, out_specs=[VMEM] * 3,
-            scratch_shapes=[pltpu.SMEM((rows,), I32), vmem((rows, GROUP * LANES), BF16)]
-            + [vmem((early, length, LANES), BF16)] * 2 + [dma((4,))],
-            compiler_params=params(12), cost_estimate=effort(early),
-        )(placed, *far(lengths, queries, key_cache, value_cache))
+        first_state = attend(0, early, placed)
     with jax.named_scope("down"):
         partial, ids, up_near = pl.pallas_call(
             down_kernel,
@@ -343,34 +352,37 @@
         )(pair_sum, handed, *others)
     with jax.named_scope("gather_core"):
         other = over_core(near)
+    with jax.named_scope("inner"):
+        second_state = attend(early, inner, pair_sum) if inner else []
     with jax.named_scope("up"):
         served = pl.pallas_call(
             up_kernel, out_shape=shape((slots, LANES), BF16),
-            in_specs=[ANY] + [VMEM] * 6, out_specs=VMEM, compiler_params=params(8),
-        )(near, pair_sum, *sums_y, ids, up_near)
+            in_specs=[ANY] * 2 + [VMEM] * 6, out_specs=VMEM, compiler_params=params(8),
+        )(near, second_state[0] if inner else near, pair_sum, *sums_y, ids, up_near)
     with jax.named_scope("answers"):
         returned = lax.all_to_all(
             served.reshape(peers, CAPACITY, LANES), "dp", split_axis=0, concat_axis=0, tiled=True, axis_index_groups=ring
         ).reshape(slots, LANES)
-    with jax.named_scope("middle"):
-        *second_state, weight_near, queries_near, cosine, sine, back = pl.pallas_call(
-            lambda *refs: middle_kernel(scale, pool, peers, *refs),
-            out_shape=states(late) + [
+    with jax.named_scope("tables"):
+        *third_state, weight_near, queries_near, cosine, sine, back = pl.pallas_call(
+            lambda *refs: tables_kernel(scale, pool, peers, *refs),
+            out_shape=(states(late) if late else []) + [
                 shape(weight.shape, BF16), shape(queries.shape, BF16),
                 shape((rows, LANES), F32), shape((rows, LANES), F32), shape((rows, LANES), BF16),
             ],
-            in_specs=[ANY] + [HBM] * 8, out_specs=[VMEM] * 8,
-            scratch_shapes=[pltpu.SMEM((rows,), I32)] + [vmem((late, length, LANES), BF16)] * 2
+            in_specs=[ANY] + [HBM] * 8, out_specs=[VMEM] * (8 if late else 5),
+            scratch_shapes=[pltpu.SMEM((rows,), I32)] + [vmem((max(late, 1), length, LANES), BF16)] * 2
             + [vmem((1, rows), I32), vmem((1, rows), I32), vmem((1, LANES), F32), dma((8,))],
-            compiler_params=params(12), cost_estimate=effort(late),
+            compiler_params=params(14), cost_estimate=effort(max(late, 8)),
         )(served, *far(lengths, queries, key_cache, value_cache, tenant_row, length_row, inverse, weight))
+    past = [*first_state, *second_state, *third_state]
     with jax.named_scope("late"):
         value, key, mixed, share = pl.pallas_call(
             lambda *refs: late_kernel(scale, *refs),
             out_shape=[shape((rows, LANES), F32), shape((rows, LANES), BF16)] + [shape((GROUP * rows, LANES), F32)] * 2,
-            in_specs=[SMEM] + [VMEM] * 12, out_specs=[VMEM] * 4, compiler_params=params(8),
+            in_specs=[SMEM] + [VMEM] * (6 + len(past)), out_specs=[VMEM] * 4, compiler_params=params(8),
             cost_estimate=cost(2 * rows * count * depth * 2 * LANES, weight.size * 2),
-        )(me, near, other, weight_near, queries_near, cosine, sine, *first_state, *second_state)
+        )(me, near, other, weight_near, queries_near, cosine, sine, *past)
     with jax.named_scope("finish"):
         return tuple(pl.pallas_call(
             final_kernel,

time: 48.8 us -> 47.8 us (0.980); the launches traced: 47.9 us -> 47.4 us
  waiting for transfers between devices: 4.72 us -> 2.84 us
  Pallas kernels: 12 us -> 13.5 us
    ppermute x6, waiting for transfers between devices: 2.4 us -> 0.02 us  [on_device(): lax.ppermute(x, 'tensor', [(i, (i + 2 * k) % count) for i in range(count)])]
    pallas_call x2 -> x3, Pallas kernels: 6.05 us -> 7.58 us  [the longest x2 4.75 us: attend(): pl.pallas_call(lambda *refs: cache_kernel(scale, first, *refs), out_shape...]
    all_to_all x1, starting transfers between devices: 9.04 us -> 8.21 us  [on_device(): lax.all_to_all(served.reshape(peers, CAPACITY, LANES), 'dp', split_axis=0...]
    ppermute x6, starting transfers between devices: 10.3 us -> 11 us  [on_device(): lax.ppermute(x, 'tensor', [(i, (i + 2 * k) % count) for i in range(count)])]
    all_to_all x1, waiting for transfers between devices: 1.15 us -> 1.65 us  [on_device(): lax.all_to_all(served.reshape(peers, CAPACITY, LANES), 'dp', split_axis=0...]
  transfers between devices with their start and end apart: 10 -> 10, of which waited for: 5 -> 2; matrix products, arithmetic and copies ran while one was open for 0% -> 0% of each run, Pallas kernels for 19% -> 22%
where the time goes in v6:
time: 47.8 us; the launch traced here: 47.4 us
  starting transfers between devices  30.3 us (63%)
  Pallas kernels  13.5 us (28%)
  waiting for transfers between devices  2.84 us (6%)
  between operations  0.79 us (2%)
    ppermute x6, starting transfers between devices, on_device(): lax.ppermute(x, 'tensor', [(i, (i + 2 * k) % count) for i in range(count)])  11 us
    all_to_all x1, starting transfers between devices, on_device(): lax.all_to_all(placed.reshape(peers, chunks, CAPACITY, LANES), 'dp', spli...  10.8 us
    all_to_all x1, starting transfers between devices, on_device(): lax.all_to_all(served.reshape(peers, CAPACITY, LANES), 'dp', split_axis=0...  8.21 us
    pallas_call x2, Pallas kernels, attend(): pl.pallas_call(lambda *refs: cache_kernel(scale, first, *refs), out_shape...  4.75 us
    pallas_call x1, Pallas kernels, on_device(): pl.pallas_call(lambda *refs: tables_kernel(scale, pool, peers, *refs), ou...  2.83 us
    pallas_call x1, Pallas kernels, on_device(): pl.pallas_call(lambda *refs: place_kernel(pool, *refs), out_shape=[shape(...  1.89 us
    all_to_all x1, waiting for transfers between devices, on_device(): lax.all_to_all(served.reshape(peers, CAPACITY, LANES), 'dp', split_axis=0...  1.65 us
    ppermute x2, waiting for transfers between devices, on_device(): lax.ppermute(x, 'tensor', [(i, i ^ 1) for i in range(count)])  1.17 us
  transfers between devices with their start and end apart: 10, of which 2 were waited for; matrix products, arithmetic and copies ran while one was open for 0% of the time, Pallas kernels for 22%

profile of v6, /device:TPU:2, one launch (start us, length us, event | category | flops | bytes accessed | tf_op | source)
XLA Modules:
  0.0 47.4 jit_solution(8071580543237176656)
XLA Ops:
  0.6 1.9 %place.1 = (bf16[576,128]{1,0:T(8,128)(2,1)}, bf16[32,1024]{1,0:T(8,128)(2,1)S(1)}) custom-call(s32[1,32]{1,0:T(1,128)} %bitcast.16, bf16[32,1024]{1,0:T(8,128)(2,1)} %refs_1_.4), custom_call_target="tpu_custom_call" | custom-call | tf_op jit(solution)/shard_map/place/pallas_call | solution.py:321
  2.5 10.8 %all-to-all-start = ((bf16[32,9,2,128]{3,2,1,0:T(2,128)(2,1)}), bf16[32,9,2,128]{3,2,1,0:T(2,128)(2,1)S(1)}, u32[]{:S(2)}, u32[]{:S(2)}) async-start(bf16[32,9,2,128]{3,2,1,0:T(2,128)(2,1)} %bitcast.1), calls=%async_computation | async-start | bytes 294912 | tf_op jit(solution)/shard_map/rows_to_owners/all_to_all | solution.py:328
  13.3 0.0 copy-start
  13.3 1.7 %collective-permute-start.1 = (bf16[32,1024]{1,0:T(8,128)(2,1)S(1)}, bf16[32,1024]{1,0:T(8,128)(2,1)S(1)}, u32[]{:S(2)}, u32[]{:S(2)}) collective-permute-start(bf16[32,1024]{1,0:T(8,128)(2,1)S(1)} %get-tuple-element.28.own_any), channel_id=1, source_target_pairs={{0,2},{1,3},{2,4},{3,5},{4,6},{5,7},{6,0},{7,1},{8,10},{9,11},{10,... | collective-permute-start | bytes 196616 | tf_op jit(solution)/shard_map/gather_hidden/ppermute | solution.py:299
  15.0 2.9 %collective-permute-start.2 = (bf16[32,1024]{1,0:T(8,128)(2,1)S(1)}, bf16[32,1024]{1,0:T(8,128)(2,1)S(1)}, u32[]{:S(2)}, u32[]{:S(2)}) collective-permute-start(bf16[32,1024]{1,0:T(8,128)(2,1)S(1)} %get-tuple-element.28.own_any), channel_id=1, source_target_pairs={{0,4},{1,5},{2,6},{3,7},{4,0},{5,1},{6,2},{7,3},{8,12},{9,13},{10,... | collective-permute-start | bytes 196616 | tf_op jit(solution)/shard_map/gather_hidden/ppermute | solution.py:299
  17.9 1.3 %collective-permute-start.3 = (bf16[32,1024]{1,0:T(8,128)(2,1)S(1)}, bf16[32,1024]{1,0:T(8,128)(2,1)S(1)}, u32[]{:S(2)}, u32[]{:S(2)}) collective-permute-start(bf16[32,1024]{1,0:T(8,128)(2,1)S(1)} %get-tuple-element.28.own_any), channel_id=1, source_target_pairs={{0,6},{1,7},{2,0},{3,1},{4,2},{5,3},{6,4},{7,5},{8,14},{9,15},{10,... | collective-permute-start | bytes 196616 | tf_op jit(solution)/shard_map/gather_hidden/ppermute | solution.py:299
  19.2 2.0 %early.1 = (f32[64,128]{1,0:T(8,128)S(1)}, f32[64,128]{1,0:T(8,128)S(1)}, f32[64,128]{1,0:T(8,128)S(1)}) custom-call(bf16[576,128]{1,0:T(8,128)(2,1)} %get-tuple-element.25.refs_0_, s32[32]{0:T(128)} %refs_1_.7, bf16[32,1024]{1,0:T(8,128)(2,1)} %refs_2_.5, bf16[32,384,128]{2,1,0:T(8,128)(2,1)} %refs_3_.5, bf16[32,384,128]{2,1,0:T(8,128)(2,1)} %refs_4_.5), custom_call_target="tpu_custom_call" | custom-call | flops 12582912 | bytes 1572864 | tf_op jit(solution)/shard_map/early/pallas_call | solution.py:311
  21.3 0.0 all-to-all-done
  21.3 0.0 copy-done
  21.3 1.0 %down.1 = (f32[32,128]{1,0:T(8,128)S(1)}, f32[64,128]{1,0:T(8,128)S(1)}, bf16[1024,128]{1,0:T(8,128)(2,1)S(1)}) custom-call(bf16[576,128]{1,0:T(8,128)(2,1)S(1)} %bitcast.12, bf16[1024,1024]{1,0:T(8,128)(2,1)S(1)} %bitcast.11, bf16[1024,128]{1,0:T(8,128)(2,1)} %bitcast.14, f32[64,128]{1,0:T(8,128)S(1)} %get-tuple-element.26.after_ref.refs_7_), custom_call_target="tpu_custom_call" | custom-call | tf_op jit(solution)/shard_map/down/pallas_call | solution.py:336
  22.3 0.1 collective-permute-start
  22.4 1.2 %collective-permute-done = f32[32,128]{1,0:T(8,128)S(1)} collective-permute-done((f32[32,128]{1,0:T(8,128)S(1)}, f32[32,128]{1,0:T(8,128)S(1)}, u32[]{:S(2)}, u32[]{:S(2)}) %collective-permute-start) | collective-permute-done | bytes 16416 | tf_op jit(solution)/shard_map/reduce/ppermute | solution.py:298
  23.5 0.0 collective-permute-done.1.y1_any
  23.5 0.0 collective-permute-done.2.y2_any
  23.6 0.0 collective-permute-done.3.y3_any
  23.6 0.4 join.1.after_ref.refs_1_
  24.0 0.2 collective-permute-start.7
  24.2 0.8 %collective-permute-start.4 = (f32[32,128]{1,0:T(8,128)S(1)}, f32[32,128]{1,0:T(8,128)S(1)}, u32[]{:S(2)}, u32[]{:S(2)}) collective-permute-start(f32[32,128]{1,0:T(8,128)S(1)} %add.3.after_ref.refs_0_.a_ref), channel_id=1, source_target_pairs={{0,2},{1,3},{2,4},{3,5},{4,6},{5,7},{6,0},{7,1},{8,10},{9,11},{10,... | collective-permute-start | bytes 49160 | tf_op jit(solution)/shard_map/reduce/ppermute | solution.py:299
  25.0 2.9 %collective-permute-start.5 = (f32[32,128]{1,0:T(8,128)S(1)}, f32[32,128]{1,0:T(8,128)S(1)}, u32[]{:S(2)}, u32[]{:S(2)}) collective-permute-start(f32[32,128]{1,0:T(8,128)S(1)} %add.3.after_ref.refs_0_.a_ref), channel_id=1, source_target_pairs={{0,4},{1,5},{2,6},{3,7},{4,0},{5,1},{6,2},{7,3},{8,12},{9,13},{10,... | collective-permute-start | bytes 49160 | tf_op jit(solution)/shard_map/reduce/ppermute | solution.py:299
  27.9 1.3 %collective-permute-start.6 = (f32[32,128]{1,0:T(8,128)S(1)}, f32[32,128]{1,0:T(8,128)S(1)}, u32[]{:S(2)}, u32[]{:S(2)}) collective-permute-start(f32[32,128]{1,0:T(8,128)S(1)} %add.3.after_ref.refs_0_.a_ref), channel_id=1, source_target_pairs={{0,6},{1,7},{2,0},{3,1},{4,2},{5,3},{6,4},{7,5},{8,14},{9,15},{10,... | collective-permute-start | bytes 49160 | tf_op jit(solution)/shard_map/reduce/ppermute | solution.py:299
  29.3 2.7 %inner.1 = (f32[128,128]{1,0:T(8,128)S(1)}, f32[128,128]{1,0:T(8,128)S(1)}, f32[128,128]{1,0:T(8,128)S(1)}) custom-call(f32[32,128]{1,0:T(8,128)S(1)} %add.3.after_ref.refs_0_.a_ref, s32[32]{0:T(128)} %refs_1_.7, bf16[32,1024]{1,0:T(8,128)(2,1)} %refs_2_.5, bf16[32,384,128]{2,1,0:T(8,128)(2,1)} %refs_3_.5, bf16[32,384,128]{2,1,0:T(8,128)(2,1)} %refs_4_.5), custom_call_target="tpu_custom_call" | custom-call | flops 25165824 | bytes 3145728 | tf_op jit(solution)/shard_map/inner/pallas_call | solution.py:311
  32.0 0.0 collective-permute-done.4.b_ref
  32.0 0.0 collective-permute-done.5.c_ref
  32.1 0.0 collective-permute-done.6.d_ref
  32.1 0.8 %up.1.refs_0_ = bf16[64,128]{1,0:T(8,128)(2,1)} custom-call(bf16[128,1024]{1,0:T(8,128)(2,1)S(1)} %join.1.after_ref.refs_1_, f32[128,128]{1,0:T(8,128)S(1)} %get-tuple-element.29.after2_ref.refs_10_, f32[32,128]{1,0:T(8,128)S(1)} %add.3.after_ref.refs_0_.a_ref, f32[32,128]{1,0:T(8,128)S(1)} %collective-permute-done.4.b_ref, ...), custom_call_target="tpu_custom_call" | custom-call | tf_op jit(solution)/shard_map/up/pallas_call | solution.py:358
  32.9 8.2 %all-to-all-start.1 = ((bf16[32,2,128]{2,1,0:T(2,128)(2,1)}), bf16[32,2,128]{2,1,0:T(2,128)(2,1)S(1)}, u32[]{:S(2)}, u32[]{:S(2)}) async-start(bf16[32,2,128]{2,1,0:T(2,128)(2,1)} %bitcast.6), calls=%async_computation.1 | async-start | bytes 32768 | tf_op jit(solution)/shard_map/answers/all_to_all | solution.py:363
  41.1 2.8 %tables.1 = (f32[64,128]{1,0:T(8,128)S(1)}, f32[64,128]{1,0:T(8,128)S(1)}, f32[64,128]{1,0:T(8,128)S(1)}, bf16[8192,256]{1,0:T(8,128)(2,1)S(1)}, bf16[32,1024]{1...) custom-call(bf16[64,128]{1,0:T(8,128)(2,1)} %up.1.refs_0_, ...), custom_call_target="tpu_custom_call" | custom-call | flops 12582912 | bytes 1572864 | tf_op jit(solution)/shard_map/tables/pallas_call | solution.py:367
  44.0 0.0 collective-permute-done.7.refs_2_
  44.0 1.0 %late.1 = (f32[32,128]{1,0:T(8,128)S(1)}, bf16[32,128]{1,0:T(8,128)(2,1)S(1)}, f32[256,128]{1,0:T(8,128)S(1)}, f32[256,128]{1,0:T(8,128)S(1)}) custom-call(s32[1]{0:T(128)} %bitcast.9.refs_0_, bf16[128,1024]{1,0:T(8,128)(2,1)S(1)} %join.1.after_ref.refs_1_, bf16[128,1024]{1,0:T(8,128)(2,1)S(1)} %collective-permute-done.7.refs_2_, ...), custom_call_target="tpu_custom_call" | custom-call | flops 134217728 | bytes 4194304 | tf_op jit(solution)/shard_map/late/pallas_call | solution.py:380
  45.0 1.6 %all-to-all-done.1 = bf16[32,2,128]{2,1,0:T(2,128)(2,1)S(1)} async-done(((bf16[32,2,128]{2,1,0:T(2,128)(2,1)}), bf16[32,2,128]{2,1,0:T(2,128)(2,1)S(1)}, u32[]{:S(2)}, u32[]{:S(2)}) %all-to-all-start.1) | async-done | bytes 16416 | tf_op jit(solution)/shard_map/answers/all_to_all | solution.py:363
  46.7 0.8 %finish.1 = (bf16[32,1024]{1,0:T(8,128)(2,1)}, bf16[32,256]{1,0:T(8,128)(2,1)}) custom-call(bf16[64,128]{1,0:T(8,128)(2,1)S(1)} %bitcast.13, bf16[32,128]{1,0:T(8,128)(2,1)S(1)} %get-tuple-element.32.back_ref, f32[32,128]{1,0:T(8,128)S(1)} %get-tuple-element.44.value_ref, bf16[32,128]{1,0:T(8,128)(2,1)S(1)} %get-tuple-element.45.key_ref, ...), custom_call_target="tpu_custom_call" | custom-call | tf_op jit(solution)/shard_map/finish/pallas_call | solution.py:387
  (1 shorter events, 0.0 us)
Async XLA Ops:
  2.5 18.7 %all-to-all-start = ((bf16[32,9,2,128]{3,2,1,0:T(2,128)(2,1)}), bf16[32,9,2,128]{3,2,1,0:T(2,128)(2,1)S(1)}, u32[]{:S(2)}, u32[]{:S(2)}) async-start(bf16[32,9,2,128]{3,2,1,0:T(2,128)(2,1)} %bitcast.1), calls=%async_computation | async-start | bytes 294912 | tf_op jit(solution)/shard_map/rows_to_owners/all_to_all | solution.py:328
  13.3 8.0 %copy-start = (bf16[16,1024,64]{1,2,0:T(8,128)(2,1)S(1)}, bf16[16,1024,64]{1,2,0:T(8,128)(2,1)}, u32[]{:S(2)}) copy-start(bf16[16,1024,64]{1,2,0:T(8,128)(2,1)} %param.17) | copy-start | bytes 6291460
  13.3 10.2 %collective-permute-start.1 = (bf16[32,1024]{1,0:T(8,128)(2,1)S(1)}, bf16[32,1024]{1,0:T(8,128)(2,1)S(1)}, u32[]{:S(2)}, u32[]{:S(2)}) collective-permute-start(bf16[32,1024]{1,0:T(8,128)(2,1)S(1)} %get-tuple-element.28.own_any), channel_id=1, source_target_pairs={{0,2},{1,3},{2,4},{3,5},{4,6},{5,7},{6,0},{7,1},{8,10},{9,11},{10,... | collective-permute-start | bytes 196616 | tf_op jit(solution)/shard_map/gather_hidden/ppermute | solution.py:299
  15.0 8.6 %collective-permute-start.2 = (bf16[32,1024]{1,0:T(8,128)(2,1)S(1)}, bf16[32,1024]{1,0:T(8,128)(2,1)S(1)}, u32[]{:S(2)}, u32[]{:S(2)}) collective-permute-start(bf16[32,1024]{1,0:T(8,128)(2,1)S(1)} %get-tuple-element.28.own_any), channel_id=1, source_target_pairs={{0,4},{1,5},{2,6},{3,7},{4,0},{5,1},{6,2},{7,3},{8,12},{9,13},{10,... | collective-permute-start | bytes 196616 | tf_op jit(solution)/shard_map/gather_hidden/ppermute | solution.py:299
  17.9 5.7 %collective-permute-start.3 = (bf16[32,1024]{1,0:T(8,128)(2,1)S(1)}, bf16[32,1024]{1,0:T(8,128)(2,1)S(1)}, u32[]{:S(2)}, u32[]{:S(2)}) collective-permute-start(bf16[32,1024]{1,0:T(8,128)(2,1)S(1)} %get-tuple-element.28.own_any), channel_id=1, source_target_pairs={{0,6},{1,7},{2,0},{3,1},{4,2},{5,3},{6,4},{7,5},{8,14},{9,15},{10,... | collective-permute-start | bytes 196616 | tf_op jit(solution)/shard_map/gather_hidden/ppermute | solution.py:299
  22.3 1.3 %collective-permute-start = (f32[32,128]{1,0:T(8,128)S(1)}, f32[32,128]{1,0:T(8,128)S(1)}, u32[]{:S(2)}, u32[]{:S(2)}) collective-permute-start(f32[32,128]{1,0:T(8,128)S(1)} %get-tuple-element.27), channel_id=1, source_target_pairs={{0,1},{1,0},{2,3},{3,2},{4,5},{5,4},{6,7},{7,6},{8,9},{9,8},{10,11... | collective-permute-start | bytes 49160 | tf_op jit(solution)/shard_map/reduce/ppermute | solution.py:298
  24.0 20.0 %collective-permute-start.7 = (bf16[128,1024]{1,0:T(8,128)(2,1)S(1)}, bf16[128,1024]{1,0:T(8,128)(2,1)S(1)}, u32[]{:S(2)}, u32[]{:S(2)}) collective-permute-start(bf16[128,1024]{1,0:T(8,128)(2,1)S(1)} %join.1.after_ref.refs_1_), channel_id=1, source_target_pairs={{0,1},{1,0},{2,3},{3,2},{4,5},{5,4},{6,7},{7,6},{8,9},{9,8},{10,11... | collective-permute-start | bytes 786440 | tf_op jit(solution)/shard_map/gather_core/ppermute | solution.py:298
  24.2 7.8 %collective-permute-start.4 = (f32[32,128]{1,0:T(8,128)S(1)}, f32[32,128]{1,0:T(8,128)S(1)}, u32[]{:S(2)}, u32[]{:S(2)}) collective-permute-start(f32[32,128]{1,0:T(8,128)S(1)} %add.3.after_ref.refs_0_.a_ref), channel_id=1, source_target_pairs={{0,2},{1,3},{2,4},{3,5},{4,6},{5,7},{6,0},{7,1},{8,10},{9,11},{10,... | collective-permute-start | bytes 49160 | tf_op jit(solution)/shard_map/reduce/ppermute | solution.py:299
  25.0 7.0 %collective-permute-start.5 = (f32[32,128]{1,0:T(8,128)S(1)}, f32[32,128]{1,0:T(8,128)S(1)}, u32[]{:S(2)}, u32[]{:S(2)}) collective-permute-start(f32[32,128]{1,0:T(8,128)S(1)} %add.3.after_ref.refs_0_.a_ref), channel_id=1, source_target_pairs={{0,4},{1,5},{2,6},{3,7},{4,0},{5,1},{6,2},{7,3},{8,12},{9,13},{10,... | collective-permute-start | bytes 49160 | tf_op jit(solution)/shard_map/reduce/ppermute | solution.py:299
  27.9 4.1 %collective-permute-start.6 = (f32[32,128]{1,0:T(8,128)S(1)}, f32[32,128]{1,0:T(8,128)S(1)}, u32[]{:S(2)}, u32[]{:S(2)}) collective-permute-start(f32[32,128]{1,0:T(8,128)S(1)} %add.3.after_ref.refs_0_.a_ref), channel_id=1, source_target_pairs={{0,6},{1,7},{2,0},{3,1},{4,2},{5,3},{6,4},{7,5},{8,14},{9,15},{10,... | collective-permute-start | bytes 49160 | tf_op jit(solution)/shard_map/reduce/ppermute | solution.py:299
  32.9 13.8 %all-to-all-start.1 = ((bf16[32,2,128]{2,1,0:T(2,128)(2,1)}), bf16[32,2,128]{2,1,0:T(2,128)(2,1)S(1)}, u32[]{:S(2)}, u32[]{:S(2)}) async-start(bf16[32,2,128]{2,1,0:T(2,128)(2,1)} %bitcast.6), calls=%async_computation.1 | async-start | bytes 32768 | tf_op jit(solution)/shard_map/answers/all_to_all | solution.py:363

commit v7 on v5

--- a/solution.py
+++ b/solution.py
@@ -12,8 +12,8 @@
 LANES = 128
 ROPE_BASE = 500000.0
 MIB = 1 << 20
-EARLY_ROWS = 16
 TURN = 26
+MARKS = 3
 
 F32, BF16, I32 = jnp.float32, jnp.bfloat16, jnp.int32
 VMEM = pl.BlockSpec(memory_space=pltpu.VMEM)
@@ -98,9 +98,9 @@
         out_ref[g * wide : (g + 1) * wide, :] = turned[:, g * LANES : (g + 1) * LANES]
 
 
-def down_kernel(got_ref, down_ref, up_hbm, after_ref, partial_ref, ids_ref, up_ref, sem):
-    fetch_up = pltpu.make_async_copy(up_hbm, up_ref, sem)
-    fetch_up.start()
+def down_kernel(got_ref, down_ref, up_hbm, query_hbm, length_hbm, after_ref, partial_ref, ids_ref, up_ref, query_ref,
+                length_ref, sems):
+    copies = fetches([(up_hbm, up_ref), (query_hbm, query_ref), (length_hbm, length_ref)], sems)
     slots = ids_ref.shape[0]
     chunks = got_ref.shape[0] // slots
     groups, wide = slots // 16, 16 * chunks
@@ -127,10 +127,11 @@
     half = slots // 2
     partial_ref[...] = jnp.where(lane[:half] < 64, total[:half], total[half:])
     ids_ref[...] = ids
-    fetch_up.wait()
-
-
-def up_kernel(after_ref, a_ref, b_ref, c_ref, d_ref, ids_ref, up_ref, out_ref):
+    for copy in copies:
+        copy.wait()
+
+
+def up_kernel(after_ref, after2_ref, a_ref, b_ref, c_ref, d_ref, ids_ref, up_ref, out_ref):
     total = (a_ref[...] + b_ref[...]) + (c_ref[...] + d_ref[...])
     turned = pltpu.roll(total, 64, 1)
     left = iota(total.shape, 1) < 64
@@ -143,67 +144,45 @@
     out_ref[...] = dot(jnp.concatenate(spread, axis=1), up_ref[...]).astype(BF16)
 
 
-def attend_cache(scale, first, count, rows, length_at, query_ref, key_ref, value_ref, wait_key, wait_value, sum_ref,
-                 top_ref, whole_ref):
-    length = key_ref.shape[1]
-    wide = count * GROUP
+def cache_kernel(scale, after_ref, length_ref, query_ref, key_ref, value_ref, sum_ref, top_ref, whole_ref):
+    rows, length = key_ref.shape[0], key_ref.shape[1]
+    wide = rows * GROUP
     by_head = jnp.concatenate([query_ref[:, h * LANES : (h + 1) * LANES] for h in range(GROUP)], axis=0)
-    row, col = iota((wide, GROUP * rows), 0), iota((wide, GROUP * rows), 1)
-    turn = jnp.where(col == (row % GROUP) * rows + row // GROUP + first, 1.0, 0.0).astype(BF16)
+    row, col = iota((wide, wide), 0), iota((wide, wide), 1)
+    turn = jnp.where(col == (row % GROUP) * rows + row // GROUP, 1.0, 0.0).astype(BF16)
     by_row = dot(turn, by_head)
-    position = iota((GROUP, length), 1)
-    wait_key()
+    position = iota((GROUP, length), 1).astype(F32)
+    limit = jnp.broadcast_to(upright(length_ref[...].astype(F32)), (rows, length))
     scores = []
-    for r in range(count):
+    for r in range(rows):
         query = by_row[r * GROUP : (r + 1) * GROUP].astype(BF16)
         score = dot_t(query, key_ref[r]) * scale
-        scores.append(jnp.where(position < length_at(first + r), score, -jnp.inf))
+        scores.append(jnp.where(position < limit[r : r + 1], score, -jnp.inf))
     scores = jnp.concatenate(scores, axis=0)
     top = jnp.max(scores, axis=1, keepdims=True)
     weights = jnp.exp(scores - top)
     whole = jnp.broadcast_to(jnp.sum(weights, axis=1, keepdims=True), (wide, LANES))
     top = jnp.broadcast_to(top, (wide, LANES))
-    wait_value()
-    for r in range(count):
+    for r in range(rows):
         some = slice(r * GROUP, (r + 1) * GROUP)
-        place = pl.ds(r, GROUP, stride=count)
+        place = pl.ds(r, GROUP, stride=rows)
         sum_ref[place, :] = dot(weights[some].astype(BF16), value_ref[r])
         top_ref[place, :] = top[some]
         whole_ref[place, :] = whole[some]
 
 
-def early_kernel(scale, after_ref, length_hbm, query_hbm, key_hbm, value_hbm, sum_ref, top_ref, whole_ref, length_ref,
-                 query_ref, key_ref, value_ref, sems):
-    rows, count = query_ref.shape[0], key_ref.shape[0]
-    some = pl.ds(0, count)
+def mark_kernel(*refs):
+    out_ref = refs[-1]
+    out_ref[...] = jnp.zeros(out_ref.shape, F32)
+
+
+def tables_kernel(pool, peers, after_ref, tenant_hbm, row_hbm, inverse_hbm, weight_hbm, weight_ref, cosine_ref, sine_ref,
+                  back_ref, tenant_ref, row_ref, inverse_ref, sems):
+    rows = back_ref.shape[0]
     copies = fetches(
-        [
-            (query_hbm, query_ref), (length_hbm, length_ref), (key_hbm.at[some], key_ref),
-            (value_hbm.at[some], value_ref),
-        ],
-        sems,
-    )
-    copies[0].wait()
-    copies[1].wait()
-    attend_cache(scale, 0, count, rows, lambda r: length_ref[r], query_ref, key_ref, value_ref, copies[2].wait,
-                 copies[3].wait, sum_ref, top_ref, whole_ref)
-
-
-def middle_kernel(scale, pool, peers, after_ref, length_hbm, query_hbm, key_hbm, value_hbm, tenant_hbm, row_hbm, inverse_hbm,
-                  weight_hbm, sum_ref, top_ref, whole_ref, weight_ref,
-                  query_ref, cosine_ref, sine_ref, back_ref, length_ref, key_ref, value_ref, tenant_ref, row_ref,
-                  inverse_ref, sems):
-    rows, count = query_ref.shape[0], key_ref.shape[0]
-    some = pl.ds(rows - count, count)
-    copies = fetches(
-        [
-            (query_hbm, query_ref), (length_hbm, length_ref), (tenant_hbm, tenant_ref), (row_hbm, row_ref),
-            (inverse_hbm, inverse_ref), (key_hbm.at[some], key_ref), (value_hbm.at[some], value_ref),
-            (weight_hbm, weight_ref),
-        ],
-        sems,
-    )
-    for copy in copies[:5]:
+        [(tenant_hbm, tenant_ref), (row_hbm, row_ref), (inverse_hbm, inverse_ref), (weight_hbm, weight_ref)], sems
+    )
+    for copy in copies[:3]:
         copy.wait()
     lane = iota((rows, LANES), 1)
     slot_col = upright(slots_of(tenant_ref[...].astype(F32), pool, peers, TURN))
@@ -212,10 +191,7 @@
     sine = jnp.sin(angle)
     cosine_ref[...] = jnp.cos(angle)
     sine_ref[...] = jnp.where(lane < 64, -sine, sine)
-    attend_cache(scale, rows - count, count, rows, lambda r: length_ref[r], query_ref, key_ref, value_ref,
-                 copies[5].wait, copies[6].wait, sum_ref, top_ref, whole_ref)
-    for copy in copies[7:]:
-        copy.wait()
+    copies[-1].wait()
 
 
 def join_kernel(after_ref, own_any, y1_any, y2_any, y3_any, near_ref, sems):
@@ -225,10 +201,9 @@
         copy.wait()
 
 
-def late_kernel(scale, index_ref, near_ref, far_ref, weight_ref, query_ref, cosine_ref, sine_ref, *refs):
-    state_refs, (projected_ref, entry_ref, mixed_ref, share_ref) = refs[:6], refs[6:]
+def late_kernel(scale, index_ref, near_ref, far_ref, weight_ref, query_ref, cosine_ref, sine_ref, sum_ref, top_ref,
+                whole_ref, projected_ref, entry_ref, mixed_ref, share_ref):
     rows, depth = query_ref.shape[0], near_ref.shape[1]
-    first = state_refs[0].shape[0] // GROUP
     me = index_ref[0]
     devices = weight_ref.shape[0] // depth
 
@@ -246,18 +221,16 @@
     key = (key * cosine_ref[...] + pltpu.roll(key, 64, 1) * sine_ref[...]).astype(BF16)
     entry_ref[...] = key
     key = key.astype(F32)
-    halves = ((0, first, state_refs[:3]), (first, rows - first, state_refs[3:]))
     for h in range(GROUP):
+        place = slice(h * rows, (h + 1) * rows)
         query = query_ref[:, h * LANES : (h + 1) * LANES].astype(F32)
         own = jnp.sum(query * key, axis=1, keepdims=True) * scale
-        for start, many, (sums, tops, wholes) in halves:
-            here, place = slice(h * many, (h + 1) * many), slice(h * rows + start, h * rows + start + many)
-            mine, top = own[start : start + many], tops[here, :]
-            highest = jnp.maximum(top, mine)
-            old, new = jnp.exp(top - highest), jnp.exp(mine - highest)
-            under = 1.0 / (old * wholes[here, :] + new)
-            mixed_ref[place, :] = sums[here, :] * (old * under)
-            share_ref[place, :] = new * under
+        top = top_ref[place, :]
+        highest = jnp.maximum(top, own)
+        old, new = jnp.exp(top - highest), jnp.exp(own - highest)
+        under = 1.0 / (old * whole_ref[place, :] + new)
+        mixed_ref[place, :] = sum_ref[place, :] * (old * under)
+        share_ref[place, :] = new * under
 
 
 def final_kernel(got_ref, back_ref, value_ref, key_ref, mixed_ref, share_ref, out_ref, entry_ref):
@@ -280,7 +253,6 @@
     slots = peers * CAPACITY
     pool, _, rank = down.shape
     chunks = depth // LANES + 1
-    length = key_cache.shape[1]
     scale = HEAD_SIZE ** -0.5
     shape, vmem, dma = jax.ShapeDtypeStruct, pltpu.VMEM, pltpu.SemaphoreType.DMA
     params = lambda size: pltpu.CompilerParams(vmem_limit_bytes=size * MIB)
@@ -293,11 +265,7 @@
     over_core = lambda x: lax.ppermute(x, "tensor", [(i, i ^ 1) for i in range(count)])
     over_y = lambda x, k: lax.ppermute(x, "tensor", [(i, (i + 2 * k) % count) for i in range(count)])
 
-    early = EARLY_ROWS
     ring = [[(k + TURN) % peers for k in range(peers)]]
-    late = rows - early
-    states = lambda n: [shape((GROUP * n, LANES), F32)] * 3
-    effort = lambda n: cost(4 * n * GROUP * length * LANES, 4 * n * length * LANES)
     inverse = ROPE_BASE ** (-(np.arange(HEAD_SIZE // 2, dtype=np.float32) * 2.0) / HEAD_SIZE)
     inverse = jnp.asarray(np.concatenate([inverse, inverse])[None, :], F32)
 
@@ -314,25 +282,22 @@
         ).reshape(slots * chunks, LANES)
     with jax.named_scope("gather_hidden"):
         others = [over_y(handed, k) for k in (1, 2, 3)]
-    with jax.named_scope("early"):
-        first_state = pl.pallas_call(
-            lambda *refs: early_kernel(scale, *refs),
-            out_shape=states(early),
-            in_specs=[ANY] + [HBM] * 4, out_specs=[VMEM] * 3,
-            scratch_shapes=[pltpu.SMEM((rows,), I32), vmem((rows, GROUP * LANES), BF16)]
-            + [vmem((early, length, LANES), BF16)] * 2 + [dma((4,))],
-            compiler_params=params(12), cost_estimate=effort(early),
-        )(placed, *far(lengths, queries, key_cache, value_cache))
+    with jax.named_scope("mark"):
+        mark = pl.pallas_call(
+            mark_kernel, out_shape=shape((8, LANES), F32), in_specs=[ANY] + [HBM] * 2, out_specs=VMEM,
+            compiler_params=params(2),
+        )(placed, *far(key_cache, value_cache))
     with jax.named_scope("down"):
-        partial, ids, up_near = pl.pallas_call(
+        partial, ids, up_near, queries_near, length_near = pl.pallas_call(
             down_kernel,
             out_shape=[
-                shape((slots // 2, LANES), F32), shape((slots, LANES), F32), shape((pool * rank, LANES), BF16)
+                shape((slots // 2, LANES), F32), shape((slots, LANES), F32), shape((pool * rank, LANES), BF16),
+                shape(queries.shape, BF16), shape((1, rows), I32),
             ],
-            in_specs=[VMEM] * 2 + [HBM, ANY], out_specs=[VMEM] * 3, compiler_params=params(16),
-            scratch_shapes=[dma],
-        )(got, jnp.swapaxes(down, 1, 2).reshape(pool * rank, depth), *far(up.reshape(pool * rank, LANES)),
-          first_state[0])
+            in_specs=[VMEM] * 2 + [HBM] * 3 + [ANY], out_specs=[VMEM] * 5, compiler_params=params(8),
+            scratch_shapes=[dma((3,))],
+        )(got, jnp.swapaxes(down, 1, 2).reshape(pool * rank, depth),
+          *far(up.reshape(pool * rank, LANES), queries, length_row), mark)
     with jax.named_scope("reduce"):
         pair_sum = partial + over_core(partial)
         sums_y = [over_y(pair_sum, k) for k in (1, 2, 3)]
@@ -343,34 +308,44 @@
         )(pair_sum, handed, *others)
     with jax.named_scope("gather_core"):
         other = over_core(near)
+    with jax.named_scope("mark2"):
+        mark = pl.pallas_call(
+            mark_kernel, out_shape=shape((8, LANES), F32), in_specs=[ANY] + [HBM] * MARKS, out_specs=VMEM,
+            compiler_params=params(2),
+        )(pair_sum, *far(key_cache, value_cache, weight)[:MARKS])
+    with jax.named_scope("cache"):
+        states = pl.pallas_call(
+            lambda *refs: cache_kernel(scale, *refs),
+            out_shape=[shape((GROUP * rows, LANES), F32)] * 3,
+            in_specs=[ANY] + [VMEM] * 4, out_specs=[VMEM] * 3, compiler_params=params(8),
+        )(mark, length_near, queries_near, key_cache, value_cache)
     with jax.named_scope("up"):
         served = pl.pallas_call(
             up_kernel, out_shape=shape((slots, LANES), BF16),
-            in_specs=[ANY] + [VMEM] * 6, out_specs=VMEM, compiler_params=params(8),
-        )(near, pair_sum, *sums_y, ids, up_near)
+            in_specs=[ANY] * 2 + [VMEM] * 6, out_specs=VMEM, compiler_params=params(8),
+        )(near, states[0], pair_sum, *sums_y, ids, up_near)
     with jax.named_scope("answers"):
         returned = lax.all_to_all(
             served.reshape(peers, CAPACITY, LANES), "dp", split_axis=0, concat_axis=0, tiled=True, axis_index_groups=ring
         ).reshape(slots, LANES)
-    with jax.named_scope("middle"):
-        *second_state, weight_near, queries_near, cosine, sine, back = pl.pallas_call(
-            lambda *refs: middle_kernel(scale, pool, peers, *refs),
-            out_shape=states(late) + [
-                shape(weight.shape, BF16), shape(queries.shape, BF16),
-                shape((rows, LANES), F32), shape((rows, LANES), F32), shape((rows, LANES), BF16),
+    with jax.named_scope("tables"):
+        weight_near, cosine, sine, back = pl.pallas_call(
+            lambda *refs: tables_kernel(pool, peers, *refs),
+            out_shape=[
+                shape(weight.shape, BF16), shape((rows, LANES), F32), shape((rows, LANES), F32),
+                shape((rows, LANES), BF16),
             ],
-            in_specs=[ANY] + [HBM] * 8, out_specs=[VMEM] * 8,
-            scratch_shapes=[pltpu.SMEM((rows,), I32)] + [vmem((late, length, LANES), BF16)] * 2
-            + [vmem((1, rows), I32), vmem((1, rows), I32), vmem((1, LANES), F32), dma((8,))],
-            compiler_params=params(12), cost_estimate=effort(late),
-        )(served, *far(lengths, queries, key_cache, value_cache, tenant_row, length_row, inverse, weight))
+            in_specs=[ANY] + [HBM] * 4, out_specs=[VMEM] * 4,
+            scratch_shapes=[vmem((1, rows), I32), vmem((1, rows), I32), vmem((1, LANES), F32), dma((4,))],
+            compiler_params=params(8),
+        )(served, *far(tenant_row, length_row, inverse, weight))
     with jax.named_scope("late"):
         value, key, mixed, share = pl.pallas_call(
             lambda *refs: late_kernel(scale, *refs),
             out_shape=[shape((rows, LANES), F32), shape((rows, LANES), BF16)] + [shape((GROUP * rows, LANES), F32)] * 2,
-            in_specs=[SMEM] + [VMEM] * 12, out_specs=[VMEM] * 4, compiler_params=params(8),
+            in_specs=[SMEM] + [VMEM] * 9, out_specs=[VMEM] * 4, compiler_params=params(8),
             cost_estimate=cost(2 * rows * count * depth * 2 * LANES, weight.size * 2),
-        )(me, near, other, weight_near, queries_near, cosine, sine, *first_state, *second_state)
+        )(me, near, other, weight_near, queries_near, cosine, sine, *states)
     with jax.named_scope("finish"):
         return tuple(pl.pallas_call(
             final_kernel,

time: 48.8 us -> 47.7 us (0.977); the launches traced: 47.9 us -> 47.5 us
  Pallas kernels: 12 us -> 10.1 us
  starting transfers between devices: 30.4 us -> 31.4 us
    ppermute x6, waiting for transfers between devices: 2.4 us -> 0.48 us  [on_device(): lax.ppermute(x, 'tensor', [(i, (i + 2 * k) % count) for i in range(count)])]
    pallas_call x2 -> x4, Pallas kernels: 6.05 us -> 4.17 us  [the longest x1 2.28 us: on_device(): pl.pallas_call(lambda *refs: tables_kernel(pool, peers, *refs), out_shape...]
    ppermute x6, starting transfers between devices: 10.3 us -> 11.7 us  [on_device(): lax.ppermute(x, 'tensor', [(i, (i + 2 * k) % count) for i in range(count)])]
    all_to_all x1, waiting for transfers between devices: 0.01 us -> 1.31 us  [on_device(): lax.all_to_all(placed.reshape(peers, chunks, CAPACITY, LANES), 'dp', spli...]
    all_to_all x1, waiting for transfers between devices: 1.15 us -> 2.2 us  [on_device(): lax.all_to_all(served.reshape(peers, CAPACITY, LANES), 'dp', split_axis=0...]
  transfers between devices with their start and end apart: 10 -> 10, of which waited for: 5 -> 4; matrix products, arithmetic and copies ran while one was open for 0% -> 0% of each run, Pallas kernels for 19% -> 15%
where the time goes in v7:
time: 47.7 us; the launch traced here: 47.5 us
  starting transfers between devices  31.4 us (66%)
  Pallas kernels  10.1 us (21%)
  waiting for transfers between devices  5.17 us (11%)
  between operations  0.77 us (2%)
    ppermute x6, starting transfers between devices, on_device(): lax.ppermute(x, 'tensor', [(i, (i + 2 * k) % count) for i in range(count)])  11.7 us
    all_to_all x1, starting transfers between devices, on_device(): lax.all_to_all(placed.reshape(peers, chunks, CAPACITY, LANES), 'dp', spli...  10.8 us
    all_to_all x1, starting transfers between devices, on_device(): lax.all_to_all(served.reshape(peers, CAPACITY, LANES), 'dp', split_axis=0...  8.58 us
    pallas_call x1, Pallas kernels, on_device(): pl.pallas_call(lambda *refs: tables_kernel(pool, peers, *refs), out_shape...  2.28 us
    all_to_all x1, waiting for transfers between devices, on_device(): lax.all_to_all(served.reshape(peers, CAPACITY, LANES), 'dp', split_axis=0...  2.2 us
    pallas_call x1, Pallas kernels, on_device(): pl.pallas_call(lambda *refs: cache_kernel(scale, *refs), out_shape=[shape...  1.89 us
    pallas_call x1, Pallas kernels, on_device(): pl.pallas_call(lambda *refs: place_kernel(pool, *refs), out_shape=[shape(...  1.87 us
    all_to_all x1, waiting for transfers between devices, on_device(): lax.all_to_all(placed.reshape(peers, chunks, CAPACITY, LANES), 'dp', spli...  1.31 us
  transfers between devices with their start and end apart: 10, of which 4 were waited for; matrix products, arithmetic and copies ran while one was open for 0% of the time, Pallas kernels for 15%

profile of v7, /device:TPU:2, one launch (start us, length us, event | category | flops | bytes accessed | tf_op | source)
XLA Modules:
  0.0 47.5 jit_solution(9437526479531147443)
XLA Ops:
  0.6 1.9 %place.1 = (bf16[576,128]{1,0:T(8,128)(2,1)}, bf16[32,1024]{1,0:T(8,128)(2,1)S(1)}) custom-call(s32[1,32]{1,0:T(1,128)} %bitcast.15, bf16[32,1024]{1,0:T(8,128)(2,1)} %refs_1_.3), custom_call_target="tpu_custom_call" | custom-call | tf_op jit(solution)/shard_map/place/pallas_call | solution.py:273
  2.5 10.8 %all-to-all-start = ((bf16[32,9,2,128]{3,2,1,0:T(2,128)(2,1)}), bf16[32,9,2,128]{3,2,1,0:T(2,128)(2,1)S(1)}, u32[]{:S(2)}, u32[]{:S(2)}) async-start(bf16[32,9,2,128]{3,2,1,0:T(2,128)(2,1)} %bitcast.1), calls=%async_computation | async-start | bytes 294912 | tf_op jit(solution)/shard_map/rows_to_owners/all_to_all | solution.py:280
  13.3 0.0 copy-start.2
  13.3 1.7 %collective-permute-start.1 = (bf16[32,1024]{1,0:T(8,128)(2,1)S(1)}, bf16[32,1024]{1,0:T(8,128)(2,1)S(1)}, u32[]{:S(2)}, u32[]{:S(2)}) collective-permute-start(bf16[32,1024]{1,0:T(8,128)(2,1)S(1)} %get-tuple-element.22.own_any), channel_id=1, source_target_pairs={{0,2},{1,3},{2,4},{3,5},{4,6},{5,7},{6,0},{7,1},{8,10},{9,11},{10,... | collective-permute-start | bytes 196616 | tf_op jit(solution)/shard_map/gather_hidden/ppermute | solution.py:266
  15.0 2.9 %collective-permute-start.2 = (bf16[32,1024]{1,0:T(8,128)(2,1)S(1)}, bf16[32,1024]{1,0:T(8,128)(2,1)S(1)}, u32[]{:S(2)}, u32[]{:S(2)}) collective-permute-start(bf16[32,1024]{1,0:T(8,128)(2,1)S(1)} %get-tuple-element.22.own_any), channel_id=1, source_target_pairs={{0,4},{1,5},{2,6},{3,7},{4,0},{5,1},{6,2},{7,3},{8,12},{9,13},{10,... | collective-permute-start | bytes 196616 | tf_op jit(solution)/shard_map/gather_hidden/ppermute | solution.py:266
  17.9 1.3 %collective-permute-start.3 = (bf16[32,1024]{1,0:T(8,128)(2,1)S(1)}, bf16[32,1024]{1,0:T(8,128)(2,1)S(1)}, u32[]{:S(2)}, u32[]{:S(2)}) collective-permute-start(bf16[32,1024]{1,0:T(8,128)(2,1)S(1)} %get-tuple-element.22.own_any), channel_id=1, source_target_pairs={{0,6},{1,7},{2,0},{3,1},{4,2},{5,3},{6,4},{7,5},{8,14},{9,15},{10,... | collective-permute-start | bytes 196616 | tf_op jit(solution)/shard_map/gather_hidden/ppermute | solution.py:266
  19.2 1.3 %all-to-all-done = bf16[32,9,2,128]{3,2,1,0:T(2,128)(2,1)S(1)} async-done(((bf16[32,9,2,128]{3,2,1,0:T(2,128)(2,1)}), bf16[32,9,2,128]{3,2,1,0:T(2,128)(2,1)S(1)}, u32[]{:S(2)}, u32[]{:S(2)}) %all-to-all-start) | async-done | bytes 147488 | tf_op jit(solution)/shard_map/rows_to_owners/all_to_all | solution.py:280
  20.5 0.0 copy-done.2
  20.5 1.0 %down.1 = (f32[32,128]{1,0:T(8,128)S(1)}, f32[64,128]{1,0:T(8,128)S(1)}, bf16[1024,128]{1,0:T(8,128)(2,1)S(1)}, bf16[32,1024]{1,0:T(8,128)(2,1)S(1)}, s32[1,32]{1,0:T(1,128)S(1)}) custom-call(bf16[576,128]{1,0:T(8,128)(2,1)S(1)} %bitcast.12, bf16[1024,1024]{1,0:T(8,128)(2,1)S(1)} %bitcast.11, bf16[1024,128]{1,0:T(8,128)(2,1)} %bitcast.14, ...), custom_call_target="tpu_custom_call" | custom-call | tf_op jit(solution)/shard_map/down/pallas_call | solution.py:291
  21.5 0.1 collective-permute-start
  21.6 1.2 %collective-permute-done = f32[32,128]{1,0:T(8,128)S(1)} collective-permute-done((f32[32,128]{1,0:T(8,128)S(1)}, f32[32,128]{1,0:T(8,128)S(1)}, u32[]{:S(2)}, u32[]{:S(2)}) %collective-permute-start) | collective-permute-done | bytes 16416 | tf_op jit(solution)/shard_map/reduce/ppermute | solution.py:265
  22.8 0.0 collective-permute-done.1.y1_any
  22.8 0.0 collective-permute-done.2.y2_any
  22.8 0.0 collective-permute-done.3.y3_any
  22.8 0.4 join.1.after_ref.refs_1_
  23.2 0.0 copy-start
  23.2 0.0 copy-start.1
  23.3 0.2 collective-permute-start.7
  23.5 1.6 %collective-permute-start.4 = (f32[32,128]{1,0:T(8,128)S(1)}, f32[32,128]{1,0:T(8,128)S(1)}, u32[]{:S(2)}, u32[]{:S(2)}) collective-permute-start(f32[32,128]{1,0:T(8,128)S(1)} %add.3.after_ref.refs_0_.a_ref), channel_id=1, source_target_pairs={{0,2},{1,3},{2,4},{3,5},{4,6},{5,7},{6,0},{7,1},{8,10},{9,11},{10,... | collective-permute-start | bytes 49160 | tf_op jit(solution)/shard_map/reduce/ppermute | solution.py:266
  25.1 2.9 %collective-permute-start.5 = (f32[32,128]{1,0:T(8,128)S(1)}, f32[32,128]{1,0:T(8,128)S(1)}, u32[]{:S(2)}, u32[]{:S(2)}) collective-permute-start(f32[32,128]{1,0:T(8,128)S(1)} %add.3.after_ref.refs_0_.a_ref), channel_id=1, source_target_pairs={{0,4},{1,5},{2,6},{3,7},{4,0},{5,1},{6,2},{7,3},{8,12},{9,13},{10,... | collective-permute-start | bytes 49160 | tf_op jit(solution)/shard_map/reduce/ppermute | solution.py:266
  28.0 1.3 %collective-permute-start.6 = (f32[32,128]{1,0:T(8,128)S(1)}, f32[32,128]{1,0:T(8,128)S(1)}, u32[]{:S(2)}, u32[]{:S(2)}) collective-permute-start(f32[32,128]{1,0:T(8,128)S(1)} %add.3.after_ref.refs_0_.a_ref), channel_id=1, source_target_pairs={{0,6},{1,7},{2,0},{3,1},{4,2},{5,3},{6,4},{7,5},{8,14},{9,15},{10,... | collective-permute-start | bytes 49160 | tf_op jit(solution)/shard_map/reduce/ppermute | solution.py:266
  29.3 0.0 copy-done
  29.3 0.0 copy-done.1
  29.3 1.9 %cache.1 = (f32[256,128]{1,0:T(8,128)S(1)}, f32[256,128]{1,0:T(8,128)S(1)}, f32[256,128]{1,0:T(8,128)S(1)}) custom-call(f32[8,128]{1,0:T(8,128)S(1)} %mark2.1.refs_0_, s32[1,32]{1,0:T(1,128)S(1)} %get-tuple-element.23.refs_1_, bf16[32,1024]{1,0:T(8,128)(2,1)S(1)} %get-tuple-element.24.refs_2_.refs_4_, bf16[32,384,128]{2,1,0:T(8,128)(2,1)S(1)} %copy-done, ...), custom_call_target="tpu_custom_call" | custom-call | tf_op jit(solution)/shard_map/cache/pallas_call | solution.py:317
  31.2 0.0 collective-permute-done.4.b_ref
  31.2 0.0 collective-permute-done.5.c_ref
  31.2 0.5 collective-permute-done.6.d_ref
  31.7 0.8 %up.1.refs_0_ = bf16[64,128]{1,0:T(8,128)(2,1)} custom-call(bf16[128,1024]{1,0:T(8,128)(2,1)S(1)} %join.1.after_ref.refs_1_, f32[256,128]{1,0:T(8,128)S(1)} %get-tuple-element.25.after2_ref.refs_7_, f32[32,128]{1,0:T(8,128)S(1)} %add.3.after_ref.refs_0_.a_ref, f32[32,128]{1,0:T(8,128)S(1)} %collective-permute-done.4.b_ref, ...), custom_call_target="tpu_custom_call" | custom-call | tf_op jit(solution)/shard_map/up/pallas_call | solution.py:323
  32.5 8.6 %all-to-all-start.1 = ((bf16[32,2,128]{2,1,0:T(2,128)(2,1)}), bf16[32,2,128]{2,1,0:T(2,128)(2,1)S(1)}, u32[]{:S(2)}, u32[]{:S(2)}) async-start(bf16[32,2,128]{2,1,0:T(2,128)(2,1)} %bitcast.7), calls=%async_computation.1 | async-start | bytes 32768 | tf_op jit(solution)/shard_map/answers/all_to_all | solution.py:328
  41.1 2.3 %tables.1 = (bf16[8192,256]{1,0:T(8,128)(2,1)S(1)}, f32[32,128]{1,0:T(8,128)S(1)}, f32[32,128]{1,0:T(8,128)S(1)}, bf16[32,128]{1,0:T(8,128)(2,1)S(1)}) custom-call(bf16[64,128]{1,0:T(8,128)(2,1)} %up.1.refs_0_, s32[1,32]{1,0:T(1,128)} %bitcast.16, s32[1,32]{1,0:T(1,128)} %bitcast.18, f32[1,128]{1,0:T(1,128)} %constant.6.clone.refs_3_, bf16[8192,256]{1,0:T(8,128)(2,1)} %refs_4_.3), custom_call_target="tpu_custom_call" | custom-call | tf_op jit(solution)/shard_map/tables/pallas_call | solution.py:332
  43.4 0.0 collective-permute-done.7.refs_2_
  43.4 1.0 %late.1 = (f32[32,128]{1,0:T(8,128)S(1)}, bf16[32,128]{1,0:T(8,128)(2,1)S(1)}, f32[256,128]{1,0:T(8,128)S(1)}, f32[256,128]{1,0:T(8,128)S(1)}) custom-call(s32[1]{0:T(128)} %bitcast.9.refs_0_, bf16[128,1024]{1,0:T(8,128)(2,1)S(1)} %join.1.after_ref.refs_1_, bf16[128,1024]{1,0:T(8,128)(2,1)S(1)} %collective-permute-done.7.refs_2_, ...), custom_call_target="tpu_custom_call" | custom-call | flops 134217728 | bytes 4194304 | tf_op jit(solution)/shard_map/late/pallas_call | solution.py:343
  44.5 2.2 %all-to-all-done.1 = bf16[32,2,128]{2,1,0:T(2,128)(2,1)S(1)} async-done(((bf16[32,2,128]{2,1,0:T(2,128)(2,1)}), bf16[32,2,128]{2,1,0:T(2,128)(2,1)S(1)}, u32[]{:S(2)}, u32[]{:S(2)}) %all-to-all-start.1) | async-done | bytes 16416 | tf_op jit(solution)/shard_map/answers/all_to_all | solution.py:328
  46.7 0.8 %finish.1 = (bf16[32,1024]{1,0:T(8,128)(2,1)}, bf16[32,256]{1,0:T(8,128)(2,1)}) custom-call(bf16[64,128]{1,0:T(8,128)(2,1)S(1)} %bitcast.13, bf16[32,128]{1,0:T(8,128)(2,1)S(1)} %get-tuple-element.28.back_ref, f32[32,128]{1,0:T(8,128)S(1)} %get-tuple-element.34.value_ref, bf16[32,128]{1,0:T(8,128)(2,1)S(1)} %get-tuple-element.35.key_ref, ...), custom_call_target="tpu_custom_call" | custom-call | tf_op jit(solution)/shard_map/finish/pallas_call | solution.py:350
  (3 shorter events, 0.0 us)
Async XLA Ops:
  2.5 18.0 %all-to-all-start = ((bf16[32,9,2,128]{3,2,1,0:T(2,128)(2,1)}), bf16[32,9,2,128]{3,2,1,0:T(2,128)(2,1)S(1)}, u32[]{:S(2)}, u32[]{:S(2)}) async-start(bf16[32,9,2,128]{3,2,1,0:T(2,128)(2,1)} %bitcast.1), calls=%async_computation | async-start | bytes 294912 | tf_op jit(solution)/shard_map/rows_to_owners/all_to_all | solution.py:280
  13.3 7.2 %copy-start.2 = (bf16[16,1024,64]{1,2,0:T(8,128)(2,1)S(1)}, bf16[16,1024,64]{1,2,0:T(8,128)(2,1)}, u32[]{:S(2)}) copy-start(bf16[16,1024,64]{1,2,0:T(8,128)(2,1)} %param.17) | copy-start | bytes 6291460
  13.3 9.5 %collective-permute-start.1 = (bf16[32,1024]{1,0:T(8,128)(2,1)S(1)}, bf16[32,1024]{1,0:T(8,128)(2,1)S(1)}, u32[]{:S(2)}, u32[]{:S(2)}) collective-permute-start(bf16[32,1024]{1,0:T(8,128)(2,1)S(1)} %get-tuple-element.22.own_any), channel_id=1, source_target_pairs={{0,2},{1,3},{2,4},{3,5},{4,6},{5,7},{6,0},{7,1},{8,10},{9,11},{10,... | collective-permute-start | bytes 196616 | tf_op jit(solution)/shard_map/gather_hidden/ppermute | solution.py:266
  15.0 7.8 %collective-permute-start.2 = (bf16[32,1024]{1,0:T(8,128)(2,1)S(1)}, bf16[32,1024]{1,0:T(8,128)(2,1)S(1)}, u32[]{:S(2)}, u32[]{:S(2)}) collective-permute-start(bf16[32,1024]{1,0:T(8,128)(2,1)S(1)} %get-tuple-element.22.own_any), channel_id=1, source_target_pairs={{0,4},{1,5},{2,6},{3,7},{4,0},{5,1},{6,2},{7,3},{8,12},{9,13},{10,... | collective-permute-start | bytes 196616 | tf_op jit(solution)/shard_map/gather_hidden/ppermute | solution.py:266
  17.9 5.0 %collective-permute-start.3 = (bf16[32,1024]{1,0:T(8,128)(2,1)S(1)}, bf16[32,1024]{1,0:T(8,128)(2,1)S(1)}, u32[]{:S(2)}, u32[]{:S(2)}) collective-permute-start(bf16[32,1024]{1,0:T(8,128)(2,1)S(1)} %get-tuple-element.22.own_any), channel_id=1, source_target_pairs={{0,6},{1,7},{2,0},{3,1},{4,2},{5,3},{6,4},{7,5},{8,14},{9,15},{10,... | collective-permute-start | bytes 196616 | tf_op jit(solution)/shard_map/gather_hidden/ppermute | solution.py:266
  21.5 1.3 %collective-permute-start = (f32[32,128]{1,0:T(8,128)S(1)}, f32[32,128]{1,0:T(8,128)S(1)}, u32[]{:S(2)}, u32[]{:S(2)}) collective-permute-start(f32[32,128]{1,0:T(8,128)S(1)} %get-tuple-element.21), channel_id=1, source_target_pairs={{0,1},{1,0},{2,3},{3,2},{4,5},{5,4},{6,7},{7,6},{8,9},{9,8},{10,11... | collective-permute-start | bytes 49160 | tf_op jit(solution)/shard_map/reduce/ppermute | solution.py:265
  23.2 6.1 %copy-start = (bf16[32,384,128]{2,1,0:T(8,128)(2,1)S(1)}, bf16[32,384,128]{2,1,0:T(8,128)(2,1)}, u32[]{:S(2)}) copy-start(bf16[32,384,128]{2,1,0:T(8,128)(2,1)} %refs_3_.4) | copy-start | bytes 9437188
  23.2 6.1 %copy-start.1 = (bf16[32,384,128]{2,1,0:T(8,128)(2,1)S(1)}, bf16[32,384,128]{2,1,0:T(8,128)(2,1)}, u32[]{:S(2)}) copy-start(bf16[32,384,128]{2,1,0:T(8,128)(2,1)} %refs_4_.2) | copy-start | bytes 9437188
  23.3 20.2 %collective-permute-start.7 = (bf16[128,1024]{1,0:T(8,128)(2,1)S(1)}, bf16[128,1024]{1,0:T(8,128)(2,1)S(1)}, u32[]{:S(2)}, u32[]{:S(2)}) collective-permute-start(bf16[128,1024]{1,0:T(8,128)(2,1)S(1)} %join.1.after_ref.refs_1_), channel_id=1, source_target_pairs={{0,1},{1,0},{2,3},{3,2},{4,5},{5,4},{6,7},{7,6},{8,9},{9,8},{10,11... | collective-permute-start | bytes 786440 | tf_op jit(solution)/shard_map/gather_core/ppermute | solution.py:265
  23.5 7.7 %collective-permute-start.4 = (f32[32,128]{1,0:T(8,128)S(1)}, f32[32,128]{1,0:T(8,128)S(1)}, u32[]{:S(2)}, u32[]{:S(2)}) collective-permute-start(f32[32,128]{1,0:T(8,128)S(1)} %add.3.after_ref.refs_0_.a_ref), channel_id=1, source_target_pairs={{0,2},{1,3},{2,4},{3,5},{4,6},{5,7},{6,0},{7,1},{8,10},{9,11},{10,... | collective-permute-start | bytes 49160 | tf_op jit(solution)/shard_map/reduce/ppermute | solution.py:266
  25.1 6.2 %collective-permute-start.5 = (f32[32,128]{1,0:T(8,128)S(1)}, f32[32,128]{1,0:T(8,128)S(1)}, u32[]{:S(2)}, u32[]{:S(2)}) collective-permute-start(f32[32,128]{1,0:T(8,128)S(1)} %add.3.after_ref.refs_0_.a_ref), channel_id=1, source_target_pairs={{0,4},{1,5},{2,6},{3,7},{4,0},{5,1},{6,2},{7,3},{8,12},{9,13},{10,... | collective-permute-start | bytes 49160 | tf_op jit(solution)/shard_map/reduce/ppermute | solution.py:266
  28.0 3.7 %collective-permute-start.6 = (f32[32,128]{1,0:T(8,128)S(1)}, f32[32,128]{1,0:T(8,128)S(1)}, u32[]{:S(2)}, u32[]{:S(2)}) collective-permute-start(f32[32,128]{1,0:T(8,128)S(1)} %add.3.after_ref.refs_0_.a_ref), channel_id=1, source_target_pairs={{0,6},{1,7},{2,0},{3,1},{4,2},{5,3},{6,4},{7,5},{8,14},{9,15},{10,... | collective-permute-start | bytes 49160 | tf_op jit(solution)/shard_map/reduce/ppermute | solution.py:266
  32.5 14.1 %all-to-all-start.1 = ((bf16[32,2,128]{2,1,0:T(2,128)(2,1)}), bf16[32,2,128]{2,1,0:T(2,128)(2,1)S(1)}, u32[]{:S(2)}, u32[]{:S(2)}) async-start(bf16[32,2,128]{2,1,0:T(2,128)(2,1)} %bitcast.7), calls=%async_computation.1 | async-start | bytes 32768 | tf_op jit(solution)/shard_map/answers/all_to_all | solution.py:328

commit v8 on v7

--- a/solution.py
+++ b/solution.py
@@ -12,7 +12,8 @@
 LANES = 128
 ROPE_BASE = 500000.0
 MIB = 1 << 20
-TURN = 26
+TURN = 22
+BACK_TURN = 18
 MARKS = 3
 
 F32, BF16, I32 = jnp.float32, jnp.bfloat16, jnp.int32
@@ -132,6 +133,8 @@
 
 
 def up_kernel(after_ref, after2_ref, a_ref, b_ref, c_ref, d_ref, ids_ref, up_ref, out_ref):
+    rows = out_ref.shape[0]
+    head = (BACK_TURN - TURN) * CAPACITY % rows
     total = (a_ref[...] + b_ref[...]) + (c_ref[...] + d_ref[...])
     turned = pltpu.roll(total, 64, 1)
     left = iota(total.shape, 1) < 64
@@ -141,7 +144,10 @@
     spread = [
         jnp.where(ids == right + 2.0 * q, both, 0.0).astype(BF16) for q in range(up_ref.shape[0] // LANES)
     ]
-    out_ref[...] = dot(jnp.concatenate(spread, axis=1), up_ref[...]).astype(BF16)
+    served = dot(jnp.concatenate(spread, axis=1), up_ref[...])
+    if head:
+        served = jnp.concatenate([served[head:], served[:head]], axis=0)
+    out_ref[...] = served.astype(BF16)
 
 
 def cache_kernel(scale, after_ref, length_ref, query_ref, key_ref, value_ref, sum_ref, top_ref, whole_ref):
@@ -185,7 +191,7 @@
     for copy in copies[:3]:
         copy.wait()
     lane = iota((rows, LANES), 1)
-    slot_col = upright(slots_of(tenant_ref[...].astype(F32), pool, peers, TURN))
+    slot_col = upright(slots_of(tenant_ref[...].astype(F32), pool, peers, BACK_TURN))
     back_ref[...] = jnp.where(slot_col == lane.astype(F32), 1.0, 0.0).astype(BF16)
     angle = upright(row_ref[...].astype(F32)) * inverse_ref[...]
     sine = jnp.sin(angle)
@@ -266,6 +272,7 @@
     over_y = lambda x, k: lax.ppermute(x, "tensor", [(i, (i + 2 * k) % count) for i in range(count)])
 
     ring = [[(k + TURN) % peers for k in range(peers)]]
+    back_ring = [[(k + BACK_TURN) % peers for k in range(peers)]]
     inverse = ROPE_BASE ** (-(np.arange(HEAD_SIZE // 2, dtype=np.float32) * 2.0) / HEAD_SIZE)
     inverse = jnp.asarray(np.concatenate([inverse, inverse])[None, :], F32)
 
@@ -326,7 +333,7 @@
         )(near, states[0], pair_sum, *sums_y, ids, up_near)
     with jax.named_scope("answers"):
         returned = lax.all_to_all(
-            served.reshape(peers, CAPACITY, LANES), "dp", split_axis=0, concat_axis=0, tiled=True, axis_index_groups=ring
+            served.reshape(peers, CAPACITY, LANES), "dp", split_axis=0, concat_axis=0, tiled=True, axis_index_groups=back_ring
         ).reshape(slots, LANES)
     with jax.named_scope("tables"):
         weight_near, cosine, sine, back = pl.pallas_call(

time: 47.7 us -> 46.7 us (0.979)
  waiting for transfers between devices: 5.17 us -> 2.81 us
  starting transfers between devices: 31.4 us -> 32.5 us
    all_to_all x1, waiting for transfers between devices: 2.2 us -> 0.42 us  [on_device(): lax.all_to_all(served.reshape(peers, CAPACITY, LANES), 'dp', split_axis=0...]
    all_to_all x1, waiting for transfers between devices: 1.31 us -> 0.73 us  [on_device(): lax.all_to_all(placed.reshape(peers, chunks, CAPACITY, LANES), 'dp', spli...]
    all_to_all x1, starting transfers between devices: 8.58 us -> 9.12 us  [on_device(): lax.all_to_all(served.reshape(peers, CAPACITY, LANES), 'dp', split_axis=0...]
where the time goes in v8:
time: 46.7 us; the launch traced here: 46.1 us
  starting transfers between devices  32.5 us (70%)
  Pallas kernels  10.1 us (22%)
  waiting for transfers between devices  2.81 us (6%)
  between operations  0.77 us (2%)
    ppermute x6, starting transfers between devices, on_device(): lax.ppermute(x, 'tensor', [(i, (i + 2 * k) % count) for i in range(count)])  11.7 us
    all_to_all x1, starting transfers between devices, on_device(): lax.all_to_all(placed.reshape(peers, chunks, CAPACITY, LANES), 'dp', spli...  11.3 us
    all_to_all x1, starting transfers between devices, on_device(): lax.all_to_all(served.reshape(peers, CAPACITY, LANES), 'dp', split_axis=0...  9.12 us
    pallas_call x1, Pallas kernels, on_device(): pl.pallas_call(lambda *refs: tables_kernel(pool, peers, *refs), out_shape...  2.28 us
    pallas_call x1, Pallas kernels, on_device(): pl.pallas_call(lambda *refs: cache_kernel(scale, *refs), out_shape=[shape...  1.89 us
    pallas_call x1, Pallas kernels, on_device(): pl.pallas_call(lambda *refs: place_kernel(pool, *refs), out_shape=[shape(...  1.87 us
    ppermute x2, waiting for transfers between devices, on_device(): lax.ppermute(x, 'tensor', [(i, i ^ 1) for i in range(count)])  1.17 us
    pallas_call x1, Pallas kernels, on_device(): pl.pallas_call(lambda *refs: late_kernel(scale, *refs), out_shape=[shape(...  1.04 us
  transfers between devices with their start and end apart: 10, of which 4 were waited for; matrix products, arithmetic and copies ran while one was open for 0% of the time, Pallas kernels for 15%

profile of v8, /device:TPU:2, one launch (start us, length us, event | category | flops | bytes accessed | tf_op | source)
XLA Modules:
  0.0 46.1 jit_solution(2720568739502621984)
XLA Ops:
  0.6 1.9 %place.1 = (bf16[576,128]{1,0:T(8,128)(2,1)}, bf16[32,1024]{1,0:T(8,128)(2,1)S(1)}) custom-call(s32[1,32]{1,0:T(1,128)} %bitcast.15, bf16[32,1024]{1,0:T(8,128)(2,1)} %refs_1_.3), custom_call_target="tpu_custom_call" | custom-call | tf_op jit(solution)/shard_map/place/pallas_call | solution.py:280
  2.5 11.3 %all-to-all-start = ((bf16[32,9,2,128]{3,2,1,0:T(2,128)(2,1)}), bf16[32,9,2,128]{3,2,1,0:T(2,128)(2,1)S(1)}, u32[]{:S(2)}, u32[]{:S(2)}) async-start(bf16[32,9,2,128]{3,2,1,0:T(2,128)(2,1)} %bitcast.1), calls=%async_computation | async-start | bytes 294912 | tf_op jit(solution)/shard_map/rows_to_owners/all_to_all | solution.py:287
  13.8 0.0 copy-start.2
  13.8 1.7 %collective-permute-start.1 = (bf16[32,1024]{1,0:T(8,128)(2,1)S(1)}, bf16[32,1024]{1,0:T(8,128)(2,1)S(1)}, u32[]{:S(2)}, u32[]{:S(2)}) collective-permute-start(bf16[32,1024]{1,0:T(8,128)(2,1)S(1)} %get-tuple-element.22.own_any), channel_id=1, source_target_pairs={{0,2},{1,3},{2,4},{3,5},{4,6},{5,7},{6,0},{7,1},{8,10},{9,11},{10,... | collective-permute-start | bytes 196616 | tf_op jit(solution)/shard_map/gather_hidden/ppermute | solution.py:272
  15.4 2.9 %collective-permute-start.2 = (bf16[32,1024]{1,0:T(8,128)(2,1)S(1)}, bf16[32,1024]{1,0:T(8,128)(2,1)S(1)}, u32[]{:S(2)}, u32[]{:S(2)}) collective-permute-start(bf16[32,1024]{1,0:T(8,128)(2,1)S(1)} %get-tuple-element.22.own_any), channel_id=1, source_target_pairs={{0,4},{1,5},{2,6},{3,7},{4,0},{5,1},{6,2},{7,3},{8,12},{9,13},{10,... | collective-permute-start | bytes 196616 | tf_op jit(solution)/shard_map/gather_hidden/ppermute | solution.py:272
  18.3 1.3 %collective-permute-start.3 = (bf16[32,1024]{1,0:T(8,128)(2,1)S(1)}, bf16[32,1024]{1,0:T(8,128)(2,1)S(1)}, u32[]{:S(2)}, u32[]{:S(2)}) collective-permute-start(bf16[32,1024]{1,0:T(8,128)(2,1)S(1)} %get-tuple-element.22.own_any), channel_id=1, source_target_pairs={{0,6},{1,7},{2,0},{3,1},{4,2},{5,3},{6,4},{7,5},{8,14},{9,15},{10,... | collective-permute-start | bytes 196616 | tf_op jit(solution)/shard_map/gather_hidden/ppermute | solution.py:272
  19.7 0.7 %all-to-all-done = bf16[32,9,2,128]{3,2,1,0:T(2,128)(2,1)S(1)} async-done(((bf16[32,9,2,128]{3,2,1,0:T(2,128)(2,1)}), bf16[32,9,2,128]{3,2,1,0:T(2,128)(2,1)S(1)}, u32[]{:S(2)}, u32[]{:S(2)}) %all-to-all-start) | async-done | bytes 147488 | tf_op jit(solution)/shard_map/rows_to_owners/all_to_all | solution.py:287
  20.4 0.0 copy-done.2
  20.4 1.0 %down.1 = (f32[32,128]{1,0:T(8,128)S(1)}, f32[64,128]{1,0:T(8,128)S(1)}, bf16[1024,128]{1,0:T(8,128)(2,1)S(1)}, bf16[32,1024]{1,0:T(8,128)(2,1)S(1)}, s32[1,32]{1,0:T(1,128)S(1)}) custom-call(bf16[576,128]{1,0:T(8,128)(2,1)S(1)} %bitcast.12, bf16[1024,1024]{1,0:T(8,128)(2,1)S(1)} %bitcast.11, bf16[1024,128]{1,0:T(8,128)(2,1)} %bitcast.14, ...), custom_call_target="tpu_custom_call" | custom-call | tf_op jit(solution)/shard_map/down/pallas_call | solution.py:298
  21.4 0.1 collective-permute-start
  21.5 1.2 %collective-permute-done = f32[32,128]{1,0:T(8,128)S(1)} collective-permute-done((f32[32,128]{1,0:T(8,128)S(1)}, f32[32,128]{1,0:T(8,128)S(1)}, u32[]{:S(2)}, u32[]{:S(2)}) %collective-permute-start) | collective-permute-done | bytes 16416 | tf_op jit(solution)/shard_map/reduce/ppermute | solution.py:271
  22.7 0.0 collective-permute-done.1.y1_any
  22.7 0.0 collective-permute-done.2.y2_any
  22.7 0.0 collective-permute-done.3.y3_any
  22.7 0.4 join.1.after_ref.refs_1_
  23.1 0.0 copy-start
  23.1 0.0 copy-start.1
  23.1 0.2 collective-permute-start.7
  23.4 1.6 %collective-permute-start.4 = (f32[32,128]{1,0:T(8,128)S(1)}, f32[32,128]{1,0:T(8,128)S(1)}, u32[]{:S(2)}, u32[]{:S(2)}) collective-permute-start(f32[32,128]{1,0:T(8,128)S(1)} %add.3.after_ref.refs_0_.a_ref), channel_id=1, source_target_pairs={{0,2},{1,3},{2,4},{3,5},{4,6},{5,7},{6,0},{7,1},{8,10},{9,11},{10,... | collective-permute-start | bytes 49160 | tf_op jit(solution)/shard_map/reduce/ppermute | solution.py:272
  25.0 2.9 %collective-permute-start.5 = (f32[32,128]{1,0:T(8,128)S(1)}, f32[32,128]{1,0:T(8,128)S(1)}, u32[]{:S(2)}, u32[]{:S(2)}) collective-permute-start(f32[32,128]{1,0:T(8,128)S(1)} %add.3.after_ref.refs_0_.a_ref), channel_id=1, source_target_pairs={{0,4},{1,5},{2,6},{3,7},{4,0},{5,1},{6,2},{7,3},{8,12},{9,13},{10,... | collective-permute-start | bytes 49160 | tf_op jit(solution)/shard_map/reduce/ppermute | solution.py:272
  27.9 1.3 %collective-permute-start.6 = (f32[32,128]{1,0:T(8,128)S(1)}, f32[32,128]{1,0:T(8,128)S(1)}, u32[]{:S(2)}, u32[]{:S(2)}) collective-permute-start(f32[32,128]{1,0:T(8,128)S(1)} %add.3.after_ref.refs_0_.a_ref), channel_id=1, source_target_pairs={{0,6},{1,7},{2,0},{3,1},{4,2},{5,3},{6,4},{7,5},{8,14},{9,15},{10,... | collective-permute-start | bytes 49160 | tf_op jit(solution)/shard_map/reduce/ppermute | solution.py:272
  29.2 0.0 copy-done
  29.2 0.0 copy-done.1
  29.2 1.9 %cache.1 = (f32[256,128]{1,0:T(8,128)S(1)}, f32[256,128]{1,0:T(8,128)S(1)}, f32[256,128]{1,0:T(8,128)S(1)}) custom-call(f32[8,128]{1,0:T(8,128)S(1)} %mark2.1.refs_0_, s32[1,32]{1,0:T(1,128)S(1)} %get-tuple-element.23.refs_1_, bf16[32,1024]{1,0:T(8,128)(2,1)S(1)} %get-tuple-element.24.refs_2_.refs_4_, bf16[32,384,128]{2,1,0:T(8,128)(2,1)S(1)} %copy-done, ...), custom_call_target="tpu_custom_call" | custom-call | tf_op jit(solution)/shard_map/cache/pallas_call | solution.py:324
  31.1 0.0 collective-permute-done.4.b_ref
  31.1 0.0 collective-permute-done.5.c_ref
  31.1 0.5 %collective-permute-done.6.d_ref = f32[32,128]{1,0:T(8,128)S(1)} collective-permute-done((f32[32,128]{1,0:T(8,128)S(1)}, f32[32,128]{1,0:T(8,128)S(1)}, u32[]{:S(2)}, u32[]{:S(2)}) %collective-permute-start.6) | collective-permute-done | bytes 16416 | tf_op jit(solution)/shard_map/reduce/ppermute | solution.py:272
  31.6 0.8 %up.1.refs_0_ = bf16[64,128]{1,0:T(8,128)(2,1)} custom-call(bf16[128,1024]{1,0:T(8,128)(2,1)S(1)} %join.1.after_ref.refs_1_, f32[256,128]{1,0:T(8,128)S(1)} %get-tuple-element.25.after2_ref.refs_7_, f32[32,128]{1,0:T(8,128)S(1)} %add.3.after_ref.refs_0_.a_ref, f32[32,128]{1,0:T(8,128)S(1)} %collective-permute-done.4.b_ref, ...), custom_call_target="tpu_custom_call" | custom-call | tf_op jit(solution)/shard_map/up/pallas_call | solution.py:330
  32.4 9.1 %all-to-all-start.1 = ((bf16[32,2,128]{2,1,0:T(2,128)(2,1)}), bf16[32,2,128]{2,1,0:T(2,128)(2,1)S(1)}, u32[]{:S(2)}, u32[]{:S(2)}) async-start(bf16[32,2,128]{2,1,0:T(2,128)(2,1)} %bitcast.7), calls=%async_computation.1 | async-start | bytes 32768 | tf_op jit(solution)/shard_map/answers/all_to_all | solution.py:335
  41.6 2.3 %tables.1 = (bf16[8192,256]{1,0:T(8,128)(2,1)S(1)}, f32[32,128]{1,0:T(8,128)S(1)}, f32[32,128]{1,0:T(8,128)S(1)}, bf16[32,128]{1,0:T(8,128)(2,1)S(1)}) custom-call(bf16[64,128]{1,0:T(8,128)(2,1)} %up.1.refs_0_, s32[1,32]{1,0:T(1,128)} %bitcast.16, s32[1,32]{1,0:T(1,128)} %bitcast.18, f32[1,128]{1,0:T(1,128)} %constant.6.clone.refs_3_, bf16[8192,256]{1,0:T(8,128)(2,1)} %refs_4_.3), custom_call_target="tpu_custom_call" | custom-call | tf_op jit(solution)/shard_map/tables/pallas_call | solution.py:339
  43.9 0.0 collective-permute-done.7.refs_2_
  43.9 1.0 %late.1 = (f32[32,128]{1,0:T(8,128)S(1)}, bf16[32,128]{1,0:T(8,128)(2,1)S(1)}, f32[256,128]{1,0:T(8,128)S(1)}, f32[256,128]{1,0:T(8,128)S(1)}) custom-call(s32[1]{0:T(128)} %bitcast.9.refs_0_, bf16[128,1024]{1,0:T(8,128)(2,1)S(1)} %join.1.after_ref.refs_1_, bf16[128,1024]{1,0:T(8,128)(2,1)S(1)} %collective-permute-done.7.refs_2_, ...), custom_call_target="tpu_custom_call" | custom-call | flops 134217728 | bytes 4194304 | tf_op jit(solution)/shard_map/late/pallas_call | solution.py:350
  44.9 0.4 all-to-all-done.1
  45.3 0.8 %finish.1 = (bf16[32,1024]{1,0:T(8,128)(2,1)}, bf16[32,256]{1,0:T(8,128)(2,1)}) custom-call(bf16[64,128]{1,0:T(8,128)(2,1)S(1)} %bitcast.13, bf16[32,128]{1,0:T(8,128)(2,1)S(1)} %get-tuple-element.28.back_ref, f32[32,128]{1,0:T(8,128)S(1)} %get-tuple-element.34.value_ref, bf16[32,128]{1,0:T(8,128)(2,1)S(1)} %get-tuple-element.35.key_ref, ...), custom_call_target="tpu_custom_call" | custom-call | tf_op jit(solution)/shard_map/finish/pallas_call | solution.py:357
  (3 shorter events, 0.0 us)
Async XLA Ops:
  2.5 17.9 %all-to-all-start = ((bf16[32,9,2,128]{3,2,1,0:T(2,128)(2,1)}), bf16[32,9,2,128]{3,2,1,0:T(2,128)(2,1)S(1)}, u32[]{:S(2)}, u32[]{:S(2)}) async-start(bf16[32,9,2,128]{3,2,1,0:T(2,128)(2,1)} %bitcast.1), calls=%async_computation | async-start | bytes 294912 | tf_op jit(solution)/shard_map/rows_to_owners/all_to_all | solution.py:287
  13.8 6.7 %copy-start.2 = (bf16[16,1024,64]{1,2,0:T(8,128)(2,1)S(1)}, bf16[16,1024,64]{1,2,0:T(8,128)(2,1)}, u32[]{:S(2)}) copy-start(bf16[16,1024,64]{1,2,0:T(8,128)(2,1)} %param.17) | copy-start | bytes 6291460
  13.8 8.9 %collective-permute-start.1 = (bf16[32,1024]{1,0:T(8,128)(2,1)S(1)}, bf16[32,1024]{1,0:T(8,128)(2,1)S(1)}, u32[]{:S(2)}, u32[]{:S(2)}) collective-permute-start(bf16[32,1024]{1,0:T(8,128)(2,1)S(1)} %get-tuple-element.22.own_any), channel_id=1, source_target_pairs={{0,2},{1,3},{2,4},{3,5},{4,6},{5,7},{6,0},{7,1},{8,10},{9,11},{10,... | collective-permute-start | bytes 196616 | tf_op jit(solution)/shard_map/gather_hidden/ppermute | solution.py:272
  15.4 7.3 %collective-permute-start.2 = (bf16[32,1024]{1,0:T(8,128)(2,1)S(1)}, bf16[32,1024]{1,0:T(8,128)(2,1)S(1)}, u32[]{:S(2)}, u32[]{:S(2)}) collective-permute-start(bf16[32,1024]{1,0:T(8,128)(2,1)S(1)} %get-tuple-element.22.own_any), channel_id=1, source_target_pairs={{0,4},{1,5},{2,6},{3,7},{4,0},{5,1},{6,2},{7,3},{8,12},{9,13},{10,... | collective-permute-start | bytes 196616 | tf_op jit(solution)/shard_map/gather_hidden/ppermute | solution.py:272
  18.3 4.4 %collective-permute-start.3 = (bf16[32,1024]{1,0:T(8,128)(2,1)S(1)}, bf16[32,1024]{1,0:T(8,128)(2,1)S(1)}, u32[]{:S(2)}, u32[]{:S(2)}) collective-permute-start(bf16[32,1024]{1,0:T(8,128)(2,1)S(1)} %get-tuple-element.22.own_any), channel_id=1, source_target_pairs={{0,6},{1,7},{2,0},{3,1},{4,2},{5,3},{6,4},{7,5},{8,14},{9,15},{10,... | collective-permute-start | bytes 196616 | tf_op jit(solution)/shard_map/gather_hidden/ppermute | solution.py:272
  21.4 1.3 %collective-permute-start = (f32[32,128]{1,0:T(8,128)S(1)}, f32[32,128]{1,0:T(8,128)S(1)}, u32[]{:S(2)}, u32[]{:S(2)}) collective-permute-start(f32[32,128]{1,0:T(8,128)S(1)} %get-tuple-element.21), channel_id=1, source_target_pairs={{0,1},{1,0},{2,3},{3,2},{4,5},{5,4},{6,7},{7,6},{8,9},{9,8},{10,11... | collective-permute-start | bytes 49160 | tf_op jit(solution)/shard_map/reduce/ppermute | solution.py:271
  23.1 6.1 %copy-start = (bf16[32,384,128]{2,1,0:T(8,128)(2,1)S(1)}, bf16[32,384,128]{2,1,0:T(8,128)(2,1)}, u32[]{:S(2)}) copy-start(bf16[32,384,128]{2,1,0:T(8,128)(2,1)} %refs_3_.4) | copy-start | bytes 9437188
  23.1 6.1 %copy-start.1 = (bf16[32,384,128]{2,1,0:T(8,128)(2,1)S(1)}, bf16[32,384,128]{2,1,0:T(8,128)(2,1)}, u32[]{:S(2)}) copy-start(bf16[32,384,128]{2,1,0:T(8,128)(2,1)} %refs_4_.2) | copy-start | bytes 9437188
  23.1 20.7 %collective-permute-start.7 = (bf16[128,1024]{1,0:T(8,128)(2,1)S(1)}, bf16[128,1024]{1,0:T(8,128)(2,1)S(1)}, u32[]{:S(2)}, u32[]{:S(2)}) collective-permute-start(bf16[128,1024]{1,0:T(8,128)(2,1)S(1)} %join.1.after_ref.refs_1_), channel_id=1, source_target_pairs={{0,1},{1,0},{2,3},{3,2},{4,5},{5,4},{6,7},{7,6},{8,9},{9,8},{10,11... | collective-permute-start | bytes 786440 | tf_op jit(solution)/shard_map/gather_core/ppermute | solution.py:271
  23.4 7.7 %collective-permute-start.4 = (f32[32,128]{1,0:T(8,128)S(1)}, f32[32,128]{1,0:T(8,128)S(1)}, u32[]{:S(2)}, u32[]{:S(2)}) collective-permute-start(f32[32,128]{1,0:T(8,128)S(1)} %add.3.after_ref.refs_0_.a_ref), channel_id=1, source_target_pairs={{0,2},{1,3},{2,4},{3,5},{4,6},{5,7},{6,0},{7,1},{8,10},{9,11},{10,... | collective-permute-start | bytes 49160 | tf_op jit(solution)/shard_map/reduce/ppermute | solution.py:272
  25.0 6.2 %collective-permute-start.5 = (f32[32,128]{1,0:T(8,128)S(1)}, f32[32,128]{1,0:T(8,128)S(1)}, u32[]{:S(2)}, u32[]{:S(2)}) collective-permute-start(f32[32,128]{1,0:T(8,128)S(1)} %add.3.after_ref.refs_0_.a_ref), channel_id=1, source_target_pairs={{0,4},{1,5},{2,6},{3,7},{4,0},{5,1},{6,2},{7,3},{8,12},{9,13},{10,... | collective-permute-start | bytes 49160 | tf_op jit(solution)/shard_map/reduce/ppermute | solution.py:272
  27.9 3.7 %collective-permute-start.6 = (f32[32,128]{1,0:T(8,128)S(1)}, f32[32,128]{1,0:T(8,128)S(1)}, u32[]{:S(2)}, u32[]{:S(2)}) collective-permute-start(f32[32,128]{1,0:T(8,128)S(1)} %add.3.after_ref.refs_0_.a_ref), channel_id=1, source_target_pairs={{0,6},{1,7},{2,0},{3,1},{4,2},{5,3},{6,4},{7,5},{8,14},{9,15},{10,... | collective-permute-start | bytes 49160 | tf_op jit(solution)/shard_map/reduce/ppermute | solution.py:272
  32.4 12.9 %all-to-all-start.1 = ((bf16[32,2,128]{2,1,0:T(2,128)(2,1)}), bf16[32,2,128]{2,1,0:T(2,128)(2,1)S(1)}, u32[]{:S(2)}, u32[]{:S(2)}) async-start(bf16[32,2,128]{2,1,0:T(2,128)(2,1)} %bitcast.7), calls=%async_computation.1 | async-start | bytes 32768 | tf_op jit(solution)/shard_map/answers/all_to_all | solution.py:335

commit v9 on v8

--- a/solution.py
+++ b/solution.py
@@ -15,6 +15,7 @@
 TURN = 22
 BACK_TURN = 18
 MARKS = 3
+AHEAD_CHIPS = 2
 
 F32, BF16, I32 = jnp.float32, jnp.bfloat16, jnp.int32
 VMEM = pl.BlockSpec(memory_space=pltpu.VMEM)
@@ -150,7 +151,10 @@
     out_ref[...] = served.astype(BF16)
 
 
-def cache_kernel(scale, after_ref, length_ref, query_ref, key_ref, value_ref, sum_ref, top_ref, whole_ref):
+def cache_kernel(scale, after_ref, length_ref, query_ref, key_ref, value_ref, weight_hbm, sum_ref, top_ref, whole_ref,
+                 weight_ref, sem):
+    fetch_weight = pltpu.make_async_copy(weight_hbm.at[pl.ds(0, weight_ref.shape[0])], weight_ref, sem)
+    fetch_weight.start()
     rows, length = key_ref.shape[0], key_ref.shape[1]
     wide = rows * GROUP
     by_head = jnp.concatenate([query_ref[:, h * LANES : (h + 1) * LANES] for h in range(GROUP)], axis=0)
@@ -175,6 +179,7 @@
         sum_ref[place, :] = dot(weights[some].astype(BF16), value_ref[r])
         top_ref[place, :] = top[some]
         whole_ref[place, :] = whole[some]
+    fetch_weight.wait()
 
 
 def mark_kernel(*refs):
@@ -186,7 +191,11 @@
                   back_ref, tenant_ref, row_ref, inverse_ref, sems):
     rows = back_ref.shape[0]
     copies = fetches(
-        [(tenant_hbm, tenant_ref), (row_hbm, row_ref), (inverse_hbm, inverse_ref), (weight_hbm, weight_ref)], sems
+        [
+            (tenant_hbm, tenant_ref), (row_hbm, row_ref), (inverse_hbm, inverse_ref),
+            (weight_hbm.at[pl.ds(weight_hbm.shape[0] - weight_ref.shape[0], weight_ref.shape[0])], weight_ref),
+        ],
+        sems,
     )
     for copy in copies[:3]:
         copy.wait()
@@ -207,21 +216,20 @@
         copy.wait()
 
 
-def late_kernel(scale, index_ref, near_ref, far_ref, weight_ref, query_ref, cosine_ref, sine_ref, sum_ref, top_ref,
+def late_kernel(scale, index_ref, near_ref, far_ref, first_ref, second_ref, query_ref, cosine_ref, sine_ref, sum_ref, top_ref,
                 whole_ref, projected_ref, entry_ref, mixed_ref, share_ref):
     rows, depth = query_ref.shape[0], near_ref.shape[1]
     me = index_ref[0]
-    devices = weight_ref.shape[0] // depth
-
-    def part(block, other):
-        start = pl.multiple_of(other * depth, depth)
-        return dot(block, weight_ref[pl.ds(start, depth), :])
-
+    chips = near_ref.shape[0] // rows
+    mine, core = me // 2, me % 2
+    split = first_ref.shape[0] // (2 * depth)
     total = jnp.zeros((rows, 2 * LANES), F32)
-    for shift in range(devices // 2):
-        other = (me + devices - 2 * shift) % devices
-        block = slice(shift * rows, (shift + 1) * rows)
-        total += part(near_ref[block], other) + part(far_ref[block], other ^ 1)
+    for chip in range(chips):
+        place = pl.ds(pl.multiple_of((mine + chips - chip) % chips * rows, rows), rows)
+        weight_ref, base = (first_ref, chip) if chip < split else (second_ref, chip - split)
+        for block_ref, half in ((near_ref, core), (far_ref, 1 - core)):
+            start = pl.multiple_of((2 * base + half) * depth, depth)
+            total += dot(block_ref[place, :], weight_ref[pl.ds(start, depth), :])
     projected_ref[...] = total[:, LANES:]
     key = total[:, :LANES]
     key = (key * cosine_ref[...] + pltpu.roll(key, 64, 1) * sine_ref[...]).astype(BF16)
@@ -271,6 +279,7 @@
     over_core = lambda x: lax.ppermute(x, "tensor", [(i, i ^ 1) for i in range(count)])
     over_y = lambda x, k: lax.ppermute(x, "tensor", [(i, (i + 2 * k) % count) for i in range(count)])
 
+    ahead = AHEAD_CHIPS * 2 * depth
     ring = [[(k + TURN) % peers for k in range(peers)]]
     back_ring = [[(k + BACK_TURN) % peers for k in range(peers)]]
     inverse = ROPE_BASE ** (-(np.arange(HEAD_SIZE // 2, dtype=np.float32) * 2.0) / HEAD_SIZE)
@@ -321,11 +330,12 @@
             compiler_params=params(2),
         )(pair_sum, *far(key_cache, value_cache, weight)[:MARKS])
     with jax.named_scope("cache"):
-        states = pl.pallas_call(
+        *states, weight_first = pl.pallas_call(
             lambda *refs: cache_kernel(scale, *refs),
-            out_shape=[shape((GROUP * rows, LANES), F32)] * 3,
-            in_specs=[ANY] + [VMEM] * 4, out_specs=[VMEM] * 3, compiler_params=params(8),
-        )(mark, length_near, queries_near, key_cache, value_cache)
+            out_shape=[shape((GROUP * rows, LANES), F32)] * 3 + [shape((ahead, 2 * LANES), BF16)],
+            in_specs=[ANY] + [VMEM] * 4 + [HBM], out_specs=[VMEM] * 4, compiler_params=params(8),
+            scratch_shapes=[dma],
+        )(mark, length_near, queries_near, key_cache, value_cache, *far(weight))
     with jax.named_scope("up"):
         served = pl.pallas_call(
             up_kernel, out_shape=shape((slots, LANES), BF16),
@@ -336,10 +346,10 @@
             served.reshape(peers, CAPACITY, LANES), "dp", split_axis=0, concat_axis=0, tiled=True, axis_index_groups=back_ring
         ).reshape(slots, LANES)
     with jax.named_scope("tables"):
-        weight_near, cosine, sine, back = pl.pallas_call(
+        weight_second, cosine, sine, back = pl.pallas_call(
             lambda *refs: tables_kernel(pool, peers, *refs),
             out_shape=[
-                shape(weight.shape, BF16), shape((rows, LANES), F32), shape((rows, LANES), F32),
+                shape((count * depth - ahead, 2 * LANES), BF16), shape((rows, LANES), F32), shape((rows, LANES), F32),
                 shape((rows, LANES), BF16),
             ],
             in_specs=[ANY] + [HBM] * 4, out_specs=[VMEM] * 4,
@@ -350,9 +360,9 @@
         value, key, mixed, share = pl.pallas_call(
             lambda *refs: late_kernel(scale, *refs),
             out_shape=[shape((rows, LANES), F32), shape((rows, LANES), BF16)] + [shape((GROUP * rows, LANES), F32)] * 2,
-            in_specs=[SMEM] + [VMEM] * 9, out_specs=[VMEM] * 4, compiler_params=params(8),
+            in_specs=[SMEM] + [VMEM] * 10, out_specs=[VMEM] * 4, compiler_params=params(8),
             cost_estimate=cost(2 * rows * count * depth * 2 * LANES, weight.size * 2),
-        )(me, near, other, weight_near, queries_near, cosine, sine, *states)
+        )(me, near, other, weight_first, weight_second, queries_near, cosine, sine, *states)
     with jax.named_scope("finish"):
         return tuple(pl.pallas_call(
             final_kernel,

time: 46.7 us -> 46.4 us (level)
  Pallas kernels: 10.1 us -> 9.52 us
  waiting for transfers between devices: 2.81 us -> 3.34 us
    pallas_call x1, Pallas kernels: 2.28 us -> 1.68 us  [on_device(): pl.pallas_call(lambda *refs: tables_kernel(pool, peers, *refs), out_shape...]
    all_to_all x1, waiting for transfers between devices: 0.42 us -> 0.99 us  [on_device(): lax.all_to_all(served.reshape(peers, CAPACITY, LANES), 'dp', split_axis=0...]
  transfers between devices with their start and end apart: 10 -> 10, of which waited for: 4 -> 4; matrix products, arithmetic and copies ran while one was open for 0% -> 0% of each run, Pallas kernels for 15% -> 14%
where the time goes in v9:
time: 46.4 us; the launch traced here: 46.1 us
  starting transfers between devices  32.5 us (70%)
  Pallas kernels  9.52 us (21%)
  waiting for transfers between devices  3.34 us (7%)
  between operations  0.78 us (2%)
    ppermute x6, starting transfers between devices, on_device(): lax.ppermute(x, 'tensor', [(i, (i + 2 * k) % count) for i in range(count)])  11.7 us
    all_to_all x1, starting transfers between devices, on_device(): lax.all_to_all(placed.reshape(peers, chunks, CAPACITY, LANES), 'dp', spli...  11.3 us
    all_to_all x1, starting transfers between devices, on_device(): lax.all_to_all(served.reshape(peers, CAPACITY, LANES), 'dp', split_axis=0...  9.12 us
    pallas_call x1, Pallas kernels, on_device(): pl.pallas_call(lambda *refs: cache_kernel(scale, *refs), out_shape=[shape...  1.92 us
    pallas_call x1, Pallas kernels, on_device(): pl.pallas_call(lambda *refs: place_kernel(pool, *refs), out_shape=[shape(...  1.87 us
    pallas_call x1, Pallas kernels, on_device(): pl.pallas_call(lambda *refs: tables_kernel(pool, peers, *refs), out_shape...  1.68 us
    ppermute x2, waiting for transfers between devices, on_device(): lax.ppermute(x, 'tensor', [(i, i ^ 1) for i in range(count)])  1.17 us
    pallas_call x1, Pallas kernels, on_device(): pl.pallas_call(lambda *refs: late_kernel(scale, *refs), out_shape=[shape(...  1.07 us
  transfers between devices with their start and end apart: 10, of which 4 were waited for; matrix products, arithmetic and copies ran while one was open for 0% of the time, Pallas kernels for 14%

profile of v9, /device:TPU:2, one launch (start us, length us, event | category | flops | bytes accessed | tf_op | source)
XLA Modules:
  0.0 46.1 jit_solution(478698691330271482)
XLA Ops:
  0.6 1.9 %place.1 = (bf16[576,128]{1,0:T(8,128)(2,1)}, bf16[32,1024]{1,0:T(8,128)(2,1)S(1)}) custom-call(s32[1,32]{1,0:T(1,128)} %bitcast.15, bf16[32,1024]{1,0:T(8,128)(2,1)} %refs_1_.3), custom_call_target="tpu_custom_call" | custom-call | tf_op jit(solution)/shard_map/place/pallas_call | solution.py:289
  2.5 11.3 %all-to-all-start = ((bf16[32,9,2,128]{3,2,1,0:T(2,128)(2,1)}), bf16[32,9,2,128]{3,2,1,0:T(2,128)(2,1)S(1)}, u32[]{:S(2)}, u32[]{:S(2)}) async-start(bf16[32,9,2,128]{3,2,1,0:T(2,128)(2,1)} %bitcast.1), calls=%async_computation | async-start | bytes 294912 | tf_op jit(solution)/shard_map/rows_to_owners/all_to_all | solution.py:296
  13.8 0.0 copy-start.2
  13.8 1.7 %collective-permute-start.1 = (bf16[32,1024]{1,0:T(8,128)(2,1)S(1)}, bf16[32,1024]{1,0:T(8,128)(2,1)S(1)}, u32[]{:S(2)}, u32[]{:S(2)}) collective-permute-start(bf16[32,1024]{1,0:T(8,128)(2,1)S(1)} %get-tuple-element.23.own_any), channel_id=1, source_target_pairs={{0,2},{1,3},{2,4},{3,5},{4,6},{5,7},{6,0},{7,1},{8,10},{9,11},{10,... | collective-permute-start | bytes 196616 | tf_op jit(solution)/shard_map/gather_hidden/ppermute | solution.py:280
  15.4 2.9 %collective-permute-start.2 = (bf16[32,1024]{1,0:T(8,128)(2,1)S(1)}, bf16[32,1024]{1,0:T(8,128)(2,1)S(1)}, u32[]{:S(2)}, u32[]{:S(2)}) collective-permute-start(bf16[32,1024]{1,0:T(8,128)(2,1)S(1)} %get-tuple-element.23.own_any), channel_id=1, source_target_pairs={{0,4},{1,5},{2,6},{3,7},{4,0},{5,1},{6,2},{7,3},{8,12},{9,13},{10,... | collective-permute-start | bytes 196616 | tf_op jit(solution)/shard_map/gather_hidden/ppermute | solution.py:280
  18.3 1.3 %collective-permute-start.3 = (bf16[32,1024]{1,0:T(8,128)(2,1)S(1)}, bf16[32,1024]{1,0:T(8,128)(2,1)S(1)}, u32[]{:S(2)}, u32[]{:S(2)}) collective-permute-start(bf16[32,1024]{1,0:T(8,128)(2,1)S(1)} %get-tuple-element.23.own_any), channel_id=1, source_target_pairs={{0,6},{1,7},{2,0},{3,1},{4,2},{5,3},{6,4},{7,5},{8,14},{9,15},{10,... | collective-permute-start | bytes 196616 | tf_op jit(solution)/shard_map/gather_hidden/ppermute | solution.py:280
  19.7 0.7 %all-to-all-done = bf16[32,9,2,128]{3,2,1,0:T(2,128)(2,1)S(1)} async-done(((bf16[32,9,2,128]{3,2,1,0:T(2,128)(2,1)}), bf16[32,9,2,128]{3,2,1,0:T(2,128)(2,1)S(1)}, u32[]{:S(2)}, u32[]{:S(2)}) %all-to-all-start) | async-done | bytes 147488 | tf_op jit(solution)/shard_map/rows_to_owners/all_to_all | solution.py:296
  20.4 0.0 copy-done.2
  20.4 1.0 %down.1 = (f32[32,128]{1,0:T(8,128)S(1)}, f32[64,128]{1,0:T(8,128)S(1)}, bf16[1024,128]{1,0:T(8,128)(2,1)S(1)}, bf16[32,1024]{1,0:T(8,128)(2,1)S(1)}, s32[1,32]{1,0:T(1,128)S(1)}) custom-call(bf16[576,128]{1,0:T(8,128)(2,1)S(1)} %bitcast.12, bf16[1024,1024]{1,0:T(8,128)(2,1)S(1)} %bitcast.11, bf16[1024,128]{1,0:T(8,128)(2,1)} %bitcast.14, ...), custom_call_target="tpu_custom_call" | custom-call | tf_op jit(solution)/shard_map/down/pallas_call | solution.py:307
  21.4 0.1 collective-permute-start
  21.5 1.2 %collective-permute-done = f32[32,128]{1,0:T(8,128)S(1)} collective-permute-done((f32[32,128]{1,0:T(8,128)S(1)}, f32[32,128]{1,0:T(8,128)S(1)}, u32[]{:S(2)}, u32[]{:S(2)}) %collective-permute-start) | collective-permute-done | bytes 16416 | tf_op jit(solution)/shard_map/reduce/ppermute | solution.py:279
  22.7 0.0 collective-permute-done.1.y1_any
  22.7 0.0 collective-permute-done.2.y2_any
  22.7 0.0 collective-permute-done.3.y3_any
  22.7 0.4 join.1.after_ref.refs_1_
  23.1 0.0 copy-start
  23.1 0.0 copy-start.1
  23.1 0.2 collective-permute-start.7
  23.4 1.6 %collective-permute-start.4 = (f32[32,128]{1,0:T(8,128)S(1)}, f32[32,128]{1,0:T(8,128)S(1)}, u32[]{:S(2)}, u32[]{:S(2)}) collective-permute-start(f32[32,128]{1,0:T(8,128)S(1)} %add.3.after_ref.refs_0_.a_ref), channel_id=1, source_target_pairs={{0,2},{1,3},{2,4},{3,5},{4,6},{5,7},{6,0},{7,1},{8,10},{9,11},{10,... | collective-permute-start | bytes 49160 | tf_op jit(solution)/shard_map/reduce/ppermute | solution.py:280
  25.0 2.9 %collective-permute-start.5 = (f32[32,128]{1,0:T(8,128)S(1)}, f32[32,128]{1,0:T(8,128)S(1)}, u32[]{:S(2)}, u32[]{:S(2)}) collective-permute-start(f32[32,128]{1,0:T(8,128)S(1)} %add.3.after_ref.refs_0_.a_ref), channel_id=1, source_target_pairs={{0,4},{1,5},{2,6},{3,7},{4,0},{5,1},{6,2},{7,3},{8,12},{9,13},{10,... | collective-permute-start | bytes 49160 | tf_op jit(solution)/shard_map/reduce/ppermute | solution.py:280
  27.9 1.3 %collective-permute-start.6 = (f32[32,128]{1,0:T(8,128)S(1)}, f32[32,128]{1,0:T(8,128)S(1)}, u32[]{:S(2)}, u32[]{:S(2)}) collective-permute-start(f32[32,128]{1,0:T(8,128)S(1)} %add.3.after_ref.refs_0_.a_ref), channel_id=1, source_target_pairs={{0,6},{1,7},{2,0},{3,1},{4,2},{5,3},{6,4},{7,5},{8,14},{9,15},{10,... | collective-permute-start | bytes 49160 | tf_op jit(solution)/shard_map/reduce/ppermute | solution.py:280
  29.2 0.0 copy-done
  29.2 0.0 copy-done.1
  29.2 1.9 %cache.1 = (f32[256,128]{1,0:T(8,128)S(1)}, f32[256,128]{1,0:T(8,128)S(1)}, f32[256,128]{1,0:T(8,128)S(1)}, bf16[4096,256]{1,0:T(8,128)(2,1)S(1)}) custom-call(f32[8,128]{1,0:T(8,128)S(1)} %mark2.1.refs_0_, s32[1,32]{1,0:T(1,128)S(1)} %get-tuple-element.24.refs_1_, bf16[32,1024]{1,0:T(8,128)(2,1)S(1)} %get-tuple-element.25.refs_2_.refs_5_, ...), custom_call_target="tpu_custom_call" | custom-call | tf_op jit(solution)/shard_map/cache/pallas_call | solution.py:333
  31.1 0.0 collective-permute-done.4.b_ref
  31.2 0.0 collective-permute-done.5.c_ref
  31.2 0.4 collective-permute-done.6.d_ref
  31.6 0.8 %up.1.refs_0_ = bf16[64,128]{1,0:T(8,128)(2,1)} custom-call(bf16[128,1024]{1,0:T(8,128)(2,1)S(1)} %join.1.after_ref.refs_1_, f32[256,128]{1,0:T(8,128)S(1)} %get-tuple-element.26.after2_ref.refs_8_, f32[32,128]{1,0:T(8,128)S(1)} %add.3.after_ref.refs_0_.a_ref, f32[32,128]{1,0:T(8,128)S(1)} %collective-permute-done.4.b_ref, ...), custom_call_target="tpu_custom_call" | custom-call | tf_op jit(solution)/shard_map/up/pallas_call | solution.py:340
  32.4 9.1 %all-to-all-start.1 = ((bf16[32,2,128]{2,1,0:T(2,128)(2,1)}), bf16[32,2,128]{2,1,0:T(2,128)(2,1)S(1)}, u32[]{:S(2)}, u32[]{:S(2)}) async-start(bf16[32,2,128]{2,1,0:T(2,128)(2,1)} %bitcast.7), calls=%async_computation.1 | async-start | bytes 32768 | tf_op jit(solution)/shard_map/answers/all_to_all | solution.py:345
  41.6 1.7 %tables.1 = (bf16[4096,256]{1,0:T(8,128)(2,1)S(1)}, f32[32,128]{1,0:T(8,128)S(1)}, f32[32,128]{1,0:T(8,128)S(1)}, bf16[32,128]{1,0:T(8,128)(2,1)S(1)}) custom-call(bf16[64,128]{1,0:T(8,128)(2,1)} %up.1.refs_0_, s32[1,32]{1,0:T(1,128)} %bitcast.16, s32[1,32]{1,0:T(1,128)} %bitcast.18, f32[1,128]{1,0:T(1,128)} %constant.6.clone.refs_3_, bf16[8192,256]{1,0:T(8,128)(2,1)} %refs_4_.3), custom_call_target="tpu_custom_call" | custom-call | tf_op jit(solution)/shard_map/tables/pallas_call | solution.py:349
  43.3 0.0 collective-permute-done.7.refs_2_
  43.3 1.1 %late.1 = (f32[32,128]{1,0:T(8,128)S(1)}, bf16[32,128]{1,0:T(8,128)(2,1)S(1)}, f32[256,128]{1,0:T(8,128)S(1)}, f32[256,128]{1,0:T(8,128)S(1)}) custom-call(s32[1]{0:T(128)} %bitcast.9.refs_0_, bf16[128,1024]{1,0:T(8,128)(2,1)S(1)} %join.1.after_ref.refs_1_, bf16[128,1024]{1,0:T(8,128)(2,1)S(1)} %collective-permute-done.7.refs_2_, ...), custom_call_target="tpu_custom_call" | custom-call | flops 134217728 | bytes 4194304 | tf_op jit(solution)/shard_map/late/pallas_call | solution.py:360
  44.4 1.0 %all-to-all-done.1 = bf16[32,2,128]{2,1,0:T(2,128)(2,1)S(1)} async-done(((bf16[32,2,128]{2,1,0:T(2,128)(2,1)}), bf16[32,2,128]{2,1,0:T(2,128)(2,1)S(1)}, u32[]{:S(2)}, u32[]{:S(2)}) %all-to-all-start.1) | async-done | bytes 16416 | tf_op jit(solution)/shard_map/answers/all_to_all | solution.py:345
  45.3 0.8 %finish.1 = (bf16[32,1024]{1,0:T(8,128)(2,1)}, bf16[32,256]{1,0:T(8,128)(2,1)}) custom-call(bf16[64,128]{1,0:T(8,128)(2,1)S(1)} %bitcast.13, bf16[32,128]{1,0:T(8,128)(2,1)S(1)} %get-tuple-element.29.back_ref, f32[32,128]{1,0:T(8,128)S(1)} %get-tuple-element.36.value_ref, bf16[32,128]{1,0:T(8,128)(2,1)S(1)} %get-tuple-element.37.key_ref, ...), custom_call_target="tpu_custom_call" | custom-call | tf_op jit(solution)/shard_map/finish/pallas_call | solution.py:367
  (3 shorter events, 0.0 us)
Async XLA Ops:
  2.5 17.9 %all-to-all-start = ((bf16[32,9,2,128]{3,2,1,0:T(2,128)(2,1)}), bf16[32,9,2,128]{3,2,1,0:T(2,128)(2,1)S(1)}, u32[]{:S(2)}, u32[]{:S(2)}) async-start(bf16[32,9,2,128]{3,2,1,0:T(2,128)(2,1)} %bitcast.1), calls=%async_computation | async-start | bytes 294912 | tf_op jit(solution)/shard_map/rows_to_owners/all_to_all | solution.py:296
  13.8 6.7 %copy-start.2 = (bf16[16,1024,64]{1,2,0:T(8,128)(2,1)S(1)}, bf16[16,1024,64]{1,2,0:T(8,128)(2,1)}, u32[]{:S(2)}) copy-start(bf16[16,1024,64]{1,2,0:T(8,128)(2,1)} %param.17) | copy-start | bytes 6291460
  13.8 8.9 %collective-permute-start.1 = (bf16[32,1024]{1,0:T(8,128)(2,1)S(1)}, bf16[32,1024]{1,0:T(8,128)(2,1)S(1)}, u32[]{:S(2)}, u32[]{:S(2)}) collective-permute-start(bf16[32,1024]{1,0:T(8,128)(2,1)S(1)} %get-tuple-element.23.own_any), channel_id=1, source_target_pairs={{0,2},{1,3},{2,4},{3,5},{4,6},{5,7},{6,0},{7,1},{8,10},{9,11},{10,... | collective-permute-start | bytes 196616 | tf_op jit(solution)/shard_map/gather_hidden/ppermute | solution.py:280
  15.4 7.3 %collective-permute-start.2 = (bf16[32,1024]{1,0:T(8,128)(2,1)S(1)}, bf16[32,1024]{1,0:T(8,128)(2,1)S(1)}, u32[]{:S(2)}, u32[]{:S(2)}) collective-permute-start(bf16[32,1024]{1,0:T(8,128)(2,1)S(1)} %get-tuple-element.23.own_any), channel_id=1, source_target_pairs={{0,4},{1,5},{2,6},{3,7},{4,0},{5,1},{6,2},{7,3},{8,12},{9,13},{10,... | collective-permute-start | bytes 196616 | tf_op jit(solution)/shard_map/gather_hidden/ppermute | solution.py:280
  18.3 4.4 %collective-permute-start.3 = (bf16[32,1024]{1,0:T(8,128)(2,1)S(1)}, bf16[32,1024]{1,0:T(8,128)(2,1)S(1)}, u32[]{:S(2)}, u32[]{:S(2)}) collective-permute-start(bf16[32,1024]{1,0:T(8,128)(2,1)S(1)} %get-tuple-element.23.own_any), channel_id=1, source_target_pairs={{0,6},{1,7},{2,0},{3,1},{4,2},{5,3},{6,4},{7,5},{8,14},{9,15},{10,... | collective-permute-start | bytes 196616 | tf_op jit(solution)/shard_map/gather_hidden/ppermute | solution.py:280
  21.4 1.3 %collective-permute-start = (f32[32,128]{1,0:T(8,128)S(1)}, f32[32,128]{1,0:T(8,128)S(1)}, u32[]{:S(2)}, u32[]{:S(2)}) collective-permute-start(f32[32,128]{1,0:T(8,128)S(1)} %get-tuple-element.22), channel_id=1, source_target_pairs={{0,1},{1,0},{2,3},{3,2},{4,5},{5,4},{6,7},{7,6},{8,9},{9,8},{10,11... | collective-permute-start | bytes 49160 | tf_op jit(solution)/shard_map/reduce/ppermute | solution.py:279
  23.1 6.1 %copy-start = (bf16[32,384,128]{2,1,0:T(8,128)(2,1)S(1)}, bf16[32,384,128]{2,1,0:T(8,128)(2,1)}, u32[]{:S(2)}) copy-start(bf16[32,384,128]{2,1,0:T(8,128)(2,1)} %refs_3_.4) | copy-start | bytes 9437188
  23.1 6.1 %copy-start.1 = (bf16[32,384,128]{2,1,0:T(8,128)(2,1)S(1)}, bf16[32,384,128]{2,1,0:T(8,128)(2,1)}, u32[]{:S(2)}) copy-start(bf16[32,384,128]{2,1,0:T(8,128)(2,1)} %refs_4_.2) | copy-start | bytes 9437188
  23.1 20.1 %collective-permute-start.7 = (bf16[128,1024]{1,0:T(8,128)(2,1)S(1)}, bf16[128,1024]{1,0:T(8,128)(2,1)S(1)}, u32[]{:S(2)}, u32[]{:S(2)}) collective-permute-start(bf16[128,1024]{1,0:T(8,128)(2,1)S(1)} %join.1.after_ref.refs_1_), channel_id=1, source_target_pairs={{0,1},{1,0},{2,3},{3,2},{4,5},{5,4},{6,7},{7,6},{8,9},{9,8},{10,11... | collective-permute-start | bytes 786440 | tf_op jit(solution)/shard_map/gather_core/ppermute | solution.py:279
  23.4 7.8 %collective-permute-start.4 = (f32[32,128]{1,0:T(8,128)S(1)}, f32[32,128]{1,0:T(8,128)S(1)}, u32[]{:S(2)}, u32[]{:S(2)}) collective-permute-start(f32[32,128]{1,0:T(8,128)S(1)} %add.3.after_ref.refs_0_.a_ref), channel_id=1, source_target_pairs={{0,2},{1,3},{2,4},{3,5},{4,6},{5,7},{6,0},{7,1},{8,10},{9,11},{10,... | collective-permute-start | bytes 49160 | tf_op jit(solution)/shard_map/reduce/ppermute | solution.py:280
  25.0 6.2 %collective-permute-start.5 = (f32[32,128]{1,0:T(8,128)S(1)}, f32[32,128]{1,0:T(8,128)S(1)}, u32[]{:S(2)}, u32[]{:S(2)}) collective-permute-start(f32[32,128]{1,0:T(8,128)S(1)} %add.3.after_ref.refs_0_.a_ref), channel_id=1, source_target_pairs={{0,4},{1,5},{2,6},{3,7},{4,0},{5,1},{6,2},{7,3},{8,12},{9,13},{10,... | collective-permute-start | bytes 49160 | tf_op jit(solution)/shard_map/reduce/ppermute | solution.py:280
  27.9 3.7 %collective-permute-start.6 = (f32[32,128]{1,0:T(8,128)S(1)}, f32[32,128]{1,0:T(8,128)S(1)}, u32[]{:S(2)}, u32[]{:S(2)}) collective-permute-start(f32[32,128]{1,0:T(8,128)S(1)} %add.3.after_ref.refs_0_.a_ref), channel_id=1, source_target_pairs={{0,6},{1,7},{2,0},{3,1},{4,2},{5,3},{6,4},{7,5},{8,14},{9,15},{10,... | collective-permute-start | bytes 49160 | tf_op jit(solution)/shard_map/reduce/ppermute | solution.py:280
  32.4 12.9 %all-to-all-start.1 = ((bf16[32,2,128]{2,1,0:T(2,128)(2,1)}), bf16[32,2,128]{2,1,0:T(2,128)(2,1)S(1)}, u32[]{:S(2)}, u32[]{:S(2)}) async-start(bf16[32,2,128]{2,1,0:T(2,128)(2,1)} %bitcast.7), calls=%async_computation.1 | async-start | bytes 32768 | tf_op jit(solution)/shard_map/answers/all_to_all | solution.py:345

commit v10 on v9

--- a/solution.py
+++ b/solution.py
@@ -297,7 +297,8 @@
             placed.reshape(peers, chunks, CAPACITY, LANES), "dp", split_axis=0, concat_axis=0, tiled=True, axis_index_groups=ring
         ).reshape(slots * chunks, LANES)
     with jax.named_scope("gather_hidden"):
-        others = [over_y(handed, k) for k in (1, 2, 3)]
+        sent = {k: over_y(handed, k) for k in (2, 1, 3)}
+        others = [sent[k] for k in (1, 2, 3)]
     with jax.named_scope("mark"):
         mark = pl.pallas_call(
             mark_kernel, out_shape=shape((8, LANES), F32), in_specs=[ANY] + [HBM] * 2, out_specs=VMEM,

time: 46.4 us -> 46.4 us (level)
  no operation moved by 1% of the time
where the time goes in v10:
time: 46.4 us; the launch traced here: 46.1 us
  starting transfers between devices  32.5 us (70%)
  Pallas kernels  9.52 us (21%)
  waiting for transfers between devices  3.34 us (7%)
  between operations  0.78 us (2%)
    ppermute x6, starting transfers between devices, on_device(): lax.ppermute(x, 'tensor', [(i, (i + 2 * k) % count) for i in range(count)])  11.7 us
    all_to_all x1, starting transfers between devices, on_device(): lax.all_to_all(placed.reshape(peers, chunks, CAPACITY, LANES), 'dp', spli...  11.3 us
    all_to_all x1, starting transfers between devices, on_device(): lax.all_to_all(served.reshape(peers, CAPACITY, LANES), 'dp', split_axis=0...  9.12 us
    pallas_call x1, Pallas kernels, on_device(): pl.pallas_call(lambda *refs: cache_kernel(scale, *refs), out_shape=[shape...  1.92 us
    pallas_call x1, Pallas kernels, on_device(): pl.pallas_call(lambda *refs: place_kernel(pool, *refs), out_shape=[shape(...  1.87 us
    pallas_call x1, Pallas kernels, on_device(): pl.pallas_call(lambda *refs: tables_kernel(pool, peers, *refs), out_shape...  1.68 us
    ppermute x2, waiting for transfers between devices, on_device(): lax.ppermute(x, 'tensor', [(i, i ^ 1) for i in range(count)])  1.17 us
    pallas_call x1, Pallas kernels, on_device(): pl.pallas_call(lambda *refs: late_kernel(scale, *refs), out_shape=[shape(...  1.07 us
  transfers between devices with their start and end apart: 10, of which 4 were waited for; matrix products, arithmetic and copies ran while one was open for 0% of the time, Pallas kernels for 14%

profile of v10, /device:TPU:2, one launch (start us, length us, event | category | flops | bytes accessed | tf_op | source)
XLA Modules:
  0.0 46.1 jit_solution(8549158886989528610)
XLA Ops:
  0.6 1.9 %place.1 = (bf16[576,128]{1,0:T(8,128)(2,1)}, bf16[32,1024]{1,0:T(8,128)(2,1)S(1)}) custom-call(s32[1,32]{1,0:T(1,128)} %bitcast.15, bf16[32,1024]{1,0:T(8,128)(2,1)} %refs_1_.3), custom_call_target="tpu_custom_call" | custom-call | tf_op jit(solution)/shard_map/place/pallas_call | solution.py:289
  2.5 11.3 %all-to-all-start = ((bf16[32,9,2,128]{3,2,1,0:T(2,128)(2,1)}), bf16[32,9,2,128]{3,2,1,0:T(2,128)(2,1)S(1)}, u32[]{:S(2)}, u32[]{:S(2)}) async-start(bf16[32,9,2,128]{3,2,1,0:T(2,128)(2,1)} %bitcast.1), calls=%async_computation | async-start | bytes 294912 | tf_op jit(solution)/shard_map/rows_to_owners/all_to_all | solution.py:296
  13.8 0.0 copy-start.2
  13.8 1.7 %collective-permute-start.1 = (bf16[32,1024]{1,0:T(8,128)(2,1)S(1)}, bf16[32,1024]{1,0:T(8,128)(2,1)S(1)}, u32[]{:S(2)}, u32[]{:S(2)}) collective-permute-start(bf16[32,1024]{1,0:T(8,128)(2,1)S(1)} %get-tuple-element.23.own_any), channel_id=1, source_target_pairs={{0,2},{1,3},{2,4},{3,5},{4,6},{5,7},{6,0},{7,1},{8,10},{9,11},{10,... | collective-permute-start | bytes 196616 | tf_op jit(solution)/shard_map/gather_hidden/ppermute | solution.py:280
  15.4 2.9 %collective-permute-start.2 = (bf16[32,1024]{1,0:T(8,128)(2,1)S(1)}, bf16[32,1024]{1,0:T(8,128)(2,1)S(1)}, u32[]{:S(2)}, u32[]{:S(2)}) collective-permute-start(bf16[32,1024]{1,0:T(8,128)(2,1)S(1)} %get-tuple-element.23.own_any), channel_id=1, source_target_pairs={{0,4},{1,5},{2,6},{3,7},{4,0},{5,1},{6,2},{7,3},{8,12},{9,13},{10,... | collective-permute-start | bytes 196616 | tf_op jit(solution)/shard_map/gather_hidden/ppermute | solution.py:280
  18.3 1.3 %collective-permute-start.3 = (bf16[32,1024]{1,0:T(8,128)(2,1)S(1)}, bf16[32,1024]{1,0:T(8,128)(2,1)S(1)}, u32[]{:S(2)}, u32[]{:S(2)}) collective-permute-start(bf16[32,1024]{1,0:T(8,128)(2,1)S(1)} %get-tuple-element.23.own_any), channel_id=1, source_target_pairs={{0,6},{1,7},{2,0},{3,1},{4,2},{5,3},{6,4},{7,5},{8,14},{9,15},{10,... | collective-permute-start | bytes 196616 | tf_op jit(solution)/shard_map/gather_hidden/ppermute | solution.py:280
  19.7 0.7 %all-to-all-done = bf16[32,9,2,128]{3,2,1,0:T(2,128)(2,1)S(1)} async-done(((bf16[32,9,2,128]{3,2,1,0:T(2,128)(2,1)}), bf16[32,9,2,128]{3,2,1,0:T(2,128)(2,1)S(1)}, u32[]{:S(2)}, u32[]{:S(2)}) %all-to-all-start) | async-done | bytes 147488 | tf_op jit(solution)/shard_map/rows_to_owners/all_to_all | solution.py:296
  20.4 0.0 copy-done.2
  20.4 1.0 %down.1 = (f32[32,128]{1,0:T(8,128)S(1)}, f32[64,128]{1,0:T(8,128)S(1)}, bf16[1024,128]{1,0:T(8,128)(2,1)S(1)}, bf16[32,1024]{1,0:T(8,128)(2,1)S(1)}, s32[1,32]{1,0:T(1,128)S(1)}) custom-call(bf16[576,128]{1,0:T(8,128)(2,1)S(1)} %bitcast.12, bf16[1024,1024]{1,0:T(8,128)(2,1)S(1)} %bitcast.11, bf16[1024,128]{1,0:T(8,128)(2,1)} %bitcast.14, ...), custom_call_target="tpu_custom_call" | custom-call | tf_op jit(solution)/shard_map/down/pallas_call | solution.py:308
  21.4 0.1 collective-permute-start
  21.5 1.2 %collective-permute-done = f32[32,128]{1,0:T(8,128)S(1)} collective-permute-done((f32[32,128]{1,0:T(8,128)S(1)}, f32[32,128]{1,0:T(8,128)S(1)}, u32[]{:S(2)}, u32[]{:S(2)}) %collective-permute-start) | collective-permute-done | bytes 16416 | tf_op jit(solution)/shard_map/reduce/ppermute | solution.py:279
  22.7 0.0 collective-permute-done.1.y1_any
  22.7 0.0 collective-permute-done.2.y2_any
  22.7 0.0 collective-permute-done.3.y3_any
  22.7 0.4 join.1.after_ref.refs_1_
  23.1 0.0 copy-start
  23.1 0.0 copy-start.1
  23.1 0.2 collective-permute-start.7
  23.4 1.6 %collective-permute-start.4 = (f32[32,128]{1,0:T(8,128)S(1)}, f32[32,128]{1,0:T(8,128)S(1)}, u32[]{:S(2)}, u32[]{:S(2)}) collective-permute-start(f32[32,128]{1,0:T(8,128)S(1)} %add.3.after_ref.refs_0_.a_ref), channel_id=1, source_target_pairs={{0,2},{1,3},{2,4},{3,5},{4,6},{5,7},{6,0},{7,1},{8,10},{9,11},{10,... | collective-permute-start | bytes 49160 | tf_op jit(solution)/shard_map/reduce/ppermute | solution.py:280
  25.0 2.9 %collective-permute-start.5 = (f32[32,128]{1,0:T(8,128)S(1)}, f32[32,128]{1,0:T(8,128)S(1)}, u32[]{:S(2)}, u32[]{:S(2)}) collective-permute-start(f32[32,128]{1,0:T(8,128)S(1)} %add.3.after_ref.refs_0_.a_ref), channel_id=1, source_target_pairs={{0,4},{1,5},{2,6},{3,7},{4,0},{5,1},{6,2},{7,3},{8,12},{9,13},{10,... | collective-permute-start | bytes 49160 | tf_op jit(solution)/shard_map/reduce/ppermute | solution.py:280
  27.9 1.3 %collective-permute-start.6 = (f32[32,128]{1,0:T(8,128)S(1)}, f32[32,128]{1,0:T(8,128)S(1)}, u32[]{:S(2)}, u32[]{:S(2)}) collective-permute-start(f32[32,128]{1,0:T(8,128)S(1)} %add.3.after_ref.refs_0_.a_ref), channel_id=1, source_target_pairs={{0,6},{1,7},{2,0},{3,1},{4,2},{5,3},{6,4},{7,5},{8,14},{9,15},{10,... | collective-permute-start | bytes 49160 | tf_op jit(solution)/shard_map/reduce/ppermute | solution.py:280
  29.2 0.0 copy-done
  29.2 0.0 copy-done.1
  29.2 1.9 %cache.1 = (f32[256,128]{1,0:T(8,128)S(1)}, f32[256,128]{1,0:T(8,128)S(1)}, f32[256,128]{1,0:T(8,128)S(1)}, bf16[4096,256]{1,0:T(8,128)(2,1)S(1)}) custom-call(f32[8,128]{1,0:T(8,128)S(1)} %mark2.1.refs_0_, s32[1,32]{1,0:T(1,128)S(1)} %get-tuple-element.24.refs_1_, bf16[32,1024]{1,0:T(8,128)(2,1)S(1)} %get-tuple-element.25.refs_2_.refs_5_, ...), custom_call_target="tpu_custom_call" | custom-call | tf_op jit(solution)/shard_map/cache/pallas_call | solution.py:334
  31.1 0.0 collective-permute-done.4.b_ref
  31.2 0.0 collective-permute-done.5.c_ref
  31.2 0.4 collective-permute-done.6.d_ref
  31.6 0.8 %up.1.refs_0_ = bf16[64,128]{1,0:T(8,128)(2,1)} custom-call(bf16[128,1024]{1,0:T(8,128)(2,1)S(1)} %join.1.after_ref.refs_1_, f32[256,128]{1,0:T(8,128)S(1)} %get-tuple-element.26.after2_ref.refs_8_, f32[32,128]{1,0:T(8,128)S(1)} %add.3.after_ref.refs_0_.a_ref, f32[32,128]{1,0:T(8,128)S(1)} %collective-permute-done.4.b_ref, ...), custom_call_target="tpu_custom_call" | custom-call | tf_op jit(solution)/shard_map/up/pallas_call | solution.py:341
  32.4 9.1 %all-to-all-start.1 = ((bf16[32,2,128]{2,1,0:T(2,128)(2,1)}), bf16[32,2,128]{2,1,0:T(2,128)(2,1)S(1)}, u32[]{:S(2)}, u32[]{:S(2)}) async-start(bf16[32,2,128]{2,1,0:T(2,128)(2,1)} %bitcast.7), calls=%async_computation.1 | async-start | bytes 32768 | tf_op jit(solution)/shard_map/answers/all_to_all | solution.py:346
  41.6 1.7 %tables.1 = (bf16[4096,256]{1,0:T(8,128)(2,1)S(1)}, f32[32,128]{1,0:T(8,128)S(1)}, f32[32,128]{1,0:T(8,128)S(1)}, bf16[32,128]{1,0:T(8,128)(2,1)S(1)}) custom-call(bf16[64,128]{1,0:T(8,128)(2,1)} %up.1.refs_0_, s32[1,32]{1,0:T(1,128)} %bitcast.16, s32[1,32]{1,0:T(1,128)} %bitcast.18, f32[1,128]{1,0:T(1,128)} %constant.6.clone.refs_3_, bf16[8192,256]{1,0:T(8,128)(2,1)} %refs_4_.3), custom_call_target="tpu_custom_call" | custom-call | tf_op jit(solution)/shard_map/tables/pallas_call | solution.py:350
  43.3 0.0 collective-permute-done.7.refs_2_
  43.3 1.1 %late.1 = (f32[32,128]{1,0:T(8,128)S(1)}, bf16[32,128]{1,0:T(8,128)(2,1)S(1)}, f32[256,128]{1,0:T(8,128)S(1)}, f32[256,128]{1,0:T(8,128)S(1)}) custom-call(s32[1]{0:T(128)} %bitcast.9.refs_0_, bf16[128,1024]{1,0:T(8,128)(2,1)S(1)} %join.1.after_ref.refs_1_, bf16[128,1024]{1,0:T(8,128)(2,1)S(1)} %collective-permute-done.7.refs_2_, ...), custom_call_target="tpu_custom_call" | custom-call | flops 134217728 | bytes 4194304 | tf_op jit(solution)/shard_map/late/pallas_call | solution.py:361
  44.4 1.0 %all-to-all-done.1 = bf16[32,2,128]{2,1,0:T(2,128)(2,1)S(1)} async-done(((bf16[32,2,128]{2,1,0:T(2,128)(2,1)}), bf16[32,2,128]{2,1,0:T(2,128)(2,1)S(1)}, u32[]{:S(2)}, u32[]{:S(2)}) %all-to-all-start.1) | async-done | bytes 16416 | tf_op jit(solution)/shard_map/answers/all_to_all | solution.py:346
  45.3 0.8 %finish.1 = (bf16[32,1024]{1,0:T(8,128)(2,1)}, bf16[32,256]{1,0:T(8,128)(2,1)}) custom-call(bf16[64,128]{1,0:T(8,128)(2,1)S(1)} %bitcast.13, bf16[32,128]{1,0:T(8,128)(2,1)S(1)} %get-tuple-element.29.back_ref, f32[32,128]{1,0:T(8,128)S(1)} %get-tuple-element.36.value_ref, bf16[32,128]{1,0:T(8,128)(2,1)S(1)} %get-tuple-element.37.key_ref, ...), custom_call_target="tpu_custom_call" | custom-call | tf_op jit(solution)/shard_map/finish/pallas_call | solution.py:368
  (3 shorter events, 0.0 us)
Async XLA Ops:
  2.5 17.9 %all-to-all-start = ((bf16[32,9,2,128]{3,2,1,0:T(2,128)(2,1)}), bf16[32,9,2,128]{3,2,1,0:T(2,128)(2,1)S(1)}, u32[]{:S(2)}, u32[]{:S(2)}) async-start(bf16[32,9,2,128]{3,2,1,0:T(2,128)(2,1)} %bitcast.1), calls=%async_computation | async-start | bytes 294912 | tf_op jit(solution)/shard_map/rows_to_owners/all_to_all | solution.py:296
  13.8 6.7 %copy-start.2 = (bf16[16,1024,64]{1,2,0:T(8,128)(2,1)S(1)}, bf16[16,1024,64]{1,2,0:T(8,128)(2,1)}, u32[]{:S(2)}) copy-start(bf16[16,1024,64]{1,2,0:T(8,128)(2,1)} %param.17) | copy-start | bytes 6291460
  13.8 8.9 %collective-permute-start.1 = (bf16[32,1024]{1,0:T(8,128)(2,1)S(1)}, bf16[32,1024]{1,0:T(8,128)(2,1)S(1)}, u32[]{:S(2)}, u32[]{:S(2)}) collective-permute-start(bf16[32,1024]{1,0:T(8,128)(2,1)S(1)} %get-tuple-element.23.own_any), channel_id=1, source_target_pairs={{0,2},{1,3},{2,4},{3,5},{4,6},{5,7},{6,0},{7,1},{8,10},{9,11},{10,... | collective-permute-start | bytes 196616 | tf_op jit(solution)/shard_map/gather_hidden/ppermute | solution.py:280
  15.4 7.3 %collective-permute-start.2 = (bf16[32,1024]{1,0:T(8,128)(2,1)S(1)}, bf16[32,1024]{1,0:T(8,128)(2,1)S(1)}, u32[]{:S(2)}, u32[]{:S(2)}) collective-permute-start(bf16[32,1024]{1,0:T(8,128)(2,1)S(1)} %get-tuple-element.23.own_any), channel_id=1, source_target_pairs={{0,4},{1,5},{2,6},{3,7},{4,0},{5,1},{6,2},{7,3},{8,12},{9,13},{10,... | collective-permute-start | bytes 196616 | tf_op jit(solution)/shard_map/gather_hidden/ppermute | solution.py:280
  18.3 4.4 %collective-permute-start.3 = (bf16[32,1024]{1,0:T(8,128)(2,1)S(1)}, bf16[32,1024]{1,0:T(8,128)(2,1)S(1)}, u32[]{:S(2)}, u32[]{:S(2)}) collective-permute-start(bf16[32,1024]{1,0:T(8,128)(2,1)S(1)} %get-tuple-element.23.own_any), channel_id=1, source_target_pairs={{0,6},{1,7},{2,0},{3,1},{4,2},{5,3},{6,4},{7,5},{8,14},{9,15},{10,... | collective-permute-start | bytes 196616 | tf_op jit(solution)/shard_map/gather_hidden/ppermute | solution.py:280
  21.4 1.3 %collective-permute-start = (f32[32,128]{1,0:T(8,128)S(1)}, f32[32,128]{1,0:T(8,128)S(1)}, u32[]{:S(2)}, u32[]{:S(2)}) collective-permute-start(f32[32,128]{1,0:T(8,128)S(1)} %get-tuple-element.22), channel_id=1, source_target_pairs={{0,1},{1,0},{2,3},{3,2},{4,5},{5,4},{6,7},{7,6},{8,9},{9,8},{10,11... | collective-permute-start | bytes 49160 | tf_op jit(solution)/shard_map/reduce/ppermute | solution.py:279
  23.1 6.1 %copy-start = (bf16[32,384,128]{2,1,0:T(8,128)(2,1)S(1)}, bf16[32,384,128]{2,1,0:T(8,128)(2,1)}, u32[]{:S(2)}) copy-start(bf16[32,384,128]{2,1,0:T(8,128)(2,1)} %refs_3_.4) | copy-start | bytes 9437188
  23.1 6.1 %copy-start.1 = (bf16[32,384,128]{2,1,0:T(8,128)(2,1)S(1)}, bf16[32,384,128]{2,1,0:T(8,128)(2,1)}, u32[]{:S(2)}) copy-start(bf16[32,384,128]{2,1,0:T(8,128)(2,1)} %refs_4_.2) | copy-start | bytes 9437188
  23.1 20.1 %collective-permute-start.7 = (bf16[128,1024]{1,0:T(8,128)(2,1)S(1)}, bf16[128,1024]{1,0:T(8,128)(2,1)S(1)}, u32[]{:S(2)}, u32[]{:S(2)}) collective-permute-start(bf16[128,1024]{1,0:T(8,128)(2,1)S(1)} %join.1.after_ref.refs_1_), channel_id=1, source_target_pairs={{0,1},{1,0},{2,3},{3,2},{4,5},{5,4},{6,7},{7,6},{8,9},{9,8},{10,11... | collective-permute-start | bytes 786440 | tf_op jit(solution)/shard_map/gather_core/ppermute | solution.py:279
  23.4 7.8 %collective-permute-start.4 = (f32[32,128]{1,0:T(8,128)S(1)}, f32[32,128]{1,0:T(8,128)S(1)}, u32[]{:S(2)}, u32[]{:S(2)}) collective-permute-start(f32[32,128]{1,0:T(8,128)S(1)} %add.3.after_ref.refs_0_.a_ref), channel_id=1, source_target_pairs={{0,2},{1,3},{2,4},{3,5},{4,6},{5,7},{6,0},{7,1},{8,10},{9,11},{10,... | collective-permute-start | bytes 49160 | tf_op jit(solution)/shard_map/reduce/ppermute | solution.py:280
  25.0 6.2 %collective-permute-start.5 = (f32[32,128]{1,0:T(8,128)S(1)}, f32[32,128]{1,0:T(8,128)S(1)}, u32[]{:S(2)}, u32[]{:S(2)}) collective-permute-start(f32[32,128]{1,0:T(8,128)S(1)} %add.3.after_ref.refs_0_.a_ref), channel_id=1, source_target_pairs={{0,4},{1,5},{2,6},{3,7},{4,0},{5,1},{6,2},{7,3},{8,12},{9,13},{10,... | collective-permute-start | bytes 49160 | tf_op jit(solution)/shard_map/reduce/ppermute | solution.py:280
  27.9 3.7 %collective-permute-start.6 = (f32[32,128]{1,0:T(8,128)S(1)}, f32[32,128]{1,0:T(8,128)S(1)}, u32[]{:S(2)}, u32[]{:S(2)}) collective-permute-start(f32[32,128]{1,0:T(8,128)S(1)} %add.3.after_ref.refs_0_.a_ref), channel_id=1, source_target_pairs={{0,6},{1,7},{2,0},{3,1},{4,2},{5,3},{6,4},{7,5},{8,14},{9,15},{10,... | collective-permute-start | bytes 49160 | tf_op jit(solution)/shard_map/reduce/ppermute | solution.py:280
  32.4 12.9 %all-to-all-start.1 = ((bf16[32,2,128]{2,1,0:T(2,128)(2,1)}), bf16[32,2,128]{2,1,0:T(2,128)(2,1)S(1)}, u32[]{:S(2)}, u32[]{:S(2)}) async-start(bf16[32,2,128]{2,1,0:T(2,128)(2,1)} %bitcast.7), calls=%async_computation.1 | async-start | bytes 32768 | tf_op jit(solution)/shard_map/answers/all_to_all | solution.py:346
